TPU v7x, 32 devices: a whole 2x2x4 slice. The times are simulated.
32 devices in a mesh: groups: 2 (over y), dp: 4 (over z), seq: 2 (over x), head: 2 (over core).
Axes of the slice: x: 2, y: 2, z: 4, core: 2. Of those that a mesh axis runs over, the one named last changes fastest.
Arguments:
- tokens: bfloat16 [8, 768, 6144], P(('groups', 'dp'), 'seq'), parts along dimension 0, may hold values from -8 to 8
- ln_gain: float32 [6144], replicated, may hold values from 0.1 to 1.9
- qkv_weight: bfloat16 [6144, 24, 384], P('dp', ('seq', 'head')), may hold values from -8 to 8
Outputs:
- attended: bfloat16 [8, 768, 3072], P(('groups', 'dp'), 'seq', 'head'), parts along dimension 0
There are 2 independent parts, one for each index of `groups`. A program takes and returns all parts, laid end to end along the dimension named above; an argument that names none is the same for every part. Nothing has to cross between parts.
All inputs are finite; a program needn't handle non-finite values.
Results may differ from a plain program's by a relative error of at most 0.012.
Values may be sent and summed in bfloat16 or wider, within the bound.
No kernel may reach another device: no remote copies, remote signals or barrier semaphores. Data moves between devices by JAX's collectives and lax.ppermute only.
A program may use at most 128 MiB of HBM per device.

v0:
```python
import functools
import math

import jax
import jax.numpy as jnp
from jax import lax
from jax.experimental import pallas as pl
from jax.experimental.pallas import tpu as pltpu
from jax.sharding import PartitionSpec as P


def normalize(array, gain):
    widened = array.astype(jnp.float32)
    centered = widened - jnp.mean(widened, axis=-1, keepdims=True)
    variance = jnp.mean(centered * centered, axis=-1, keepdims=True)
    return (centered * lax.rsqrt(variance + 1e-06) * gain).astype(jnp.bfloat16)


def attend(projected):
    width = projected.shape[2] // 3
    queries = projected[:, :, :width]
    key_rows = projected[:, :, width : 2 * width]
    value_rows = projected[:, :, 2 * width :]
    scores = jnp.einsum("qhd,khd->hqk", queries, key_rows, preferred_element_type=jnp.float32) * (
        1.0 / math.sqrt(width)
    )
    highest = jnp.max(scores, axis=-1, keepdims=True)
    expo = jnp.exp(scores - highest)
    probs = (expo / jnp.sum(expo, axis=-1, keepdims=True)).astype(jnp.bfloat16)
    mixed = jnp.einsum("hqk,khd->qhd", probs, value_rows, preferred_element_type=jnp.float32)
    return mixed.astype(jnp.bfloat16).reshape(projected.shape[0], -1)


def plain(tokens, ln_gain, qkv_weight):
    images = tokens.shape[0]
    width = tokens.shape[2]
    heads_here = qkv_weight.shape[1]
    columns = heads_here * qkv_weight.shape[2]
    source = normalize(tokens, ln_gain)
    half_width = width // lax.axis_size("head")
    core_index = lax.axis_index("head")
    own_half = lax.dynamic_slice_in_dim(source, core_index * half_width, half_width, 2)
    fetched = lax.all_gather(own_half, "seq", axis=1, tiled=True)
    gathered = lax.all_gather(fetched, "head", axis=2, tiled=True)
    full_tokens = gathered.shape[1]
    features = gathered.reshape(images * full_tokens, width)
    piece = lax.all_gather(qkv_weight, "dp", axis=0, tiled=True)
    projected = jnp.dot(
        features, piece.reshape(piece.shape[0], columns), preferred_element_type=jnp.float32
    )
    projected = projected.astype(jnp.bfloat16).reshape(
        images, full_tokens, heads_here, qkv_weight.shape[2]
    )
    mixed = lax.map(attend, projected)
    return lax.all_to_all(mixed, "seq", split_axis=1, concat_axis=2, tiled=True)


def slab_order(plane):
    inner = (plane == 1) | (plane == 2)
    near, far = plane ^ 1, 2 - plane // 2
    return plane, jnp.where(inner, near, far), jnp.where(inner, far, near), 3 - 3 * (plane // 2)


def normalize_kernel(step, other, taken, tokens_ref, gain_ref, weight_ref, *refs):
    refs = list(refs)
    take = lambda n: [refs.pop(0) for _ in range(n)]
    normed_refs, own_refs, (tokens_buf, *normed_bufs) = take(2), take(len(taken)), take(3)
    own_bufs, (in_sems, out_sems, own_sems) = take(len(taken)), take(3)
    part, width = tokens_buf.shape
    lanes = 128
    slab, span = width // 4, width // 2
    core = lax.axis_index("head")
    first = pl.multiple_of((1 - core if other else core) * part, part)
    order = slab_order(lax.axis_index("dp"))
    heads = weight_ref.shape[0] // lax.axis_size("groups")

    def rows_in(i):
        return pltpu.make_async_copy(
            tokens_ref.at[0, pl.ds(pl.multiple_of(first + i * step, step), step)],
            tokens_buf.at[pl.ds(pl.multiple_of(i * step, step), step)],
            in_sems.at[i],
        )

    def rows_out(i):
        rows = pl.ds(pl.multiple_of(i * step, step), step)
        return [
            pltpu.make_async_copy(buf.at[rows], ref.at[rows], out_sems.at[i, cut])
            for cut, (buf, ref) in enumerate(zip(normed_bufs, normed_refs))
        ]

    def own_in(k):
        head = lax.axis_index("groups") * heads + taken[k]
        return pltpu.make_async_copy(weight_ref.at[head], own_bufs[k], own_sems.at[k, 0])

    def own_out(k):
        return pltpu.make_async_copy(own_bufs[k], own_refs[k], own_sems.at[k, 1])

    for i in range(part // step):
        rows_in(i).start()
    for k in range(len(taken)):
        own_in(k).start()

    @pl.loop(0, part // step)
    def _(i):
        rows_in(i).wait()
        rows = pl.ds(pl.multiple_of(i * step, step), step)

        def widened(begin):
            return tokens_buf[rows, pl.ds(begin, lanes)].astype(jnp.float32)

        total = jnp.zeros((step, lanes), jnp.float32)
        for begin in range(0, width, lanes):
            total += widened(begin)
        mean = jnp.sum(total, axis=-1, keepdims=True) / width
        total = jnp.zeros((step, lanes), jnp.float32)
        for begin in range(0, width, lanes):
            centered = widened(begin) - mean
            total += centered * centered
        scale = lax.rsqrt(jnp.sum(total, axis=-1, keepdims=True) / width + 1e-06)
        for k in range(4):
            for begin in range(0, slab, lanes):
                column = pl.multiple_of(order[k] * slab + begin, lanes)
                value = (widened(column) - mean) * scale * gain_ref[:, pl.ds(column, lanes)]
                target = k * slab % span + begin
                normed_bufs[k * slab // span][rows, target : target + lanes] = value.astype(
                    jnp.bfloat16
                )
        for copy in rows_out(i):
            copy.start()

    for k in range(len(taken)):
        own_in(k).wait()
        own_out(k).start()
    for i in range(part // step):
        for copy in rows_out(i):
            copy.wait()
    for k in range(len(taken)):
        own_out(k).wait()


def normalize_part(tokens, ln_gain, weight, part, other, taken=()):
    width = tokens.shape[2]
    piece = weight.shape[1:]
    step = 64 if part % 64 == 0 else 32
    anywhere = pl.BlockSpec(memory_space=pl.ANY)
    half = jax.ShapeDtypeStruct((part, width // 2), jnp.bfloat16)
    got = pl.pallas_call(
        functools.partial(normalize_kernel, step, other, taken),
        out_shape=[half] * 2 + [jax.ShapeDtypeStruct(piece, jnp.bfloat16)] * len(taken),
        in_specs=[anywhere, pl.BlockSpec(memory_space=pltpu.VMEM), anywhere],
        out_specs=[anywhere] * (2 + len(taken)),
        scratch_shapes=[
            pltpu.VMEM((part, width), jnp.bfloat16),
            *[pltpu.VMEM((part, width // 2), jnp.bfloat16)] * 2,
            *[pltpu.VMEM(piece, jnp.bfloat16)] * len(taken),
            pltpu.SemaphoreType.DMA((part // step,)),
            pltpu.SemaphoreType.DMA((part // step, 2)),
            pltpu.SemaphoreType.DMA((max(len(taken), 1), 2)),
        ],
        compiler_params=pltpu.CompilerParams(vmem_limit_bytes=62 << 20),
        cost_estimate=pl.CostEstimate(
            flops=8 * part * width, bytes_accessed=4 * part * width, transcendentals=part
        ),
    )(tokens, ln_gain[None], weight)
    return got[:2], got[2:]


def attend_rows(projected_ref, parts, column):
    width = projected_ref.shape[1] // 3
    key_rows = projected_ref[:, width : 2 * width]
    value_rows = projected_ref[:, 2 * width :]
    value_rows = jnp.concatenate([value_rows, jnp.ones_like(value_rows)], axis=1)
    begin = 0
    for part in parts:
        step = part.shape[0]
        queries = projected_ref[begin : begin + step, :width]
        scores = lax.dot_general(
            queries, key_rows, (((1,), (1,)), ((), ())), preferred_element_type=jnp.float32
        )
        highest = jnp.max(scores, axis=-1, keepdims=True)
        expo = jnp.exp2((scores - highest) * (math.log2(math.e) / math.sqrt(width)))
        mixed = jnp.dot(expo.astype(jnp.bfloat16), value_rows, preferred_element_type=jnp.float32)
        mixed = mixed[:, :width] / mixed[:, width:]
        part[:, column : column + width] = mixed.astype(jnp.bfloat16)
        begin += step


class Jobs:
    def __init__(self, **numbers):
        self.__dict__.update(numbers)

    def jobs(self, image):
        return sorted({j for use in self.uses[image] if use for j in range(*use)})


def job_kernel(plan, role_ref, *refs):
    refs = list(refs)
    take = lambda n: [refs.pop(0) for _ in range(n)]
    images, ns = range(len(plan.uses)), range(len(plan.slots))
    pieces = [[[take(2) for _ in place] for place in image] for image in plan.origins]
    weights = [[take(1) * 2 if alike else take(2) for alike in row] for row in plan.same]
    partials = [{j: take(1)[0] for j in plan.added[i]} for i in images]
    carried = [[take(plan.carried[i]) for _ in range(2)] for i in images]
    outs = [
        {j: take(2) if j in plan.finished[i] else take(1)[0] for j in plan.jobs(i)} for i in images
    ]
    features_ref, weight_ref, total_ref, projected_ref = take(4)
    token_sems, weight_sems, sum_sems, out_sems, carry_sems = take(5)
    core, inner = role_ref[0], role_ref[1]
    slab = pieces[0][0][0][0].shape[1] // 2
    tokens, wide = projected_ref.shape[1:]
    part = tokens // 4

    def features(i, n):
        return features_ref.at[pl.ds(i * tokens, tokens), pl.ds(n * slab, slab)]

    def weight(n, j):
        return weight_ref.at[pl.ds(n * slab, slab), pl.ds(j * wide, wide)]

    def total(i, j):
        return total_ref.at[pl.ds(i * tokens, tokens), pl.ds(j * wide, wide)]

    def start_tokens(i, n):
        cut, begin = plan.slots[n] // 2, plan.slots[n] % 2 * slab
        for place in range(2):
            split = len(plan.origins[i][place])
            for owner in range(split):
                row = i * tokens + 2 * place * part
                if split == 2:
                    row += (1 - core if owner else core) * part
                count = 2 * part // split
                from_rows = pl.ds(plan.origins[i][place][owner][cut], count)
                rows = pl.ds(pl.multiple_of(row, 32), count)
                pltpu.make_async_copy(
                    pieces[i][place][owner][cut].at[from_rows, pl.ds(begin, slab)],
                    features_ref.at[rows, pl.ds(n * slab, slab)],
                    token_sems.at[i, n],
                ).start()

    def start_weight(n, j, role):
        source = weights[n][j - plan.first[n]][role]
        if source.shape[0] == slab:
            pltpu.make_async_copy(source, weight(n, j), weight_sems.at[n, j]).start()
            return
        for b in range(source.shape[1] // wide):
            pltpu.make_async_copy(
                source.at[:, pl.ds(b * wide, wide)],
                weight_ref.at[pl.ds(n * slab + b * part, part), pl.ds(j * wide, wide)],
                weight_sems.at[n, j],
            ).start()

    def start_role_weight(n, j):
        if plan.same[n][j - plan.first[n]]:
            start_weight(n, j, 0)
            return

        @pl.when(inner == 1)
        def _():
            start_weight(n, j, 0)

        @pl.when(inner != 1)
        def _():
            start_weight(n, j, 1)

    def partial_copy(i, j):
        return pltpu.make_async_copy(partials[i][j], total(i, j), sum_sems.at[i, j])

    def out_copy(i, j):
        return pltpu.make_async_copy(total(i, j), outs[i][j], out_sems.at[i, j])

    def carry_copies():
        for i in images:
            for place in range(2):
                for k in range(plan.carried[i]):
                    (finished,) = plan.finished[i]
                    target = outs[i][finished][place].at[:, pl.ds(k * wide // 3, wide // 3)]
                    yield pltpu.make_async_copy(
                        carried[i][place][k], target, carry_sems.at[i, place, k]
                    )

    stages = [(i, n) for i in images for n in ns if plan.uses[i][n]]
    held = set()

    def start_stage(i, n):
        start_tokens(i, n)
        for j in range(*plan.uses[i][n]):
            if (n, j) not in held:
                held.add((n, j))
                start_role_weight(n, j)
        if not any((i, n) > (i, m) and plan.uses[i][m] for m in ns):
            for j in plan.added[i]:
                partial_copy(i, j).start()

    ahead = 2
    for stage in stages[:ahead]:
        start_stage(*stage)
    for copy in carry_copies():
        copy.start()
    ready, waiting, step = set(), [], plan.step
    for index, (i, n) in enumerate(stages):
        low, high = plan.uses[i][n]
        pltpu.make_async_copy(features(i, n), features(i, n), token_sems.at[i, n]).wait()
        for j in range(low, high):
            if (n, j) not in ready:
                ready.add((n, j))
                pltpu.make_async_copy(weight(n, j), weight(n, j), weight_sems.at[n, j]).wait()
        if index + ahead < len(stages):
            start_stage(*stages[index + ahead])
        mine = {
            j: [m for m in ns if plan.uses[i][m] and j in range(*plan.uses[i][m])]
            for j in range(low, high)
        }
        for j in range(low, high):
            if n == mine[j][0] and j in plan.added[i]:
                partial_copy(i, j).wait()

        def project(r):
            local = pl.ds(pl.multiple_of(r * step, step), step)
            rows = pl.ds(pl.multiple_of(i * tokens + r * step, step), step)
            term = jnp.dot(
                features_ref[rows, n * slab : (n + 1) * slab],
                weight_ref[n * slab : (n + 1) * slab, low * wide : high * wide],
                preferred_element_type=jnp.float32,
            )
            for j in range(low, high):
                value = term[:, (j - low) * wide : (j - low + 1) * wide]
                if n != mine[j][0] or j in plan.added[i]:
                    value += total_ref[rows, j * wide : (j + 1) * wide]
                if n == mine[j][-1] and j in plan.finished[i]:
                    projected_ref[i % 2, local, :] = value.astype(jnp.bfloat16)
                else:
                    total_ref[rows, j * wide : (j + 1) * wide] = value

        if step == tokens:
            project(0)
        else:
            pl.loop(0, tokens // step)(project)

        for j in range(low, high):
            if n != mine[j][-1]:
                continue
            if j in plan.finished[i]:
                if waiting:
                    attend_rows(*waiting.pop())
                column = plan.carried[i] * wide // 3
                waiting.append((projected_ref.at[i % 2], outs[i][j], column))
            else:
                out_copy(i, j).start()
    if waiting:
        attend_rows(*waiting.pop())
    for copy in carry_copies():
        copy.wait()
    for i in images:
        for j in plan.jobs(i):
            if j not in plan.finished[i]:
                out_copy(i, j).wait()


def run_jobs(role, tokens, wide, images, weights, step=384):
    images = [
        dict(
            image,
            pieces=[
                [[x if isinstance(x, tuple) else (x, 0) for x in owner] for owner in place]
                for place in image["pieces"]
            ],
            sums=image.get("sums", {}),
            finish=image.get("finish", ()),
            carry=image.get("carry", ((), ())),
        )
        for image in images
    ]
    plan = Jobs(
        origins=[[[[r for _, r in o] for o in p] for p in image["pieces"]] for image in images],
        slots=[slot for slot, _, _ in weights],
        first=[first for _, first, _ in weights],
        same=[[not isinstance(w, tuple) for w in row] for _, _, row in weights],
        uses=[image["uses"] for image in images],
        added=[tuple(image["sums"]) for image in images],
        finished=[image["finish"] for image in images],
        carried=[len(image["carry"][0]) for image in images],
        step=step,
    )
    operands = [x for i in images for place in i["pieces"] for owner in place for x, _ in owner]
    slab = operands[0].shape[1] // 2
    for _, _, row in weights:
        for w in row:
            operands += list(w) if isinstance(w, tuple) else [w]
    operands += [x for image in images for x in image["sums"].values()]
    operands += [x for image in images for place in image["carry"] for x in place]
    anywhere, vmem = pl.BlockSpec(memory_space=pl.ANY), pl.BlockSpec(memory_space=pltpu.VMEM)
    head = wide // 3
    shapes, specs = [], []
    for i in range(len(images)):
        for j in plan.jobs(i):
            if j in plan.finished[i]:
                shape = (tokens // 2, head * (plan.carried[i] + 1))
                shapes += [jax.ShapeDtypeStruct(shape, jnp.bfloat16)] * 2
                specs += [vmem] * 2
            else:
                shapes.append(jax.ShapeDtypeStruct((tokens, wide), jnp.float32))
                specs.append(anywhere)
    jobs = 1 + max(j for i in range(len(images)) for j in plan.jobs(i))
    count, depth, total = len(images), len(weights) * slab, len(images) * tokens
    added = sum(high - low for uses in plan.uses for low, high in filter(None, uses))
    got = pl.pallas_call(
        functools.partial(job_kernel, plan),
        out_shape=shapes,
        in_specs=[pl.BlockSpec(memory_space=pltpu.SMEM)] + [anywhere] * len(operands),
        out_specs=specs,
        scratch_shapes=[
            pltpu.VMEM((total, depth), jnp.bfloat16),
            pltpu.VMEM((depth, jobs * wide), jnp.bfloat16),
            pltpu.VMEM((total, jobs * wide), jnp.float32),
            pltpu.VMEM((2, tokens, wide), jnp.bfloat16),
            pltpu.SemaphoreType.DMA((count, len(weights))),
            pltpu.SemaphoreType.DMA((len(weights), jobs)),
            pltpu.SemaphoreType.DMA((count, jobs)),
            pltpu.SemaphoreType.DMA((count, jobs)),
            pltpu.SemaphoreType.DMA((count, 2, max(*plan.carried, 1))),
        ],
        compiler_params=pltpu.CompilerParams(vmem_limit_bytes=62 << 20),
        cost_estimate=pl.CostEstimate(
            flops=2 * tokens * slab * wide * added, bytes_accessed=0, transcendentals=0
        ),
    )(role, *operands)
    got = list(got)
    return [
        {
            j: (got.pop(0), got.pop(0)) if j in plan.finished[i] else got.pop(0)
            for j in plan.jobs(i)
        }
        for i in range(count)
    ]


def join_kernel(place_ref, *refs):
    *parts, out_ref, sems = refs
    count = len(parts) // 2
    inner = place_ref[count]
    wide, head = parts[0].shape[1], parts[count].shape[1]

    def copies(i, role):
        begin = pl.multiple_of(place_ref[i] * wide, wide)
        if role:
            yield parts[i], out_ref.at[:, pl.ds(begin, wide)], sems.at[i, 0]
            return
        kept = wide - head
        yield parts[i].at[:, pl.ds(head, kept)], out_ref.at[:, pl.ds(begin, kept)], sems.at[i, 0]
        last = pl.multiple_of(begin + kept, head)
        yield parts[count + i], out_ref.at[:, pl.ds(last, head)], sems.at[i, 1]

    for role in (1, 0):

        @pl.when((inner == 1) == (role == 1))
        def _():
            every = [pltpu.make_async_copy(*c) for i in range(count) for c in copies(i, role)]
            for copy in every:
                copy.start()
            for copy in every:
                copy.wait()


def join(places, inner, parts, back):
    rows, wide = parts[0].shape
    anywhere = pl.BlockSpec(memory_space=pl.ANY)
    return pl.pallas_call(
        join_kernel,
        out_shape=jax.ShapeDtypeStruct((rows, wide * len(parts)), jnp.bfloat16),
        in_specs=[pl.BlockSpec(memory_space=pltpu.SMEM)] + [anywhere] * (2 * len(parts)),
        out_specs=pl.BlockSpec(memory_space=pltpu.VMEM),
        scratch_shapes=[pltpu.SemaphoreType.DMA((len(parts), 2))],
        cost_estimate=pl.CostEstimate(
            flops=0, bytes_accessed=4 * rows * wide * len(parts), transcendentals=0
        ),
    )(jnp.stack([*places, inner]).astype(jnp.int32), *parts, *back)


def shared(tokens, ln_gain, qkv_weight):
    groups, planes, seqs, cores = (lax.axis_size(a) for a in ("groups", "dp", "seq", "head"))
    group, plane, seq, core = (lax.axis_index(a) for a in ("groups", "dp", "seq", "head"))
    _, rows, _ = tokens.shape
    slab, heads, columns = qkv_weight.shape
    heads, part = heads // groups, rows // cores
    inner = (plane == 1) | (plane == 2)
    wait = lax.optimization_barrier

    def fold(piece):
        piece = piece.reshape(-1, part, columns).transpose(1, 0, 2)
        return piece.reshape(part, -1)

    def pick(for_inner, for_ends):
        return jnp.where(inner, for_inner, for_ends)

    def pair(value):
        return lax.ppermute(value, "dp", [(0, 1), (1, 0), (2, 3), (3, 2)])

    def outward(value):
        return lax.ppermute(value, "dp", [(1, 0), (2, 3)])

    def middle(value):
        return lax.ppermute(value, "dp", [(1, 2), (2, 1)])

    swap = [(0, 1), (1, 0)]
    beside = lambda value: lax.ppermute(value, "seq", swap)
    across = lambda value: lax.ppermute(value, "groups", swap)

    def others(*values):
        got = []
        for value in values:
            if got:
                value, got[-1] = wait((value, got[-1]))
            got.append(lax.ppermute(value, "head", swap))
        return got


    def exchange(mixed):
        got = []
        for a in range(groups):
            for b in range(seqs):
                sent = mixed[a * seqs + b]
                if a or b:
                    steps = [
                        (g * seqs + s, (g + a) % groups * seqs + (s + b) % seqs)
                        for g in range(groups)
                        for s in range(seqs)
                    ]
                    sent = lax.ppermute(sent, ("groups", "seq"), steps)
                got.append(sent)
        return got

    weight = qkv_weight.transpose(1, 0, 2)
    normed, (own0,) = normalize_part(tokens, ln_gain, weight, part, False, (0,))
    normed, own0, later_weight = wait((normed, own0, weight))
    cut0, cut1 = normed
    pair1, middle1 = pair(own0), middle(own0)
    beside1, across1 = beside(cut0), across(cut0)
    own1, own2 = [
        lax.dynamic_index_in_dim(later_weight, group * heads + j, 0, keepdims=False) for j in (1, 2)
    ]
    give = pick(fold(own1), cut0)
    role = jnp.stack([core, inner]).astype(jnp.int32)
    beside1, across1, own1, own2, cut1, tokens, give, role = wait(
        (beside1, across1, own1, own2, cut1, tokens, give, role)
    )
    pair1, middle1, give = wait((pair1, middle1, give))
    run = functools.partial(run_jobs, role, seqs * rows, columns)

    pair2, middle2 = pair(give), middle(pair1)
    beside2, across2 = beside(cut1), across(cut1)
    give = pick(fold(middle1), cut1)
    far_normed, _ = normalize_part(tokens, ln_gain, weight, part, True)
    far1 = others(beside1, across1)
    pair2, middle2, beside2, across2, across1, own1, own2, far_normed, far1, give = wait(
        (pair2, middle2, beside2, across2, across1, own1, own2, far_normed, far1, give)
    )

    pair3, middle3 = pair(give), middle(own1)
    beside3, across3 = beside(across1), across(beside2)
    give = pick(middle2, own1)
    far2 = others(across2, beside2)[::-1]
    pair3, middle3, beside3, across3, pair1, pair2, own2, far2, give = wait(
        (pair3, middle3, beside3, across3, pair1, pair2, own2, far2, give)
    )

    pair4, middle4 = pair(give), middle(own2)
    beside4, across4 = beside(pair2), across(pair2)
    give = pick(middle3, own2)
    pieces0 = ((normed, far_normed), ((beside1, beside2), (far1[0], far2[0])))
    owns = [own0, (own1, own0), (own2, own1)]
    ((head0, sum20, sum30),) = [
        tuple(got.values())
        for got in run(
            [dict(pieces=pieces0, uses=[(0, 3), (0, 2), (0, 1), (0, 1)], finish=(0,))],
            [(0, 0, owns), (2, 0, [middle1, (middle3, pair1)]), (1, 0, [pair1]), (3, 0, [middle2])],
        )
    ]
    far3 = others(beside3, across3)
    lent = jnp.concatenate([pair2, pair3])
    pair4, middle4, beside4, across4, own2, pair3, lent, head0, sum20, sum30, far3, give = wait(
        (pair4, middle4, beside4, across4, own2, pair3, lent, head0, sum20, sum30, far3, give)
    )

    pair5, middle5 = pair(give), middle(pair4)
    beside5, across5 = beside(pair3), across(pair3)
    pieces1 = (((across1, across2), (far1[1], far2[1])), ((beside3, across3), far3))
    image1, image0 = run(
        [
            dict(pieces=pieces1, uses=[(0, 3), (0, 3), (0, 2), (0, 1)], finish=(0,)),
            dict(pieces=pieces0, uses=[None, (2, 3), (1, 2), None], sums={1: sum20, 2: sum30}),
        ],
        [
            (0, 0, owns),
            (2, 0, [middle1, (middle3, pair1), (middle4, pair2)]),
            (1, 0, [pair1, (pair4, pair3)]),
            (3, 0, [middle2]),
        ],
    )
    far_lent, far4 = others(lent, beside4)
    pair5, middle5, beside5, across5, across4, image0, image1, far_lent, far4 = wait(
        (
            *(pair5, middle5, beside5, across5, across4),
            *(image0, image1, far_lent, far4),
        )
    )

    pair6, middle6 = outward(middle5), middle(pair5)
    beside6, across6 = beside(across4), across(beside5)
    far5, far_across4 = others(beside5, across4)
    ahead0, ahead1 = run(
        [
            dict(
                pieces=pieces,
                uses=[(0, 1), (1, 2)],
                sums={0: image[1], 1: image[2]},
                finish=(0,),
            )
            for pieces, image in ((pieces0, image0), (pieces1, image1))
        ],
        [(3, 0, [(middle5, pair4)]), (1, 1, [pair5])],
    )
    lent0 = (((pair2, pair3), (far_lent, (far_lent, part))), ((beside4, beside5), (far4, far5)))
    lent_weights = [(0, 0, [pair5]), (1, 0, [middle4]), (2, 0, [own2])]
    ((sum4,),) = [
        tuple(got.values()) for got in run([dict(pieces=lent0, uses=[(0, 1)] * 3)], lent_weights)
    ]
    pair6, middle6, beside6, across6, across5, ahead0, ahead1, sum4, far_across4 = wait(
        (pair6, middle6, beside6, across6, across5, ahead0, ahead1, sum4, far_across4)
    )

    far_across5, *far6 = [
        lax.ppermute(value, "head", swap) for value in (across5, beside6, across6)
    ]
    done0, done1, lent0 = run(
        [
            dict(pieces=p, uses=[(0, 1)], sums={0: x[1]}, finish=(0,), carry=tuple(zip(h, x[0])))
            for p, h, x in ((pieces0, head0, ahead0), (pieces1, image1[0], ahead1))
        ]
        + [dict(pieces=lent0, uses=[(0, 1)], sums={0: sum4}, finish=(0,))],
        [(3, 0, [(middle6, pair6)])],
    )
    lent1 = (((across4, across5), (far_across4, far_across5)), ((beside6, across6), far6))
    (lent1,) = run(
        [dict(pieces=lent1, uses=[(0, 1)] * 4, finish=(0,))],
        [*lent_weights, (3, 0, [middle6])],
        step=seqs * rows,
    )

    def hand_back(mixed):
        got = []
        for a in range(groups):
            for b in range(seqs):
                steps = [
                    (
                        (g * planes + z) * seqs + s,
                        ((g + a) % groups * planes + (z ^ 1)) * seqs + (s + b) % seqs,
                    )
                    for g in range(groups)
                    for z in (1, 2)
                    for s in range(seqs)
                ]
                sent = mixed[a * seqs + b]
                got.append(lax.ppermute(sent, ("groups", "dp", "seq"), steps))
        return got

    sent = exchange((*done0[0], *done1[0]))
    back = hand_back((*lent0[0], *lent1[0]))
    places = [
        (seq - b) % seqs * groups + (group - a) % groups
        for a in range(groups)
        for b in range(seqs)
    ]
    return join(places, inner, sent, back)[None]


def per_device(tokens, ln_gain, qkv_weight):
    groups, planes, seqs, cores = (lax.axis_size(a) for a in ("groups", "dp", "seq", "head"))
    images, rows, width = tokens.shape
    slab, heads, _ = qkv_weight.shape
    if (groups, planes, seqs, cores) == (2, 4, 2, 2) and images == 1 and heads == 3 * groups:
        part = rows // cores
        if rows % (32 * cores) == 0 and slab % part == 0 and 2 * slab == qkv_weight.shape[2] * slab // part:
            return shared(tokens, ln_gain, qkv_weight)
    return plain(tokens, ln_gain, qkv_weight)


def solution(mesh):
    return jax.shard_map(
        per_device,
        mesh=mesh,
        in_specs=(P(("groups", "dp"), "seq", None), P(), P("dp", ("seq", "head"), None)),
        out_specs=P(("groups", "dp"), "seq", "head"),
        check_vma=False,
    )
```

profile of v0, /device:TPU:0, one launch (start us, length us, event | category | flops | bytes accessed | tf_op | source)
XLA Modules:
  0.0 243.8 jit_solution(12296656587745878827)
XLA Ops:
  0.0 5.2 %shard_map.37 = (bf16[192,3072]{1,0:T(8,128)(2,1)}, bf16[192,3072]{1,0:T(8,128)(2,1)}, bf16[1536,384]{1,0:T(8,128)(2,1)}) custom-call(bf16[1,384,6144]{2,1,0:T(8,128)(2,1)} %tokens_ref.2, f32[1,6144]{1,0:T(1,128)} %bitcast.35, bf16[6,1536,384]{2,1,0:T(8,128)(2,1)} %bitcast.23), custom_call_target="tpu_custom_call" | custom-call | flops 9437184 | bytes 4718592 | tf_op jit(solution)/shard_map/pallas_call | solution.py:147
  5.2 3.0 %collective-permute-start = (bf16[192,3072]{1,0:T(8,128)(2,1)}, bf16[192,3072]{1,0:T(8,128)(2,1)}, u32[]{:S(2)}, u32[]{:S(2)}) collective-permute-start(bf16[192,3072]{1,0:T(8,128)(2,1)} %get-tuple-element.124.refs_0_.refs_8_), channel_id=1, source_target_pairs={{0,2},{2,0},{1,3},{3,1},{4,6},{6,4},{5,7},{7,5},{8,10},{10,8},{9,1... | collective-permute-start | bytes 3538952 | tf_op jit(solution)/shard_map/ppermute | solution.py:505
  8.2 1.5 collective-permute-start.1
  9.7 1.6 collective-permute-start.2
  11.3 1.7 collective-permute-start.3
  13.0 2.9 %dynamic-slice_bitcast_fusion = (bf16[1536,384]{1,0:T(8,128)(2,1)}, bf16[1,1536,384]{2,1,0:T(8,128)(2,1)S(1)}) fusion(bf16[6,1536,384]{2,1,0:T(8,128)(2,1)} %bitcast.24, s32[]{:T(128)S(6)} %select_n.63, s32[]{:T(128)S(6)} %select_n.62), kind=kLoop, calls=%fused_computation.1 | loop fusion | bytes 4718600 | tf_op jit(solution)/shard_map/jit(dynamic_index_in_dim)/squeeze | solution.py:539
  15.9 1.2 copy.7
  17.1 0.9 copy-done.1
  18.0 1.1 broadcast_select_fusion.3
  19.1 0.6 pad_add_fusion.role_ref
  19.7 14.8 %collective-permute-done.refs_4_.refs_12_ = bf16[192,3072]{1,0:T(8,128)(2,1)} collective-permute-done((bf16[192,3072]{1,0:T(8,128)(2,1)}, bf16[192,3072]{1,0:T(8,128)(2,1)}, u32[]{:S(2)}, u32[]{:S(2)}) %collective-permute-start) | collective-permute-done | bytes 1179680 | tf_op jit(solution)/shard_map/ppermute | solution.py:505
  34.5 1.5 collective-permute-done.1.refs_0_.refs_8_
  36.3 1.7 collective-permute-start.7
  38.0 3.8 %collective-permute-start.4 = (bf16[192,3072]{1,0:T(8,128)(2,1)}, bf16[192,3072]{1,0:T(8,128)(2,1)}, u32[]{:S(2)}, u32[]{:S(2)}) collective-permute-start(bf16[192,3072]{1,0:T(8,128)(2,1)} %broadcast_select_fusion.3), channel_id=1, source_target_pairs={{0,4},{4,0},{8,12},{12,8},{1,5},{5,1},{9,13},{13,9},{2,6},{6,2},{1... | collective-permute-start | bytes 3538952 | tf_op jit(solution)/shard_map/ppermute | solution.py:496
  41.8 1.7 collective-permute-start.5
  43.4 2.5 %copy.8 = bf16[24,8,8,384]{3,1,2,0:T(8,128)(2,1)} copy(bf16[24,8,8,384]{3,1,0,2:T(8,128)(2,1)} %bitcast.21) | data formatting | bytes 2359296
  45.9 4.8 %shard_map.38 = (bf16[192,3072]{1,0:T(8,128)(2,1)}, bf16[192,3072]{1,0:T(8,128)(2,1)}) custom-call(bf16[1,384,6144]{2,1,0:T(8,128)(2,1)} %tokens_ref.2, f32[1,6144]{1,0:T(1,128)} %bitcast.36, bf16[6,1536,384]{2,1,0:T(8,128)(2,1)} %bitcast.25), custom_call_target="tpu_custom_call" | custom-call | flops 9437184 | bytes 4718592 | tf_op jit(solution)/shard_map/pallas_call | solution.py:147
  50.7 1.4 broadcast_select_fusion.2
  52.1 14.5 %collective-permute-done.4.refs_25_.refs_0_.refs_16_ = bf16[192,3072]{1,0:T(8,128)(2,1)} collective-permute-done((bf16[192,3072]{1,0:T(8,128)(2,1)}, bf16[192,3072]{1,0:T(8,128)(2,1)}, u32[]{:S(2)}, u32[]{:S(2)}) %collective-permute-start.4) | collective-permute-done | bytes 1179680 | tf_op jit(solution)/shard_map/ppermute | solution.py:496
  66.7 4.2 %collective-permute-start.10 = (bf16[192,3072]{1,0:T(8,128)(2,1)S(1)}, bf16[192,3072]{1,0:T(8,128)(2,1)S(1)}, u32[]{:S(2)}, u32[]{:S(2)}) collective-permute-start(bf16[192,3072]{1,0:T(8,128)(2,1)S(1)} %broadcast_select_fusion.2), channel_id=1, source_target_pairs={{0,4},{4,0},{8,12},{12,8},{1,5},{5,1},{9,13},{13,9},{2,6},{6,2},{1... | collective-permute-start | bytes 3538952 | tf_op jit(solution)/shard_map/ppermute | solution.py:496
  70.9 0.7 collective-permute-start.11
  71.6 1.6 collective-permute-start.12
  73.2 0.5 collective-permute-start.13
  73.7 1.2 broadcast_select_fusion.1
  74.9 22.5 %collective-permute-done.10.refs_28_.refs_1_.refs_17_ = bf16[192,3072]{1,0:T(8,128)(2,1)S(1)} collective-permute-done((bf16[192,3072]{1,0:T(8,128)(2,1)S(1)}, bf16[192,3072]{1,0:T(8,128)(2,1)S(1)}, u32[]{:S(2)}, u32[]{:S(2)}) %collective-permute-start.10) | collective-permute-done | bytes 1179680 | tf_op jit(solution)/shard_map/ppermute | solution.py:496
  97.5 2.5 %collective-permute-done.12.refs_4_.refs_12_ = bf16[192,3072]{1,0:T(8,128)(2,1)S(1)} collective-permute-done((bf16[192,3072]{1,0:T(8,128)(2,1)}, bf16[192,3072]{1,0:T(8,128)(2,1)S(1)}, u32[]{:S(2)}, u32[]{:S(2)}) %collective-permute-start.12) | collective-permute-done | bytes 1179680 | tf_op jit(solution)/shard_map/ppermute | solution.py:505
  99.9 1.3 collective-permute-done.13.refs_5_.refs_13_
  101.3 1.1 collective-permute-start.18
  102.4 0.5 collective-permute-start.19
  102.9 2.9 %collective-permute-start.16 = (bf16[1536,384]{1,0:T(8,128)(2,1)}, bf16[1536,384]{1,0:T(8,128)(2,1)}, u32[]{:S(2)}, u32[]{:S(2)}) collective-permute-start(bf16[1536,384]{1,0:T(8,128)(2,1)} %broadcast_select_fusion.1), channel_id=1, source_target_pairs={{0,4},{4,0},{8,12},{12,8},{1,5},{5,1},{9,13},{13,9},{2,6},{6,2},{1... | collective-permute-start | bytes 3538952 | tf_op jit(solution)/shard_map/ppermute | solution.py:496
  105.9 1.7 collective-permute-start.17
  107.5 1.0 copy-done.6
  108.6 2.8 %pad_maximum_fusion = bf16[384,3072]{1,0:T(8,128)(2,1)} fusion(bf16[192,3072]{1,0:T(8,128)(2,1)S(1)} %collective-permute-done.10.refs_28_.refs_1_.refs_17_, bf16[192,3072]{1,0:T(8,128)(2,1)} %collective-permute-done.4.refs_25_.refs_0_.refs_16_), kind=kLoop, calls=%fused_computation | loop fusion | flops 4718592 | bytes 4718592 | tf_op jit(solution)/shard_map/concatenate | solution.py:579
  111.4 2.5 %broadcast_select_fusion = bf16[1536,384]{1,0:T(8,128)(2,1)} fusion(bf16[1536,384]{1,0:T(8,128)(2,1)S(1)} %collective-permute-done.11.refs_14_.refs_22_, bf16[1536,384]{1,0:T(8,128)(2,1)} %get-tuple-element.210.refs_11_.refs_19_.refs_10_, pred[]{:T(512)S(6)} %or.3), kind=kLoop, calls=%fused_computation.2 | loop fusion | flops 589824 | bytes 3538945 | tf_op jit(solution)/shard_map/jit(_where)/select_n | solution.py:493
  113.8 14.5 %shard_map.39 = (bf16[384,128]{1,0:T(8,128)(2,1)}, bf16[384,128]{1,0:T(8,128)(2,1)}, f32[768,384]{1,0:T(8,128)}, f32[768,384]{1,0:T(8,128)}) custom-call(s32[2]{0:T(128)} %pad_add_fusion.role_ref, bf16[192,3072]{1,0:T(8,128)(2,1)} %get-tuple-element.124.refs_0_.refs_8_, bf16[192,3072]{1,0:T(8,128)(2,1)} %get-tuple-element.132.refs_1_.refs_9_, ...), custom_call_target="tpu_custom_call" | custom-call | flops 6341787648 | tf_op jit(solution)/shard_map/pallas_call | solution.py:406
  128.3 3.9 %collective-permute-done.16.refs_27_.refs_17_ = bf16[1536,384]{1,0:T(8,128)(2,1)} collective-permute-done((bf16[1536,384]{1,0:T(8,128)(2,1)}, bf16[1536,384]{1,0:T(8,128)(2,1)}, u32[]{:S(2)}, u32[]{:S(2)}) %collective-permute-start.16) | collective-permute-done | bytes 1179680 | tf_op jit(solution)/shard_map/ppermute | solution.py:496
  132.4 1.0 collective-permute-start.24
  133.4 1.5 collective-permute-start.25
  134.9 3.6 %collective-permute-start.22 = (bf16[1536,384]{1,0:T(8,128)(2,1)}, bf16[1536,384]{1,0:T(8,128)(2,1)}, u32[]{:S(2)}, u32[]{:S(2)}) collective-permute-start(bf16[1536,384]{1,0:T(8,128)(2,1)} %broadcast_select_fusion), channel_id=1, source_target_pairs={{0,4},{4,0},{8,12},{12,8},{1,5},{5,1},{9,13},{13,9},{2,6},{6,2},{1... | collective-permute-start | bytes 3538952 | tf_op jit(solution)/shard_map/ppermute | solution.py:496
  138.5 1.7 collective-permute-start.23
  140.2 20.0 %shard_map.40 = (bf16[384,128]{1,0:T(8,128)(2,1)}, bf16[384,128]{1,0:T(8,128)(2,1)}, f32[768,384]{1,0:T(8,128)}, f32[768,384]{1,0:T(8,128)}, f32[768,384]{1,0:T(8,128)}, /*index=5*/f32[768,384]{1,0:T(8,128)}) custom-call(s32[2]{0:T(128)} %pad_add_fusion.role_ref, bf16[192,3072]{1,0:T(8,128)(2,1)} %collective-permute-done.1.refs_0_.refs_8_, ...), custom_call_target="tpu_custom_call" | custom-call | flops 9965666304 | tf_op jit(solution)/shard_map/pallas_call | solution.py:406
  160.2 4.6 %collective-permute-done.22.refs_18_.refs_8_ = bf16[1536,384]{1,0:T(8,128)(2,1)} collective-permute-done((bf16[1536,384]{1,0:T(8,128)(2,1)}, bf16[1536,384]{1,0:T(8,128)(2,1)}, u32[]{:S(2)}, u32[]{:S(2)}) %collective-permute-start.22) | collective-permute-done | bytes 1179680 | tf_op jit(solution)/shard_map/ppermute | solution.py:496
  164.9 0.6 collective-permute-start.32
  165.5 1.3 collective-permute-start.29
  166.8 1.7 collective-permute-start.30
  168.5 1.1 collective-permute-start.31
  169.6 13.1 %shard_map.41 = (bf16[384,128]{1,0:T(8,128)(2,1)}, bf16[384,128]{1,0:T(8,128)(2,1)}, f32[768,384]{1,0:T(8,128)}, bf16[384,128]{1,0:T(8,128)(2,1)}, bf16[384,128]{1,0:T(8,128)(2,1)}, /*index=5*/f32[768,384]{1,0:T(8,128)}) custom-call(s32[2]{0:T(128)} %pad_add_fusion.role_ref, bf16[192,3072]{1,0:T(8,128)(2,1)} %get-tuple-element.124.refs_0_.refs_8_, ...), custom_call_target="tpu_custom_call" | custom-call | flops 3623878656 | tf_op jit(solution)/shard_map/pallas_call | solution.py:406
  182.7 8.8 %shard_map.42.refs_28_ = f32[768,384]{1,0:T(8,128)} custom-call(s32[2]{0:T(128)} %pad_add_fusion.role_ref, bf16[192,3072]{1,0:T(8,128)(2,1)} %collective-permute-done.4.refs_25_.refs_0_.refs_16_, bf16[192,3072]{1,0:T(8,128)(2,1)} %copy-done.2, bf16[384,3072]{1,0:T(8,128)(2,1)} %collective-permute-done.26.refs_2_.refs_3_.refs_18_.refs_19_, ...), custom_call_target="tpu_custom_call" | custom-call | flops 2717908992 | tf_op jit(solution)/shard_map/pallas_call | solution.py:406
  191.5 5.5 %collective-permute-done.29.refs_25_ = bf16[1536,384]{1,0:T(8,128)(2,1)} collective-permute-done((bf16[1536,384]{1,0:T(8,128)(2,1)}, bf16[1536,384]{1,0:T(8,128)(2,1)}, u32[]{:S(2)}, u32[]{:S(2)}) %collective-permute-start.29) | collective-permute-done | bytes 1179680 | tf_op jit(solution)/shard_map/ppermute | solution.py:499
  197.1 0.5 collective-permute-start.40
  197.7 12.9 %shard_map.43 = (bf16[384,384]{1,0:T(8,128)(2,1)}, bf16[384,384]{1,0:T(8,128)(2,1)}, bf16[384,384]{1,0:T(8,128)(2,1)}, bf16[384,384]{1,0:T(8,128)(2,1)}, bf16[38...) custom-call(s32[2]{0:T(128)} %pad_add_fusion.role_ref, bf16[192,3072]{1,0:T(8,128)(2,1)} %get-tuple-element.124.refs_0_.refs_8_, ...), custom_call_target="tpu_custom_call" | custom-call | flops 2717908992 | tf_op jit(solution)/shard_map/pallas_call | solution.py:406
  210.6 1.1 collective-permute-start.34
  211.7 1.5 collective-permute-start.35
  213.2 0.9 collective-permute-start.36
  214.1 1.3 collective-permute-start.37
  215.4 1.6 collective-permute-start.38
  217.0 10.2 %shard_map.44 = (bf16[384,128]{1,0:T(8,128)(2,1)}, bf16[384,128]{1,0:T(8,128)(2,1)}) custom-call(s32[2]{0:T(128)} %pad_add_fusion.role_ref, bf16[192,3072]{1,0:T(8,128)(2,1)} %collective-permute-done.19.refs_0_, bf16[192,3072]{1,0:T(8,128)(2,1)} %collective-permute-done.25.refs_1_, bf16[192,3072]{1,0:T(8,128)(2,1)} %collective-permute-done.33.refs_2_, ...), custom_call_target="tpu_custom_call" | custom-call | flops 3623878656 | tf_op jit(solution)/shard_map/pallas_call | solution.py:406
  227.2 1.3 collective-permute-start.42
  228.5 1.3 collective-permute-start.43
  229.9 0.7 stack.34.place_ref
  230.6 7.4 %collective-permute-done.42.refs_6_ = bf16[384,128]{1,0:T(8,128)(2,1)S(1)} collective-permute-done((bf16[384,128]{1,0:T(8,128)(2,1)}, bf16[384,128]{1,0:T(8,128)(2,1)S(1)}, u32[]{:S(2)}, u32[]{:S(2)}) %collective-permute-start.42) | collective-permute-done | bytes 98336 | tf_op jit(solution)/shard_map/ppermute | solution.py:663
  238.0 1.8 collective-permute-done.43.refs_7_
  239.9 0.6 copy-done.15
  240.5 3.1 %shard_map.45 = bf16[384,1536]{1,0:T(8,128)(2,1)} custom-call(s32[5]{0:T(128)} %stack.34.place_ref, bf16[384,384]{1,0:T(8,128)(2,1)} %get-tuple-element.225.refs_0_, bf16[384,384]{1,0:T(8,128)(2,1)} %copy-done.10, bf16[384,384]{1,0:T(8,128)(2,1)} %copy-done.11, bf16[384,384]{1,0:T(8,128)(2,1)} %collective-permute-done.36.refs_3_, ...), custom_call_target="tpu_custom_call" | custom-call | bytes 2359296 | tf_op jit(solution)/shard_map/pallas_call | solution.py:467
  (75 shorter events, 1.0 us)
Async XLA Ops:
  5.2 29.3 %collective-permute-start = (bf16[192,3072]{1,0:T(8,128)(2,1)}, bf16[192,3072]{1,0:T(8,128)(2,1)}, u32[]{:S(2)}, u32[]{:S(2)}) collective-permute-start(bf16[192,3072]{1,0:T(8,128)(2,1)} %get-tuple-element.124.refs_0_.refs_8_), channel_id=1, source_target_pairs={{0,2},{2,0},{1,3},{3,1},{4,6},{6,4},{5,7},{7,5},{8,10},{10,8},{9,1... | collective-permute-start | bytes 3538952 | tf_op jit(solution)/shard_map/ppermute | solution.py:505
  8.2 27.7 %collective-permute-start.1 = (bf16[192,3072]{1,0:T(8,128)(2,1)}, bf16[192,3072]{1,0:T(8,128)(2,1)}, u32[]{:S(2)}, u32[]{:S(2)}) collective-permute-start(bf16[192,3072]{1,0:T(8,128)(2,1)} %get-tuple-element.124.refs_0_.refs_8_), channel_id=1, source_target_pairs={{0,16},{16,0},{1,17},{17,1},{2,18},{18,2},{3,19},{19,3},{4,20},{20... | collective-permute-start | bytes 3538952 | tf_op jit(solution)/shard_map/ppermute | solution.py:506
  9.7 28.3 %collective-permute-start.2 = (bf16[1536,384]{1,0:T(8,128)(2,1)}, bf16[1536,384]{1,0:T(8,128)(2,1)}, u32[]{:S(2)}, u32[]{:S(2)}) collective-permute-start(bf16[1536,384]{1,0:T(8,128)(2,1)} %get-tuple-element.128.refs_8_.refs_10_.refs_16_.refs_18_), channel_id=1, source_target_pairs={{0,4},{4,0},{8,12},{12,8},{1,5},{5,1},{9,13},{13,9},{2,6},{6,2},{1... | collective-permute-start | bytes 3538952 | tf_op jit(solution)/shard_map/ppermute | solution.py:496
  11.3 26.7 %collective-permute-start.3 = (bf16[1536,384]{1,0:T(8,128)(2,1)}, bf16[1536,384]{1,0:T(8,128)(2,1)}, u32[]{:S(2)}, u32[]{:S(2)}) collective-permute-start(bf16[1536,384]{1,0:T(8,128)(2,1)} %get-tuple-element.128.refs_8_.refs_10_.refs_16_.refs_18_), channel_id=1, source_target_pairs={{4,8},{8,4},{5,9},{9,5},{6,10},{10,6},{7,11},{11,7},{20,24},{24,20... | collective-permute-start | bytes 3538952 | tf_op jit(solution)/shard_map/ppermute | solution.py:502
  15.9 57.8 %copy-start = (bf16[1,1536,384]{2,1,0:T(8,128)(2,1)}, bf16[1,1536,384]{2,1,0:T(8,128)(2,1)S(1)}, u32[]{:S(2)}) copy-start(bf16[1,1536,384]{2,1,0:T(8,128)(2,1)S(1)} %get-tuple-element.238) | copy-start | bytes 3538948
  15.9 2.1 copy-start.1
  35.9 7.5 %collective-permute-start.8 = (bf16[192,3072]{1,0:T(8,128)(2,1)}, bf16[192,3072]{1,0:T(8,128)(2,1)}, u32[]{:S(2)}, u32[]{:S(2)}) collective-permute-start(bf16[192,3072]{1,0:T(8,128)(2,1)} %collective-permute-done.refs_4_.refs_12_), channel_id=1, source_target_pairs={{0,1},{1,0},{2,3},{3,2},{4,5},{5,4},{6,7},{7,6},{8,9},{9,8},{10,11... | collective-permute-start | bytes 3538952 | tf_op jit(solution)/shard_map/ppermute | solution.py:513
  35.9 30.6 %collective-permute-start.6 = (bf16[192,3072]{1,0:T(8,128)(2,1)}, bf16[192,3072]{1,0:T(8,128)(2,1)}, u32[]{:S(2)}, u32[]{:S(2)}) collective-permute-start(bf16[192,3072]{1,0:T(8,128)(2,1)} %get-tuple-element.132.refs_1_.refs_9_), channel_id=1, source_target_pairs={{0,2},{2,0},{1,3},{3,1},{4,6},{6,4},{5,7},{7,5},{8,10},{10,8},{9,1... | collective-permute-start | bytes 3538952 | tf_op jit(solution)/shard_map/ppermute | solution.py:505
  36.3 30.3 %collective-permute-start.7 = (bf16[192,3072]{1,0:T(8,128)(2,1)}, bf16[192,3072]{1,0:T(8,128)(2,1)}, u32[]{:S(2)}, u32[]{:S(2)}) collective-permute-start(bf16[192,3072]{1,0:T(8,128)(2,1)} %get-tuple-element.132.refs_1_.refs_9_), channel_id=1, source_target_pairs={{0,16},{16,0},{1,17},{17,1},{2,18},{18,2},{3,19},{19,3},{4,20},{20... | collective-permute-start | bytes 3538952 | tf_op jit(solution)/shard_map/ppermute | solution.py:506
  38.0 28.6 %collective-permute-start.4 = (bf16[192,3072]{1,0:T(8,128)(2,1)}, bf16[192,3072]{1,0:T(8,128)(2,1)}, u32[]{:S(2)}, u32[]{:S(2)}) collective-permute-start(bf16[192,3072]{1,0:T(8,128)(2,1)} %broadcast_select_fusion.3), channel_id=1, source_target_pairs={{0,4},{4,0},{8,12},{12,8},{1,5},{5,1},{9,13},{13,9},{2,6},{6,2},{1... | collective-permute-start | bytes 3538952 | tf_op jit(solution)/shard_map/ppermute | solution.py:496
  41.8 24.8 %collective-permute-start.5 = (bf16[1536,384]{1,0:T(8,128)(2,1)}, bf16[1536,384]{1,0:T(8,128)(2,1)}, u32[]{:S(2)}, u32[]{:S(2)}) collective-permute-start(bf16[1536,384]{1,0:T(8,128)(2,1)} %collective-permute-done.2.refs_15_.refs_16_.refs_23_.refs_26_), channel_id=1, source_target_pairs={{4,8},{8,4},{5,9},{9,5},{6,10},{10,6},{7,11},{11,7},{20,24},{24,20... | collective-permute-start | bytes 3538952 | tf_op jit(solution)/shard_map/ppermute | solution.py:502
  43.4 23.1 %collective-permute-start.9 = (bf16[192,3072]{1,0:T(8,128)(2,1)}, bf16[192,3072]{1,0:T(8,128)(2,1)}, u32[]{:S(2)}, u32[]{:S(2)}) collective-permute-start(bf16[192,3072]{1,0:T(8,128)(2,1)} %collective-permute-done.1.refs_0_.refs_8_), channel_id=1, source_target_pairs={{0,1},{1,0},{2,3},{3,2},{4,5},{5,4},{6,7},{7,6},{8,9},{9,8},{10,11... | collective-permute-start | bytes 3538952 | tf_op jit(solution)/shard_map/ppermute | solution.py:513
  66.6 7.1 %collective-permute-start.14 = (bf16[192,3072]{1,0:T(8,128)(2,1)}, bf16[192,3072]{1,0:T(8,128)(2,1)}, u32[]{:S(2)}, u32[]{:S(2)}) collective-permute-start(bf16[192,3072]{1,0:T(8,128)(2,1)} %collective-permute-done.7.refs_1_.refs_9_), channel_id=1, source_target_pairs={{0,1},{1,0},{2,3},{3,2},{4,5},{5,4},{6,7},{7,6},{8,9},{9,8},{10,11... | collective-permute-start | bytes 3538952 | tf_op jit(solution)/shard_map/ppermute | solution.py:513
  66.7 30.8 %collective-permute-start.10 = (bf16[192,3072]{1,0:T(8,128)(2,1)S(1)}, bf16[192,3072]{1,0:T(8,128)(2,1)S(1)}, u32[]{:S(2)}, u32[]{:S(2)}) collective-permute-start(bf16[192,3072]{1,0:T(8,128)(2,1)S(1)} %broadcast_select_fusion.2), channel_id=1, source_target_pairs={{0,4},{4,0},{8,12},{12,8},{1,5},{5,1},{9,13},{13,9},{2,6},{6,2},{1... | collective-permute-start | bytes 3538952 | tf_op jit(solution)/shard_map/ppermute | solution.py:496
  70.9 26.6 %collective-permute-start.11 = (bf16[1536,384]{1,0:T(8,128)(2,1)S(1)}, bf16[1536,384]{1,0:T(8,128)(2,1)S(1)}, u32[]{:S(2)}, u32[]{:S(2)}) collective-permute-start(bf16[1536,384]{1,0:T(8,128)(2,1)S(1)} %bitcast.27), channel_id=1, source_target_pairs={{4,8},{8,4},{5,9},{9,5},{6,10},{10,6},{7,11},{11,7},{20,24},{24,20... | collective-permute-start | bytes 3538952 | tf_op jit(solution)/shard_map/ppermute | solution.py:502
  71.6 28.3 %collective-permute-start.12 = (bf16[192,3072]{1,0:T(8,128)(2,1)}, bf16[192,3072]{1,0:T(8,128)(2,1)S(1)}, u32[]{:S(2)}, u32[]{:S(2)}) collective-permute-start(bf16[192,3072]{1,0:T(8,128)(2,1)} %collective-permute-done.1.refs_0_.refs_8_), channel_id=1, source_target_pairs={{0,2},{2,0},{1,3},{3,1},{4,6},{6,4},{5,7},{7,5},{8,10},{10,8},{9,1... | collective-permute-start | bytes 3538952 | tf_op jit(solution)/shard_map/ppermute | solution.py:505
  73.2 28.1 %collective-permute-start.13 = (bf16[192,3072]{1,0:T(8,128)(2,1)}, bf16[192,3072]{1,0:T(8,128)(2,1)}, u32[]{:S(2)}, u32[]{:S(2)}) collective-permute-start(bf16[192,3072]{1,0:T(8,128)(2,1)} %collective-permute-done.6.refs_5_.refs_13_), channel_id=1, source_target_pairs={{0,16},{16,0},{1,17},{17,1},{2,18},{18,2},{3,19},{19,3},{4,20},{20... | collective-permute-start | bytes 3538952 | tf_op jit(solution)/shard_map/ppermute | solution.py:506
  73.7 27.6 %collective-permute-start.15 = (bf16[192,3072]{1,0:T(8,128)(2,1)}, bf16[192,3072]{1,0:T(8,128)(2,1)S(1)}, u32[]{:S(2)}, u32[]{:S(2)}) collective-permute-start(bf16[192,3072]{1,0:T(8,128)(2,1)} %collective-permute-done.6.refs_5_.refs_13_), channel_id=1, source_target_pairs={{0,1},{1,0},{2,3},{3,2},{4,5},{5,4},{6,7},{7,6},{8,9},{9,8},{10,11... | collective-permute-start | bytes 3538952 | tf_op jit(solution)/shard_map/ppermute | solution.py:513
  97.5 13.9 %copy-start.2 = (bf16[192,3072]{1,0:T(8,128)(2,1)}, bf16[192,3072]{1,0:T(8,128)(2,1)S(1)}, u32[]{:S(2)}) copy-start(bf16[192,3072]{1,0:T(8,128)(2,1)S(1)} %collective-permute-done.10.refs_28_.refs_1_.refs_17_) | copy-start | bytes 3538948
  97.5 13.9 %copy-start.8 = (bf16[1536,384]{1,0:T(8,128)(2,1)}, bf16[1536,384]{1,0:T(8,128)(2,1)S(1)}, u32[]{:S(2)}) copy-start(bf16[1536,384]{1,0:T(8,128)(2,1)S(1)} %collective-permute-done.11.refs_14_.refs_22_) | copy-start | bytes 3538948
  99.9 1.3 copy-start.4
  101.3 6.3 %copy-start.5 = (bf16[192,3072]{1,0:T(8,128)(2,1)}, bf16[192,3072]{1,0:T(8,128)(2,1)S(1)}, u32[]{:S(2)}) copy-start(bf16[192,3072]{1,0:T(8,128)(2,1)S(1)} %collective-permute-done.15.refs_7_.refs_15_) | copy-start | bytes 3538948
  101.3 6.3 %collective-permute-start.20 = (bf16[192,3072]{1,0:T(8,128)(2,1)S(1)}, bf16[192,3072]{1,0:T(8,128)(2,1)S(1)}, u32[]{:S(2)}, u32[]{:S(2)}) collective-permute-start(bf16[192,3072]{1,0:T(8,128)(2,1)S(1)} %collective-permute-done.12.refs_4_.refs_12_), channel_id=1, source_target_pairs={{0,1},{1,0},{2,3},{3,2},{4,5},{5,4},{6,7},{7,6},{8,9},{9,8},{10,11... | collective-permute-start | bytes 3538952 | tf_op jit(solution)/shard_map/ppermute | solution.py:513
  101.3 30.9 %collective-permute-start.18 = (bf16[192,3072]{1,0:T(8,128)(2,1)}, bf16[192,3072]{1,0:T(8,128)(2,1)}, u32[]{:S(2)}, u32[]{:S(2)}) collective-permute-start(bf16[192,3072]{1,0:T(8,128)(2,1)} %collective-permute-done.4.refs_25_.refs_0_.refs_16_), channel_id=1, source_target_pairs={{0,2},{2,0},{1,3},{3,1},{4,6},{6,4},{5,7},{7,5},{8,10},{10,8},{9,1... | collective-permute-start | bytes 3538952 | tf_op jit(solution)/shard_map/ppermute | solution.py:505
  102.4 29.8 %collective-permute-start.19 = (bf16[192,3072]{1,0:T(8,128)(2,1)}, bf16[192,3072]{1,0:T(8,128)(2,1)}, u32[]{:S(2)}, u32[]{:S(2)}) collective-permute-start(bf16[192,3072]{1,0:T(8,128)(2,1)} %collective-permute-done.4.refs_25_.refs_0_.refs_16_), channel_id=1, source_target_pairs={{0,16},{16,0},{1,17},{17,1},{2,18},{18,2},{3,19},{19,3},{4,20},{20... | collective-permute-start | bytes 3538952 | tf_op jit(solution)/shard_map/ppermute | solution.py:506
  102.9 29.3 %collective-permute-start.16 = (bf16[1536,384]{1,0:T(8,128)(2,1)}, bf16[1536,384]{1,0:T(8,128)(2,1)}, u32[]{:S(2)}, u32[]{:S(2)}) collective-permute-start(bf16[1536,384]{1,0:T(8,128)(2,1)} %broadcast_select_fusion.1), channel_id=1, source_target_pairs={{0,4},{4,0},{8,12},{12,8},{1,5},{5,1},{9,13},{13,9},{2,6},{6,2},{1... | collective-permute-start | bytes 3538952 | tf_op jit(solution)/shard_map/ppermute | solution.py:496
  105.9 26.4 %collective-permute-start.17 = (bf16[1536,384]{1,0:T(8,128)(2,1)}, bf16[1536,384]{1,0:T(8,128)(2,1)}, u32[]{:S(2)}, u32[]{:S(2)}) collective-permute-start(bf16[1536,384]{1,0:T(8,128)(2,1)} %get-tuple-element.210.refs_11_.refs_19_.refs_10_), channel_id=1, source_target_pairs={{4,8},{8,4},{5,9},{9,5},{6,10},{10,6},{7,11},{11,7},{20,24},{24,20... | collective-permute-start | bytes 3538952 | tf_op jit(solution)/shard_map/ppermute | solution.py:502
  107.5 1.0 copy-start.6
  108.6 23.7 %collective-permute-start.21 = (bf16[192,3072]{1,0:T(8,128)(2,1)}, bf16[192,3072]{1,0:T(8,128)(2,1)}, u32[]{:S(2)}, u32[]{:S(2)}) collective-permute-start(bf16[192,3072]{1,0:T(8,128)(2,1)} %collective-permute-done.13.refs_5_.refs_13_), channel_id=1, source_target_pairs={{0,1},{1,0},{2,3},{3,2},{4,5},{5,4},{6,7},{7,6},{8,9},{9,8},{10,11... | collective-permute-start | bytes 3538952 | tf_op jit(solution)/shard_map/ppermute | solution.py:513
  113.8 18.5 %copy-start.3 = (bf16[192,3072]{1,0:T(8,128)(2,1)S(1)}, bf16[192,3072]{1,0:T(8,128)(2,1)}, u32[]{:S(2)}) copy-start(bf16[192,3072]{1,0:T(8,128)(2,1)} %copy-done.2) | copy-start | bytes 3538948
  132.3 8.0 %collective-permute-start.26 = (bf16[384,3072]{1,0:T(8,128)(2,1)}, bf16[384,3072]{1,0:T(8,128)(2,1)}, u32[]{:S(2)}, u32[]{:S(2)}) collective-permute-start(bf16[384,3072]{1,0:T(8,128)(2,1)} %pad_maximum_fusion), channel_id=1, source_target_pairs={{0,1},{1,0},{2,3},{3,2},{4,5},{5,4},{6,7},{7,6},{8,9},{9,8},{10,11... | collective-permute-start | bytes 7077896 | tf_op jit(solution)/shard_map/ppermute | solution.py:513
  132.4 32.5 %collective-permute-start.24 = (bf16[192,3072]{1,0:T(8,128)(2,1)S(1)}, bf16[192,3072]{1,0:T(8,128)(2,1)}, u32[]{:S(2)}, u32[]{:S(2)}) collective-permute-start(bf16[192,3072]{1,0:T(8,128)(2,1)S(1)} %copy-done.3), channel_id=1, source_target_pairs={{0,2},{2,0},{1,3},{3,1},{4,6},{6,4},{5,7},{7,5},{8,10},{10,8},{9,1... | collective-permute-start | bytes 3538952 | tf_op jit(solution)/shard_map/ppermute | solution.py:505
  133.4 31.5 %collective-permute-start.25 = (bf16[192,3072]{1,0:T(8,128)(2,1)S(1)}, bf16[192,3072]{1,0:T(8,128)(2,1)}, u32[]{:S(2)}, u32[]{:S(2)}) collective-permute-start(bf16[192,3072]{1,0:T(8,128)(2,1)S(1)} %copy-done.3), channel_id=1, source_target_pairs={{0,16},{16,0},{1,17},{17,1},{2,18},{18,2},{3,19},{19,3},{4,20},{20... | collective-permute-start | bytes 3538952 | tf_op jit(solution)/shard_map/ppermute | solution.py:506
  134.9 29.9 %collective-permute-start.22 = (bf16[1536,384]{1,0:T(8,128)(2,1)}, bf16[1536,384]{1,0:T(8,128)(2,1)}, u32[]{:S(2)}, u32[]{:S(2)}) collective-permute-start(bf16[1536,384]{1,0:T(8,128)(2,1)} %broadcast_select_fusion), channel_id=1, source_target_pairs={{0,4},{4,0},{8,12},{12,8},{1,5},{5,1},{9,13},{13,9},{2,6},{6,2},{1... | collective-permute-start | bytes 3538952 | tf_op jit(solution)/shard_map/ppermute | solution.py:496
  138.5 26.3 %collective-permute-start.23 = (bf16[1536,384]{1,0:T(8,128)(2,1)}, bf16[1536,384]{1,0:T(8,128)(2,1)}, u32[]{:S(2)}, u32[]{:S(2)}) collective-permute-start(bf16[1536,384]{1,0:T(8,128)(2,1)} %collective-permute-done.16.refs_27_.refs_17_), channel_id=1, source_target_pairs={{4,8},{8,4},{5,9},{9,5},{6,10},{10,6},{7,11},{11,7},{20,24},{24,20... | collective-permute-start | bytes 3538952 | tf_op jit(solution)/shard_map/ppermute | solution.py:502
  140.2 24.6 %collective-permute-start.27 = (bf16[192,3072]{1,0:T(8,128)(2,1)}, bf16[192,3072]{1,0:T(8,128)(2,1)}, u32[]{:S(2)}, u32[]{:S(2)}) collective-permute-start(bf16[192,3072]{1,0:T(8,128)(2,1)} %collective-permute-done.18.refs_4_.refs_20_), channel_id=1, source_target_pairs={{0,1},{1,0},{2,3},{3,2},{4,5},{5,4},{6,7},{7,6},{8,9},{9,8},{10,11... | collective-permute-start | bytes 3538952 | tf_op jit(solution)/shard_map/ppermute | solution.py:513
  164.9 4.7 %collective-permute-start.28 = (bf16[192,3072]{1,0:T(8,128)(2,1)}, bf16[192,3072]{1,0:T(8,128)(2,1)S(1)}, u32[]{:S(2)}, u32[]{:S(2)}) collective-permute-start(bf16[192,3072]{1,0:T(8,128)(2,1)} %collective-permute-done.24.refs_5_.refs_21_), channel_id=1, source_target_pairs={{0,1},{1,0},{2,3},{3,2},{4,5},{5,4},{6,7},{7,6},{8,9},{9,8},{10,11... | collective-permute-start | bytes 3538952 | tf_op jit(solution)/shard_map/ppermute | solution.py:513
  164.9 32.1 %collective-permute-start.32 = (bf16[192,3072]{1,0:T(8,128)(2,1)}, bf16[192,3072]{1,0:T(8,128)(2,1)}, u32[]{:S(2)}, u32[]{:S(2)}) collective-permute-start(bf16[192,3072]{1,0:T(8,128)(2,1)} %collective-permute-done.24.refs_5_.refs_21_), channel_id=1, source_target_pairs={{0,16},{16,0},{1,17},{17,1},{2,18},{18,2},{3,19},{19,3},{4,20},{20... | collective-permute-start | bytes 3538952 | tf_op jit(solution)/shard_map/ppermute | solution.py:506
  165.5 31.5 %collective-permute-start.29 = (bf16[1536,384]{1,0:T(8,128)(2,1)}, bf16[1536,384]{1,0:T(8,128)(2,1)}, u32[]{:S(2)}, u32[]{:S(2)}) collective-permute-start(bf16[1536,384]{1,0:T(8,128)(2,1)} %collective-permute-done.23.refs_16_), channel_id=1, source_target_pairs={{4,0},{8,12},{5,1},{9,13},{6,2},{10,14},{7,3},{11,15},{20,16},{24,... | collective-permute-start | bytes 3538952 | tf_op jit(solution)/shard_map/ppermute | solution.py:499
  166.8 30.2 %collective-permute-start.30 = (bf16[1536,384]{1,0:T(8,128)(2,1)}, bf16[1536,384]{1,0:T(8,128)(2,1)}, u32[]{:S(2)}, u32[]{:S(2)}) collective-permute-start(bf16[1536,384]{1,0:T(8,128)(2,1)} %collective-permute-done.22.refs_18_.refs_8_), channel_id=1, source_target_pairs={{4,8},{8,4},{5,9},{9,5},{6,10},{10,6},{7,11},{11,7},{20,24},{24,20... | collective-permute-start | bytes 3538952 | tf_op jit(solution)/shard_map/ppermute | solution.py:502
  168.5 28.5 %collective-permute-start.31 = (bf16[192,3072]{1,0:T(8,128)(2,1)}, bf16[192,3072]{1,0:T(8,128)(2,1)}, u32[]{:S(2)}, u32[]{:S(2)}) collective-permute-start(bf16[192,3072]{1,0:T(8,128)(2,1)} %collective-permute-done.19.refs_0_), channel_id=1, source_target_pairs={{0,2},{2,0},{1,3},{3,1},{4,6},{6,4},{5,7},{7,5},{8,10},{10,8},{9,1... | collective-permute-start | bytes 3538952 | tf_op jit(solution)/shard_map/ppermute | solution.py:505
  169.6 13.1 %copy-start.7 = (bf16[192,3072]{1,0:T(8,128)(2,1)}, bf16[192,3072]{1,0:T(8,128)(2,1)S(1)}, u32[]{:S(2)}) copy-start(bf16[192,3072]{1,0:T(8,128)(2,1)S(1)} %collective-permute-done.28.refs_7_.refs_23_) | copy-start | bytes 3538948
  169.6 27.4 %collective-permute-start.33 = (bf16[192,3072]{1,0:T(8,128)(2,1)}, bf16[192,3072]{1,0:T(8,128)(2,1)}, u32[]{:S(2)}, u32[]{:S(2)}) collective-permute-start(bf16[192,3072]{1,0:T(8,128)(2,1)} %collective-permute-done.19.refs_0_), channel_id=1, source_target_pairs={{0,1},{1,0},{2,3},{3,2},{4,5},{5,4},{6,7},{7,6},{8,9},{9,8},{10,11... | collective-permute-start | bytes 3538952 | tf_op jit(solution)/shard_map/ppermute | solution.py:513
  197.0 16.2 %collective-permute-start.39 = (bf16[192,3072]{1,0:T(8,128)(2,1)}, bf16[192,3072]{1,0:T(8,128)(2,1)S(1)}, u32[]{:S(2)}, u32[]{:S(2)}) collective-permute-start(bf16[192,3072]{1,0:T(8,128)(2,1)} %collective-permute-done.25.refs_1_), channel_id=1, source_target_pairs={{0,1},{1,0},{2,3},{3,2},{4,5},{5,4},{6,7},{7,6},{8,9},{9,8},{10,11... | collective-permute-start | bytes 3538952 | tf_op jit(solution)/shard_map/ppermute | solution.py:632
  197.1 17.0 %collective-permute-start.40 = (bf16[192,3072]{1,0:T(8,128)(2,1)}, bf16[192,3072]{1,0:T(8,128)(2,1)}, u32[]{:S(2)}, u32[]{:S(2)}) collective-permute-start(bf16[192,3072]{1,0:T(8,128)(2,1)} %collective-permute-done.31.refs_4_), channel_id=1, source_target_pairs={{0,1},{1,0},{2,3},{3,2},{4,5},{5,4},{6,7},{7,6},{8,9},{9,8},{10,11... | collective-permute-start | bytes 3538952 | tf_op jit(solution)/shard_map/ppermute | solution.py:632
  197.6 17.8 %collective-permute-start.41 = (bf16[192,3072]{1,0:T(8,128)(2,1)}, bf16[192,3072]{1,0:T(8,128)(2,1)}, u32[]{:S(2)}, u32[]{:S(2)}) collective-permute-start(bf16[192,3072]{1,0:T(8,128)(2,1)} %collective-permute-done.32.refs_5_), channel_id=1, source_target_pairs={{0,1},{1,0},{2,3},{3,2},{4,5},{5,4},{6,7},{7,6},{8,9},{9,8},{10,11... | collective-permute-start | bytes 3538952 | tf_op jit(solution)/shard_map/ppermute | solution.py:632
  210.6 20.0 %collective-permute-start.34 = (bf16[384,384]{1,0:T(8,128)(2,1)}, bf16[384,384]{1,0:T(8,128)(2,1)S(1)}, u32[]{:S(2)}, u32[]{:S(2)}) collective-permute-start(bf16[384,384]{1,0:T(8,128)(2,1)} %get-tuple-element.226), channel_id=1, source_target_pairs={{0,2},{2,0},{16,18},{18,16},{1,3},{3,1},{17,19},{19,17},{4,6},{6,4... | collective-permute-start | bytes 884744 | tf_op jit(solution)/shard_map/ppermute | solution.py:528
  211.7 18.9 %collective-permute-start.35 = (bf16[384,384]{1,0:T(8,128)(2,1)}, bf16[384,384]{1,0:T(8,128)(2,1)S(1)}, u32[]{:S(2)}, u32[]{:S(2)}) collective-permute-start(bf16[384,384]{1,0:T(8,128)(2,1)} %get-tuple-element.227), channel_id=1, source_target_pairs={{0,16},{2,18},{16,0},{18,2},{1,17},{3,19},{17,1},{19,3},{4,20},{6,... | collective-permute-start | bytes 884744 | tf_op jit(solution)/shard_map/ppermute | solution.py:528
  213.2 3.8 %copy-start.9 = (bf16[192,3072]{1,0:T(8,128)(2,1)}, bf16[192,3072]{1,0:T(8,128)(2,1)S(1)}, u32[]{:S(2)}) copy-start(bf16[192,3072]{1,0:T(8,128)(2,1)S(1)} %collective-permute-done.39.refs_3_) | copy-start | bytes 3538948
  213.2 17.4 %collective-permute-start.36 = (bf16[384,384]{1,0:T(8,128)(2,1)}, bf16[384,384]{1,0:T(8,128)(2,1)}, u32[]{:S(2)}, u32[]{:S(2)}) collective-permute-start(bf16[384,384]{1,0:T(8,128)(2,1)} %get-tuple-element.228), channel_id=1, source_target_pairs={{0,18},{2,16},{16,2},{18,0},{1,19},{3,17},{17,3},{19,1},{4,22},{6,... | collective-permute-start | bytes 884744 | tf_op jit(solution)/shard_map/ppermute | solution.py:528
  214.1 13.1 %collective-permute-start.37 = (bf16[384,128]{1,0:T(8,128)(2,1)}, bf16[384,128]{1,0:T(8,128)(2,1)S(1)}, u32[]{:S(2)}, u32[]{:S(2)}) collective-permute-start(bf16[384,128]{1,0:T(8,128)(2,1)} %get-tuple-element.229), channel_id=1, source_target_pairs={{4,0},{6,2},{8,12},{10,14},{20,16},{22,18},{24,28},{26,30},{5,1},{... | collective-permute-start | bytes 294920 | tf_op jit(solution)/shard_map/ppermute | solution.py:663
  215.4 13.1 %collective-permute-start.38 = (bf16[384,128]{1,0:T(8,128)(2,1)}, bf16[384,128]{1,0:T(8,128)(2,1)S(1)}, u32[]{:S(2)}, u32[]{:S(2)}) collective-permute-start(bf16[384,128]{1,0:T(8,128)(2,1)} %get-tuple-element.230), channel_id=1, source_target_pairs={{4,2},{6,0},{8,14},{10,12},{20,18},{22,16},{24,30},{26,28},{5,3},{... | collective-permute-start | bytes 294920 | tf_op jit(solution)/shard_map/ppermute | solution.py:663
  227.2 12.6 %copy-start.12 = (bf16[384,128]{1,0:T(8,128)(2,1)}, bf16[384,128]{1,0:T(8,128)(2,1)S(1)}, u32[]{:S(2)}) copy-start(bf16[384,128]{1,0:T(8,128)(2,1)S(1)} %collective-permute-done.37.refs_4_) | copy-start | bytes 294916
  227.2 10.8 %collective-permute-start.42 = (bf16[384,128]{1,0:T(8,128)(2,1)}, bf16[384,128]{1,0:T(8,128)(2,1)S(1)}, u32[]{:S(2)}, u32[]{:S(2)}) collective-permute-start(bf16[384,128]{1,0:T(8,128)(2,1)} %get-tuple-element.235), channel_id=1, source_target_pairs={{4,16},{6,18},{8,28},{10,30},{20,0},{22,2},{24,12},{26,14},{5,17},... | collective-permute-start | bytes 294920 | tf_op jit(solution)/shard_map/ppermute | solution.py:663
  228.5 11.3 %copy-start.13 = (bf16[384,128]{1,0:T(8,128)(2,1)}, bf16[384,128]{1,0:T(8,128)(2,1)S(1)}, u32[]{:S(2)}) copy-start(bf16[384,128]{1,0:T(8,128)(2,1)S(1)} %collective-permute-done.38.refs_5_) | copy-start | bytes 294916
  228.5 11.3 %collective-permute-start.43 = (bf16[384,128]{1,0:T(8,128)(2,1)}, bf16[384,128]{1,0:T(8,128)(2,1)S(1)}, u32[]{:S(2)}, u32[]{:S(2)}) collective-permute-start(bf16[384,128]{1,0:T(8,128)(2,1)} %get-tuple-element.236), channel_id=1, source_target_pairs={{4,18},{6,16},{8,30},{10,28},{20,2},{22,0},{24,14},{26,12},{5,19},... | collective-permute-start | bytes 294920 | tf_op jit(solution)/shard_map/ppermute | solution.py:663
  230.6 9.3 %copy-start.10 = (bf16[384,384]{1,0:T(8,128)(2,1)}, bf16[384,384]{1,0:T(8,128)(2,1)S(1)}, u32[]{:S(2)}) copy-start(bf16[384,384]{1,0:T(8,128)(2,1)S(1)} %collective-permute-done.34.refs_1_) | copy-start | bytes 884740
  230.6 9.3 %copy-start.11 = (bf16[384,384]{1,0:T(8,128)(2,1)}, bf16[384,384]{1,0:T(8,128)(2,1)S(1)}, u32[]{:S(2)}) copy-start(bf16[384,384]{1,0:T(8,128)(2,1)S(1)} %collective-permute-done.35.refs_2_) | copy-start | bytes 884740
  238.0 1.8 copy-start.14
  239.8 0.6 copy-start.15
where the time goes:
time: 245 us; the launch traced here: 244 us
  Pallas kernels  92.4 us (38%)
  waiting for transfers between devices  80.4 us (33%)
  starting transfers between devices  50.9 us (21%)
  local copies, waits for them, and re-layouts  9.87 us (4%)
  other arithmetic  9.6 us (4%)
    pallas_call x6, Pallas kernels, run_jobs(): pl.pallas_call(functools.partial(job_kernel, plan), out_shape=shapes, in_...  79.4 us
    ppermute x5, waiting for transfers between devices, pair(): return lax.ppermute(value, 'dp', [(0, 1), (1, 0), (2, 3), (3, 2)])  45.5 us
    ppermute x6, waiting for transfers between devices, shared(): beside = lambda value: lax.ppermute(value, 'seq', swap)  17.3 us
    ppermute x5, starting transfers between devices, pair(): return lax.ppermute(value, 'dp', [(0, 1), (1, 0), (2, 3), (3, 2)])  16.1 us
    pallas_call x2, Pallas kernels, normalize_part(): pl.pallas_call(functools.partial(normalize_kernel, step, other, taken), o...  9.92 us
    ppermute x4, waiting for transfers between devices, hand_back(): got.append(lax.ppermute(sent, ('groups', 'dp', 'seq'), steps))  9.25 us
    ppermute x6, starting transfers between devices, middle(): return lax.ppermute(value, 'dp', [(1, 2), (2, 1)])  9.15 us
    ppermute x6, starting transfers between devices, shared(): beside = lambda value: lax.ppermute(value, 'seq', swap)  8.12 us
  transfers between devices with their start and end apart: 44, of which 11 were waited for; matrix products, arithmetic and copies ran while one was open for 7% of the time, Pallas kernels for 35%

commit v1 on v0

--- a/solution.py
+++ b/solution.py
@@ -178,7 +178,7 @@
             queries, key_rows, (((1,), (1,)), ((), ())), preferred_element_type=jnp.float32
         )
         highest = jnp.max(scores, axis=-1, keepdims=True)
-        expo = jnp.exp2((scores - highest) * (math.log2(math.e) / math.sqrt(width)))
+        expo = jnp.exp((scores - highest) * (1.0 / math.sqrt(width)))
         mixed = jnp.dot(expo.astype(jnp.bfloat16), value_rows, preferred_element_type=jnp.float32)
         mixed = mixed[:, :width] / mixed[:, width:]
         part[:, column : column + width] = mixed.astype(jnp.bfloat16)
@@ -291,7 +291,7 @@
             for j in plan.added[i]:
                 partial_copy(i, j).start()
 
-    ahead = 2
+    ahead = 3
     for stage in stages[:ahead]:
         start_stage(*stage)
     for copy in carry_copies():

time: 245 us -> 246 us (level)
  Pallas kernels: 92.4 us -> 97.1 us
  waiting for transfers between devices: 80.4 us -> 77.1 us
    pallas_call x6, Pallas kernels: 79.4 us -> 84.1 us  [run_jobs(): pl.pallas_call(functools.partial(job_kernel, plan), out_shape=shapes, in_...]
  transfers between devices with their start and end apart: 44 -> 44, of which waited for: 11 -> 11; matrix products, arithmetic and copies ran while one was open for 7% -> 7% of each run, Pallas kernels for 35% -> 36%
where the time goes in v1:
time: 246 us; the launch traced here: 245 us
  Pallas kernels  97.1 us (39%)
  waiting for transfers between devices  77.1 us (31%)
  starting transfers between devices  50.9 us (21%)
  local copies, waits for them, and re-layouts  9.87 us (4%)
  other arithmetic  9.6 us (4%)
    pallas_call x6, Pallas kernels, run_jobs(): pl.pallas_call(functools.partial(job_kernel, plan), out_shape=shapes, in_...  84.1 us
    ppermute x5, waiting for transfers between devices, pair(): return lax.ppermute(value, 'dp', [(0, 1), (1, 0), (2, 3), (3, 2)])  44.1 us
    ppermute x6, waiting for transfers between devices, shared(): beside = lambda value: lax.ppermute(value, 'seq', swap)  17.3 us
    ppermute x5, starting transfers between devices, pair(): return lax.ppermute(value, 'dp', [(0, 1), (1, 0), (2, 3), (3, 2)])  16.1 us
    pallas_call x2, Pallas kernels, normalize_part(): pl.pallas_call(functools.partial(normalize_kernel, step, other, taken), o...  9.92 us
    ppermute x6, starting transfers between devices, middle(): return lax.ppermute(value, 'dp', [(1, 2), (2, 1)])  9.15 us
    ppermute x4, waiting for transfers between devices, hand_back(): got.append(lax.ppermute(sent, ('groups', 'dp', 'seq'), steps))  8.93 us
    ppermute x6, starting transfers between devices, shared(): beside = lambda value: lax.ppermute(value, 'seq', swap)  8.12 us
  transfers between devices with their start and end apart: 44, of which 11 were waited for; matrix products, arithmetic and copies ran while one was open for 7% of the time, Pallas kernels for 36%

profile of v1, /device:TPU:0, one launch (start us, length us, event | category | flops | bytes accessed | tf_op | source)
XLA Modules:
  0.0 245.1 jit_solution(9649129157108043533)
XLA Ops:
  0.0 5.2 %shard_map.37 = (bf16[192,3072]{1,0:T(8,128)(2,1)}, bf16[192,3072]{1,0:T(8,128)(2,1)}, bf16[1536,384]{1,0:T(8,128)(2,1)}) custom-call(bf16[1,384,6144]{2,1,0:T(8,128)(2,1)} %tokens_ref.2, f32[1,6144]{1,0:T(1,128)} %bitcast.35, bf16[6,1536,384]{2,1,0:T(8,128)(2,1)} %bitcast.23), custom_call_target="tpu_custom_call" | custom-call | flops 9437184 | bytes 4718592 | tf_op jit(solution)/shard_map/pallas_call | solution.py:147
  5.2 3.0 %collective-permute-start = (bf16[192,3072]{1,0:T(8,128)(2,1)}, bf16[192,3072]{1,0:T(8,128)(2,1)}, u32[]{:S(2)}, u32[]{:S(2)}) collective-permute-start(bf16[192,3072]{1,0:T(8,128)(2,1)} %get-tuple-element.124.refs_0_.refs_8_), channel_id=1, source_target_pairs={{0,2},{2,0},{1,3},{3,1},{4,6},{6,4},{5,7},{7,5},{8,10},{10,8},{9,1... | collective-permute-start | bytes 3538952 | tf_op jit(solution)/shard_map/ppermute | solution.py:505
  8.2 1.5 collective-permute-start.1
  9.7 1.6 collective-permute-start.2
  11.3 1.7 collective-permute-start.3
  13.0 2.9 %dynamic-slice_bitcast_fusion = (bf16[1536,384]{1,0:T(8,128)(2,1)}, bf16[1,1536,384]{2,1,0:T(8,128)(2,1)S(1)}) fusion(bf16[6,1536,384]{2,1,0:T(8,128)(2,1)} %bitcast.24, s32[]{:T(128)S(6)} %select_n.63, s32[]{:T(128)S(6)} %select_n.62), kind=kLoop, calls=%fused_computation.1 | loop fusion | bytes 4718600 | tf_op jit(solution)/shard_map/jit(dynamic_index_in_dim)/squeeze | solution.py:539
  15.9 1.2 copy.7
  17.1 0.9 copy-done.1
  18.0 1.1 broadcast_select_fusion.3
  19.1 0.6 pad_add_fusion.role_ref
  19.7 14.8 %collective-permute-done.refs_4_.refs_12_ = bf16[192,3072]{1,0:T(8,128)(2,1)} collective-permute-done((bf16[192,3072]{1,0:T(8,128)(2,1)}, bf16[192,3072]{1,0:T(8,128)(2,1)}, u32[]{:S(2)}, u32[]{:S(2)}) %collective-permute-start) | collective-permute-done | bytes 1179680 | tf_op jit(solution)/shard_map/ppermute | solution.py:505
  34.5 1.5 collective-permute-done.1.refs_0_.refs_8_
  36.3 1.7 collective-permute-start.7
  38.0 3.8 %collective-permute-start.4 = (bf16[192,3072]{1,0:T(8,128)(2,1)}, bf16[192,3072]{1,0:T(8,128)(2,1)}, u32[]{:S(2)}, u32[]{:S(2)}) collective-permute-start(bf16[192,3072]{1,0:T(8,128)(2,1)} %broadcast_select_fusion.3), channel_id=1, source_target_pairs={{0,4},{4,0},{8,12},{12,8},{1,5},{5,1},{9,13},{13,9},{2,6},{6,2},{1... | collective-permute-start | bytes 3538952 | tf_op jit(solution)/shard_map/ppermute | solution.py:496
  41.8 1.7 collective-permute-start.5
  43.4 2.5 %copy.8 = bf16[24,8,8,384]{3,1,2,0:T(8,128)(2,1)} copy(bf16[24,8,8,384]{3,1,0,2:T(8,128)(2,1)} %bitcast.21) | data formatting | bytes 2359296
  45.9 4.8 %shard_map.38 = (bf16[192,3072]{1,0:T(8,128)(2,1)}, bf16[192,3072]{1,0:T(8,128)(2,1)}) custom-call(bf16[1,384,6144]{2,1,0:T(8,128)(2,1)} %tokens_ref.2, f32[1,6144]{1,0:T(1,128)} %bitcast.36, bf16[6,1536,384]{2,1,0:T(8,128)(2,1)} %bitcast.25), custom_call_target="tpu_custom_call" | custom-call | flops 9437184 | bytes 4718592 | tf_op jit(solution)/shard_map/pallas_call | solution.py:147
  50.7 1.4 broadcast_select_fusion.2
  52.1 14.5 %collective-permute-done.4.refs_25_.refs_0_.refs_16_ = bf16[192,3072]{1,0:T(8,128)(2,1)} collective-permute-done((bf16[192,3072]{1,0:T(8,128)(2,1)}, bf16[192,3072]{1,0:T(8,128)(2,1)}, u32[]{:S(2)}, u32[]{:S(2)}) %collective-permute-start.4) | collective-permute-done | bytes 1179680 | tf_op jit(solution)/shard_map/ppermute | solution.py:496
  66.7 4.2 %collective-permute-start.10 = (bf16[192,3072]{1,0:T(8,128)(2,1)S(1)}, bf16[192,3072]{1,0:T(8,128)(2,1)S(1)}, u32[]{:S(2)}, u32[]{:S(2)}) collective-permute-start(bf16[192,3072]{1,0:T(8,128)(2,1)S(1)} %broadcast_select_fusion.2), channel_id=1, source_target_pairs={{0,4},{4,0},{8,12},{12,8},{1,5},{5,1},{9,13},{13,9},{2,6},{6,2},{1... | collective-permute-start | bytes 3538952 | tf_op jit(solution)/shard_map/ppermute | solution.py:496
  70.9 0.7 collective-permute-start.11
  71.6 1.6 collective-permute-start.12
  73.2 0.5 collective-permute-start.13
  73.7 1.2 broadcast_select_fusion.1
  74.9 22.5 %collective-permute-done.10.refs_28_.refs_1_.refs_17_ = bf16[192,3072]{1,0:T(8,128)(2,1)S(1)} collective-permute-done((bf16[192,3072]{1,0:T(8,128)(2,1)S(1)}, bf16[192,3072]{1,0:T(8,128)(2,1)S(1)}, u32[]{:S(2)}, u32[]{:S(2)}) %collective-permute-start.10) | collective-permute-done | bytes 1179680 | tf_op jit(solution)/shard_map/ppermute | solution.py:496
  97.5 2.5 %collective-permute-done.12.refs_4_.refs_12_ = bf16[192,3072]{1,0:T(8,128)(2,1)S(1)} collective-permute-done((bf16[192,3072]{1,0:T(8,128)(2,1)}, bf16[192,3072]{1,0:T(8,128)(2,1)S(1)}, u32[]{:S(2)}, u32[]{:S(2)}) %collective-permute-start.12) | collective-permute-done | bytes 1179680 | tf_op jit(solution)/shard_map/ppermute | solution.py:505
  99.9 1.3 collective-permute-done.13.refs_5_.refs_13_
  101.3 1.1 collective-permute-start.18
  102.4 0.5 collective-permute-start.19
  102.9 2.9 %collective-permute-start.16 = (bf16[1536,384]{1,0:T(8,128)(2,1)}, bf16[1536,384]{1,0:T(8,128)(2,1)}, u32[]{:S(2)}, u32[]{:S(2)}) collective-permute-start(bf16[1536,384]{1,0:T(8,128)(2,1)} %broadcast_select_fusion.1), channel_id=1, source_target_pairs={{0,4},{4,0},{8,12},{12,8},{1,5},{5,1},{9,13},{13,9},{2,6},{6,2},{1... | collective-permute-start | bytes 3538952 | tf_op jit(solution)/shard_map/ppermute | solution.py:496
  105.9 1.7 collective-permute-start.17
  107.5 1.0 copy-done.6
  108.6 2.8 %pad_maximum_fusion = bf16[384,3072]{1,0:T(8,128)(2,1)} fusion(bf16[192,3072]{1,0:T(8,128)(2,1)S(1)} %collective-permute-done.10.refs_28_.refs_1_.refs_17_, bf16[192,3072]{1,0:T(8,128)(2,1)} %collective-permute-done.4.refs_25_.refs_0_.refs_16_), kind=kLoop, calls=%fused_computation | loop fusion | flops 4718592 | bytes 4718592 | tf_op jit(solution)/shard_map/concatenate | solution.py:579
  111.4 2.5 %broadcast_select_fusion = bf16[1536,384]{1,0:T(8,128)(2,1)} fusion(bf16[1536,384]{1,0:T(8,128)(2,1)S(1)} %collective-permute-done.11.refs_14_.refs_22_, bf16[1536,384]{1,0:T(8,128)(2,1)} %get-tuple-element.210.refs_11_.refs_19_.refs_10_, pred[]{:T(512)S(6)} %or.3), kind=kLoop, calls=%fused_computation.2 | loop fusion | flops 589824 | bytes 3538945 | tf_op jit(solution)/shard_map/jit(_where)/select_n | solution.py:493
  113.8 15.3 %shard_map.39 = (bf16[384,128]{1,0:T(8,128)(2,1)}, bf16[384,128]{1,0:T(8,128)(2,1)}, f32[768,384]{1,0:T(8,128)}, f32[768,384]{1,0:T(8,128)}) custom-call(s32[2]{0:T(128)} %pad_add_fusion.role_ref, bf16[192,3072]{1,0:T(8,128)(2,1)} %get-tuple-element.124.refs_0_.refs_8_, bf16[192,3072]{1,0:T(8,128)(2,1)} %get-tuple-element.132.refs_1_.refs_9_, ...), custom_call_target="tpu_custom_call" | custom-call | flops 6341787648 | tf_op jit(solution)/shard_map/pallas_call | solution.py:406
  129.2 3.1 %collective-permute-done.16.refs_27_.refs_17_ = bf16[1536,384]{1,0:T(8,128)(2,1)} collective-permute-done((bf16[1536,384]{1,0:T(8,128)(2,1)}, bf16[1536,384]{1,0:T(8,128)(2,1)}, u32[]{:S(2)}, u32[]{:S(2)}) %collective-permute-start.16) | collective-permute-done | bytes 1179680 | tf_op jit(solution)/shard_map/ppermute | solution.py:496
  132.4 1.0 collective-permute-start.24
  133.4 1.5 collective-permute-start.25
  134.9 3.6 %collective-permute-start.22 = (bf16[1536,384]{1,0:T(8,128)(2,1)}, bf16[1536,384]{1,0:T(8,128)(2,1)}, u32[]{:S(2)}, u32[]{:S(2)}) collective-permute-start(bf16[1536,384]{1,0:T(8,128)(2,1)} %broadcast_select_fusion), channel_id=1, source_target_pairs={{0,4},{4,0},{8,12},{12,8},{1,5},{5,1},{9,13},{13,9},{2,6},{6,2},{1... | collective-permute-start | bytes 3538952 | tf_op jit(solution)/shard_map/ppermute | solution.py:496
  138.5 1.7 collective-permute-start.23
  140.2 20.6 %shard_map.40 = (bf16[384,128]{1,0:T(8,128)(2,1)}, bf16[384,128]{1,0:T(8,128)(2,1)}, f32[768,384]{1,0:T(8,128)}, f32[768,384]{1,0:T(8,128)}, f32[768,384]{1,0:T(8,128)}, /*index=5*/f32[768,384]{1,0:T(8,128)}) custom-call(s32[2]{0:T(128)} %pad_add_fusion.role_ref, bf16[192,3072]{1,0:T(8,128)(2,1)} %collective-permute-done.1.refs_0_.refs_8_, ...), custom_call_target="tpu_custom_call" | custom-call | flops 9965666304 | tf_op jit(solution)/shard_map/pallas_call | solution.py:406
  160.8 4.0 %collective-permute-done.22.refs_18_.refs_8_ = bf16[1536,384]{1,0:T(8,128)(2,1)} collective-permute-done((bf16[1536,384]{1,0:T(8,128)(2,1)}, bf16[1536,384]{1,0:T(8,128)(2,1)}, u32[]{:S(2)}, u32[]{:S(2)}) %collective-permute-start.22) | collective-permute-done | bytes 1179680 | tf_op jit(solution)/shard_map/ppermute | solution.py:496
  164.9 0.6 collective-permute-start.32
  165.5 1.3 collective-permute-start.29
  166.8 1.7 collective-permute-start.30
  168.5 1.1 collective-permute-start.31
  169.6 14.1 %shard_map.41 = (bf16[384,128]{1,0:T(8,128)(2,1)}, bf16[384,128]{1,0:T(8,128)(2,1)}, f32[768,384]{1,0:T(8,128)}, bf16[384,128]{1,0:T(8,128)(2,1)}, bf16[384,128]{1,0:T(8,128)(2,1)}, /*index=5*/f32[768,384]{1,0:T(8,128)}) custom-call(s32[2]{0:T(128)} %pad_add_fusion.role_ref, bf16[192,3072]{1,0:T(8,128)(2,1)} %get-tuple-element.124.refs_0_.refs_8_, ...), custom_call_target="tpu_custom_call" | custom-call | flops 3623878656 | tf_op jit(solution)/shard_map/pallas_call | solution.py:406
  183.7 9.3 %shard_map.42.refs_28_ = f32[768,384]{1,0:T(8,128)} custom-call(s32[2]{0:T(128)} %pad_add_fusion.role_ref, bf16[192,3072]{1,0:T(8,128)(2,1)} %collective-permute-done.4.refs_25_.refs_0_.refs_16_, bf16[192,3072]{1,0:T(8,128)(2,1)} %copy-done.2, bf16[384,3072]{1,0:T(8,128)(2,1)} %collective-permute-done.26.refs_2_.refs_3_.refs_18_.refs_19_, ...), custom_call_target="tpu_custom_call" | custom-call | flops 2717908992 | tf_op jit(solution)/shard_map/pallas_call | solution.py:406
  193.1 3.9 %collective-permute-done.29.refs_25_ = bf16[1536,384]{1,0:T(8,128)(2,1)} collective-permute-done((bf16[1536,384]{1,0:T(8,128)(2,1)}, bf16[1536,384]{1,0:T(8,128)(2,1)}, u32[]{:S(2)}, u32[]{:S(2)}) %collective-permute-start.29) | collective-permute-done | bytes 1179680 | tf_op jit(solution)/shard_map/ppermute | solution.py:499
  197.1 0.5 collective-permute-start.40
  197.7 14.0 %shard_map.43 = (bf16[384,384]{1,0:T(8,128)(2,1)}, bf16[384,384]{1,0:T(8,128)(2,1)}, bf16[384,384]{1,0:T(8,128)(2,1)}, bf16[384,384]{1,0:T(8,128)(2,1)}, bf16[38...) custom-call(s32[2]{0:T(128)} %pad_add_fusion.role_ref, bf16[192,3072]{1,0:T(8,128)(2,1)} %get-tuple-element.124.refs_0_.refs_8_, ...), custom_call_target="tpu_custom_call" | custom-call | flops 2717908992 | tf_op jit(solution)/shard_map/pallas_call | solution.py:406
  211.7 1.1 collective-permute-start.34
  212.8 1.5 collective-permute-start.35
  214.3 0.9 collective-permute-start.36
  215.2 1.3 collective-permute-start.37
  216.5 1.6 collective-permute-start.38
  218.1 10.8 %shard_map.44 = (bf16[384,128]{1,0:T(8,128)(2,1)}, bf16[384,128]{1,0:T(8,128)(2,1)}) custom-call(s32[2]{0:T(128)} %pad_add_fusion.role_ref, bf16[192,3072]{1,0:T(8,128)(2,1)} %collective-permute-done.19.refs_0_, bf16[192,3072]{1,0:T(8,128)(2,1)} %collective-permute-done.25.refs_1_, bf16[192,3072]{1,0:T(8,128)(2,1)} %collective-permute-done.33.refs_2_, ...), custom_call_target="tpu_custom_call" | custom-call | flops 3623878656 | tf_op jit(solution)/shard_map/pallas_call | solution.py:406
  228.9 1.3 collective-permute-start.42
  230.2 1.3 collective-permute-start.43
  231.6 0.7 stack.34.place_ref
  232.3 7.1 %collective-permute-done.42.refs_6_ = bf16[384,128]{1,0:T(8,128)(2,1)S(1)} collective-permute-done((bf16[384,128]{1,0:T(8,128)(2,1)}, bf16[384,128]{1,0:T(8,128)(2,1)S(1)}, u32[]{:S(2)}, u32[]{:S(2)}) %collective-permute-start.42) | collective-permute-done | bytes 98336 | tf_op jit(solution)/shard_map/ppermute | solution.py:663
  239.4 1.8 collective-permute-done.43.refs_7_
  241.2 0.6 copy-done.15
  241.8 3.1 %shard_map.45 = bf16[384,1536]{1,0:T(8,128)(2,1)} custom-call(s32[5]{0:T(128)} %stack.34.place_ref, bf16[384,384]{1,0:T(8,128)(2,1)} %get-tuple-element.225.refs_0_, bf16[384,384]{1,0:T(8,128)(2,1)} %copy-done.10, bf16[384,384]{1,0:T(8,128)(2,1)} %copy-done.11, bf16[384,384]{1,0:T(8,128)(2,1)} %collective-permute-done.36.refs_3_, ...), custom_call_target="tpu_custom_call" | custom-call | bytes 2359296 | tf_op jit(solution)/shard_map/pallas_call | solution.py:467
  (75 shorter events, 1.0 us)
Async XLA Ops:
  5.2 29.3 %collective-permute-start = (bf16[192,3072]{1,0:T(8,128)(2,1)}, bf16[192,3072]{1,0:T(8,128)(2,1)}, u32[]{:S(2)}, u32[]{:S(2)}) collective-permute-start(bf16[192,3072]{1,0:T(8,128)(2,1)} %get-tuple-element.124.refs_0_.refs_8_), channel_id=1, source_target_pairs={{0,2},{2,0},{1,3},{3,1},{4,6},{6,4},{5,7},{7,5},{8,10},{10,8},{9,1... | collective-permute-start | bytes 3538952 | tf_op jit(solution)/shard_map/ppermute | solution.py:505
  8.2 27.7 %collective-permute-start.1 = (bf16[192,3072]{1,0:T(8,128)(2,1)}, bf16[192,3072]{1,0:T(8,128)(2,1)}, u32[]{:S(2)}, u32[]{:S(2)}) collective-permute-start(bf16[192,3072]{1,0:T(8,128)(2,1)} %get-tuple-element.124.refs_0_.refs_8_), channel_id=1, source_target_pairs={{0,16},{16,0},{1,17},{17,1},{2,18},{18,2},{3,19},{19,3},{4,20},{20... | collective-permute-start | bytes 3538952 | tf_op jit(solution)/shard_map/ppermute | solution.py:506
  9.7 28.3 %collective-permute-start.2 = (bf16[1536,384]{1,0:T(8,128)(2,1)}, bf16[1536,384]{1,0:T(8,128)(2,1)}, u32[]{:S(2)}, u32[]{:S(2)}) collective-permute-start(bf16[1536,384]{1,0:T(8,128)(2,1)} %get-tuple-element.128.refs_8_.refs_10_.refs_16_.refs_18_), channel_id=1, source_target_pairs={{0,4},{4,0},{8,12},{12,8},{1,5},{5,1},{9,13},{13,9},{2,6},{6,2},{1... | collective-permute-start | bytes 3538952 | tf_op jit(solution)/shard_map/ppermute | solution.py:496
  11.3 26.7 %collective-permute-start.3 = (bf16[1536,384]{1,0:T(8,128)(2,1)}, bf16[1536,384]{1,0:T(8,128)(2,1)}, u32[]{:S(2)}, u32[]{:S(2)}) collective-permute-start(bf16[1536,384]{1,0:T(8,128)(2,1)} %get-tuple-element.128.refs_8_.refs_10_.refs_16_.refs_18_), channel_id=1, source_target_pairs={{4,8},{8,4},{5,9},{9,5},{6,10},{10,6},{7,11},{11,7},{20,24},{24,20... | collective-permute-start | bytes 3538952 | tf_op jit(solution)/shard_map/ppermute | solution.py:502
  15.9 57.8 %copy-start = (bf16[1,1536,384]{2,1,0:T(8,128)(2,1)}, bf16[1,1536,384]{2,1,0:T(8,128)(2,1)S(1)}, u32[]{:S(2)}) copy-start(bf16[1,1536,384]{2,1,0:T(8,128)(2,1)S(1)} %get-tuple-element.238) | copy-start | bytes 3538948
  15.9 2.1 copy-start.1
  35.9 7.5 %collective-permute-start.8 = (bf16[192,3072]{1,0:T(8,128)(2,1)}, bf16[192,3072]{1,0:T(8,128)(2,1)}, u32[]{:S(2)}, u32[]{:S(2)}) collective-permute-start(bf16[192,3072]{1,0:T(8,128)(2,1)} %collective-permute-done.refs_4_.refs_12_), channel_id=1, source_target_pairs={{0,1},{1,0},{2,3},{3,2},{4,5},{5,4},{6,7},{7,6},{8,9},{9,8},{10,11... | collective-permute-start | bytes 3538952 | tf_op jit(solution)/shard_map/ppermute | solution.py:513
  35.9 30.6 %collective-permute-start.6 = (bf16[192,3072]{1,0:T(8,128)(2,1)}, bf16[192,3072]{1,0:T(8,128)(2,1)}, u32[]{:S(2)}, u32[]{:S(2)}) collective-permute-start(bf16[192,3072]{1,0:T(8,128)(2,1)} %get-tuple-element.132.refs_1_.refs_9_), channel_id=1, source_target_pairs={{0,2},{2,0},{1,3},{3,1},{4,6},{6,4},{5,7},{7,5},{8,10},{10,8},{9,1... | collective-permute-start | bytes 3538952 | tf_op jit(solution)/shard_map/ppermute | solution.py:505
  36.3 30.3 %collective-permute-start.7 = (bf16[192,3072]{1,0:T(8,128)(2,1)}, bf16[192,3072]{1,0:T(8,128)(2,1)}, u32[]{:S(2)}, u32[]{:S(2)}) collective-permute-start(bf16[192,3072]{1,0:T(8,128)(2,1)} %get-tuple-element.132.refs_1_.refs_9_), channel_id=1, source_target_pairs={{0,16},{16,0},{1,17},{17,1},{2,18},{18,2},{3,19},{19,3},{4,20},{20... | collective-permute-start | bytes 3538952 | tf_op jit(solution)/shard_map/ppermute | solution.py:506
  38.0 28.6 %collective-permute-start.4 = (bf16[192,3072]{1,0:T(8,128)(2,1)}, bf16[192,3072]{1,0:T(8,128)(2,1)}, u32[]{:S(2)}, u32[]{:S(2)}) collective-permute-start(bf16[192,3072]{1,0:T(8,128)(2,1)} %broadcast_select_fusion.3), channel_id=1, source_target_pairs={{0,4},{4,0},{8,12},{12,8},{1,5},{5,1},{9,13},{13,9},{2,6},{6,2},{1... | collective-permute-start | bytes 3538952 | tf_op jit(solution)/shard_map/ppermute | solution.py:496
  41.8 24.8 %collective-permute-start.5 = (bf16[1536,384]{1,0:T(8,128)(2,1)}, bf16[1536,384]{1,0:T(8,128)(2,1)}, u32[]{:S(2)}, u32[]{:S(2)}) collective-permute-start(bf16[1536,384]{1,0:T(8,128)(2,1)} %collective-permute-done.2.refs_15_.refs_16_.refs_23_.refs_26_), channel_id=1, source_target_pairs={{4,8},{8,4},{5,9},{9,5},{6,10},{10,6},{7,11},{11,7},{20,24},{24,20... | collective-permute-start | bytes 3538952 | tf_op jit(solution)/shard_map/ppermute | solution.py:502
  43.4 23.1 %collective-permute-start.9 = (bf16[192,3072]{1,0:T(8,128)(2,1)}, bf16[192,3072]{1,0:T(8,128)(2,1)}, u32[]{:S(2)}, u32[]{:S(2)}) collective-permute-start(bf16[192,3072]{1,0:T(8,128)(2,1)} %collective-permute-done.1.refs_0_.refs_8_), channel_id=1, source_target_pairs={{0,1},{1,0},{2,3},{3,2},{4,5},{5,4},{6,7},{7,6},{8,9},{9,8},{10,11... | collective-permute-start | bytes 3538952 | tf_op jit(solution)/shard_map/ppermute | solution.py:513
  66.6 7.1 %collective-permute-start.14 = (bf16[192,3072]{1,0:T(8,128)(2,1)}, bf16[192,3072]{1,0:T(8,128)(2,1)}, u32[]{:S(2)}, u32[]{:S(2)}) collective-permute-start(bf16[192,3072]{1,0:T(8,128)(2,1)} %collective-permute-done.7.refs_1_.refs_9_), channel_id=1, source_target_pairs={{0,1},{1,0},{2,3},{3,2},{4,5},{5,4},{6,7},{7,6},{8,9},{9,8},{10,11... | collective-permute-start | bytes 3538952 | tf_op jit(solution)/shard_map/ppermute | solution.py:513
  66.7 30.8 %collective-permute-start.10 = (bf16[192,3072]{1,0:T(8,128)(2,1)S(1)}, bf16[192,3072]{1,0:T(8,128)(2,1)S(1)}, u32[]{:S(2)}, u32[]{:S(2)}) collective-permute-start(bf16[192,3072]{1,0:T(8,128)(2,1)S(1)} %broadcast_select_fusion.2), channel_id=1, source_target_pairs={{0,4},{4,0},{8,12},{12,8},{1,5},{5,1},{9,13},{13,9},{2,6},{6,2},{1... | collective-permute-start | bytes 3538952 | tf_op jit(solution)/shard_map/ppermute | solution.py:496
  70.9 26.6 %collective-permute-start.11 = (bf16[1536,384]{1,0:T(8,128)(2,1)S(1)}, bf16[1536,384]{1,0:T(8,128)(2,1)S(1)}, u32[]{:S(2)}, u32[]{:S(2)}) collective-permute-start(bf16[1536,384]{1,0:T(8,128)(2,1)S(1)} %bitcast.27), channel_id=1, source_target_pairs={{4,8},{8,4},{5,9},{9,5},{6,10},{10,6},{7,11},{11,7},{20,24},{24,20... | collective-permute-start | bytes 3538952 | tf_op jit(solution)/shard_map/ppermute | solution.py:502
  71.6 28.3 %collective-permute-start.12 = (bf16[192,3072]{1,0:T(8,128)(2,1)}, bf16[192,3072]{1,0:T(8,128)(2,1)S(1)}, u32[]{:S(2)}, u32[]{:S(2)}) collective-permute-start(bf16[192,3072]{1,0:T(8,128)(2,1)} %collective-permute-done.1.refs_0_.refs_8_), channel_id=1, source_target_pairs={{0,2},{2,0},{1,3},{3,1},{4,6},{6,4},{5,7},{7,5},{8,10},{10,8},{9,1... | collective-permute-start | bytes 3538952 | tf_op jit(solution)/shard_map/ppermute | solution.py:505
  73.2 28.1 %collective-permute-start.13 = (bf16[192,3072]{1,0:T(8,128)(2,1)}, bf16[192,3072]{1,0:T(8,128)(2,1)}, u32[]{:S(2)}, u32[]{:S(2)}) collective-permute-start(bf16[192,3072]{1,0:T(8,128)(2,1)} %collective-permute-done.6.refs_5_.refs_13_), channel_id=1, source_target_pairs={{0,16},{16,0},{1,17},{17,1},{2,18},{18,2},{3,19},{19,3},{4,20},{20... | collective-permute-start | bytes 3538952 | tf_op jit(solution)/shard_map/ppermute | solution.py:506
  73.7 27.6 %collective-permute-start.15 = (bf16[192,3072]{1,0:T(8,128)(2,1)}, bf16[192,3072]{1,0:T(8,128)(2,1)S(1)}, u32[]{:S(2)}, u32[]{:S(2)}) collective-permute-start(bf16[192,3072]{1,0:T(8,128)(2,1)} %collective-permute-done.6.refs_5_.refs_13_), channel_id=1, source_target_pairs={{0,1},{1,0},{2,3},{3,2},{4,5},{5,4},{6,7},{7,6},{8,9},{9,8},{10,11... | collective-permute-start | bytes 3538952 | tf_op jit(solution)/shard_map/ppermute | solution.py:513
  97.5 13.9 %copy-start.2 = (bf16[192,3072]{1,0:T(8,128)(2,1)}, bf16[192,3072]{1,0:T(8,128)(2,1)S(1)}, u32[]{:S(2)}) copy-start(bf16[192,3072]{1,0:T(8,128)(2,1)S(1)} %collective-permute-done.10.refs_28_.refs_1_.refs_17_) | copy-start | bytes 3538948
  97.5 13.9 %copy-start.8 = (bf16[1536,384]{1,0:T(8,128)(2,1)}, bf16[1536,384]{1,0:T(8,128)(2,1)S(1)}, u32[]{:S(2)}) copy-start(bf16[1536,384]{1,0:T(8,128)(2,1)S(1)} %collective-permute-done.11.refs_14_.refs_22_) | copy-start | bytes 3538948
  99.9 1.3 copy-start.4
  101.3 6.3 %copy-start.5 = (bf16[192,3072]{1,0:T(8,128)(2,1)}, bf16[192,3072]{1,0:T(8,128)(2,1)S(1)}, u32[]{:S(2)}) copy-start(bf16[192,3072]{1,0:T(8,128)(2,1)S(1)} %collective-permute-done.15.refs_7_.refs_15_) | copy-start | bytes 3538948
  101.3 6.3 %collective-permute-start.20 = (bf16[192,3072]{1,0:T(8,128)(2,1)S(1)}, bf16[192,3072]{1,0:T(8,128)(2,1)S(1)}, u32[]{:S(2)}, u32[]{:S(2)}) collective-permute-start(bf16[192,3072]{1,0:T(8,128)(2,1)S(1)} %collective-permute-done.12.refs_4_.refs_12_), channel_id=1, source_target_pairs={{0,1},{1,0},{2,3},{3,2},{4,5},{5,4},{6,7},{7,6},{8,9},{9,8},{10,11... | collective-permute-start | bytes 3538952 | tf_op jit(solution)/shard_map/ppermute | solution.py:513
  101.3 30.9 %collective-permute-start.18 = (bf16[192,3072]{1,0:T(8,128)(2,1)}, bf16[192,3072]{1,0:T(8,128)(2,1)}, u32[]{:S(2)}, u32[]{:S(2)}) collective-permute-start(bf16[192,3072]{1,0:T(8,128)(2,1)} %collective-permute-done.4.refs_25_.refs_0_.refs_16_), channel_id=1, source_target_pairs={{0,2},{2,0},{1,3},{3,1},{4,6},{6,4},{5,7},{7,5},{8,10},{10,8},{9,1... | collective-permute-start | bytes 3538952 | tf_op jit(solution)/shard_map/ppermute | solution.py:505
  102.4 29.8 %collective-permute-start.19 = (bf16[192,3072]{1,0:T(8,128)(2,1)}, bf16[192,3072]{1,0:T(8,128)(2,1)}, u32[]{:S(2)}, u32[]{:S(2)}) collective-permute-start(bf16[192,3072]{1,0:T(8,128)(2,1)} %collective-permute-done.4.refs_25_.refs_0_.refs_16_), channel_id=1, source_target_pairs={{0,16},{16,0},{1,17},{17,1},{2,18},{18,2},{3,19},{19,3},{4,20},{20... | collective-permute-start | bytes 3538952 | tf_op jit(solution)/shard_map/ppermute | solution.py:506
  102.9 29.3 %collective-permute-start.16 = (bf16[1536,384]{1,0:T(8,128)(2,1)}, bf16[1536,384]{1,0:T(8,128)(2,1)}, u32[]{:S(2)}, u32[]{:S(2)}) collective-permute-start(bf16[1536,384]{1,0:T(8,128)(2,1)} %broadcast_select_fusion.1), channel_id=1, source_target_pairs={{0,4},{4,0},{8,12},{12,8},{1,5},{5,1},{9,13},{13,9},{2,6},{6,2},{1... | collective-permute-start | bytes 3538952 | tf_op jit(solution)/shard_map/ppermute | solution.py:496
  105.9 26.4 %collective-permute-start.17 = (bf16[1536,384]{1,0:T(8,128)(2,1)}, bf16[1536,384]{1,0:T(8,128)(2,1)}, u32[]{:S(2)}, u32[]{:S(2)}) collective-permute-start(bf16[1536,384]{1,0:T(8,128)(2,1)} %get-tuple-element.210.refs_11_.refs_19_.refs_10_), channel_id=1, source_target_pairs={{4,8},{8,4},{5,9},{9,5},{6,10},{10,6},{7,11},{11,7},{20,24},{24,20... | collective-permute-start | bytes 3538952 | tf_op jit(solution)/shard_map/ppermute | solution.py:502
  107.5 1.0 copy-start.6
  108.6 23.7 %collective-permute-start.21 = (bf16[192,3072]{1,0:T(8,128)(2,1)}, bf16[192,3072]{1,0:T(8,128)(2,1)}, u32[]{:S(2)}, u32[]{:S(2)}) collective-permute-start(bf16[192,3072]{1,0:T(8,128)(2,1)} %collective-permute-done.13.refs_5_.refs_13_), channel_id=1, source_target_pairs={{0,1},{1,0},{2,3},{3,2},{4,5},{5,4},{6,7},{7,6},{8,9},{9,8},{10,11... | collective-permute-start | bytes 3538952 | tf_op jit(solution)/shard_map/ppermute | solution.py:513
  113.8 18.5 %copy-start.3 = (bf16[192,3072]{1,0:T(8,128)(2,1)S(1)}, bf16[192,3072]{1,0:T(8,128)(2,1)}, u32[]{:S(2)}) copy-start(bf16[192,3072]{1,0:T(8,128)(2,1)} %copy-done.2) | copy-start | bytes 3538948
  132.3 8.0 %collective-permute-start.26 = (bf16[384,3072]{1,0:T(8,128)(2,1)}, bf16[384,3072]{1,0:T(8,128)(2,1)}, u32[]{:S(2)}, u32[]{:S(2)}) collective-permute-start(bf16[384,3072]{1,0:T(8,128)(2,1)} %pad_maximum_fusion), channel_id=1, source_target_pairs={{0,1},{1,0},{2,3},{3,2},{4,5},{5,4},{6,7},{7,6},{8,9},{9,8},{10,11... | collective-permute-start | bytes 7077896 | tf_op jit(solution)/shard_map/ppermute | solution.py:513
  132.4 32.5 %collective-permute-start.24 = (bf16[192,3072]{1,0:T(8,128)(2,1)S(1)}, bf16[192,3072]{1,0:T(8,128)(2,1)}, u32[]{:S(2)}, u32[]{:S(2)}) collective-permute-start(bf16[192,3072]{1,0:T(8,128)(2,1)S(1)} %copy-done.3), channel_id=1, source_target_pairs={{0,2},{2,0},{1,3},{3,1},{4,6},{6,4},{5,7},{7,5},{8,10},{10,8},{9,1... | collective-permute-start | bytes 3538952 | tf_op jit(solution)/shard_map/ppermute | solution.py:505
  133.4 31.5 %collective-permute-start.25 = (bf16[192,3072]{1,0:T(8,128)(2,1)S(1)}, bf16[192,3072]{1,0:T(8,128)(2,1)}, u32[]{:S(2)}, u32[]{:S(2)}) collective-permute-start(bf16[192,3072]{1,0:T(8,128)(2,1)S(1)} %copy-done.3), channel_id=1, source_target_pairs={{0,16},{16,0},{1,17},{17,1},{2,18},{18,2},{3,19},{19,3},{4,20},{20... | collective-permute-start | bytes 3538952 | tf_op jit(solution)/shard_map/ppermute | solution.py:506
  134.9 29.9 %collective-permute-start.22 = (bf16[1536,384]{1,0:T(8,128)(2,1)}, bf16[1536,384]{1,0:T(8,128)(2,1)}, u32[]{:S(2)}, u32[]{:S(2)}) collective-permute-start(bf16[1536,384]{1,0:T(8,128)(2,1)} %broadcast_select_fusion), channel_id=1, source_target_pairs={{0,4},{4,0},{8,12},{12,8},{1,5},{5,1},{9,13},{13,9},{2,6},{6,2},{1... | collective-permute-start | bytes 3538952 | tf_op jit(solution)/shard_map/ppermute | solution.py:496
  138.5 26.3 %collective-permute-start.23 = (bf16[1536,384]{1,0:T(8,128)(2,1)}, bf16[1536,384]{1,0:T(8,128)(2,1)}, u32[]{:S(2)}, u32[]{:S(2)}) collective-permute-start(bf16[1536,384]{1,0:T(8,128)(2,1)} %collective-permute-done.16.refs_27_.refs_17_), channel_id=1, source_target_pairs={{4,8},{8,4},{5,9},{9,5},{6,10},{10,6},{7,11},{11,7},{20,24},{24,20... | collective-permute-start | bytes 3538952 | tf_op jit(solution)/shard_map/ppermute | solution.py:502
  140.2 24.6 %collective-permute-start.27 = (bf16[192,3072]{1,0:T(8,128)(2,1)}, bf16[192,3072]{1,0:T(8,128)(2,1)}, u32[]{:S(2)}, u32[]{:S(2)}) collective-permute-start(bf16[192,3072]{1,0:T(8,128)(2,1)} %collective-permute-done.18.refs_4_.refs_20_), channel_id=1, source_target_pairs={{0,1},{1,0},{2,3},{3,2},{4,5},{5,4},{6,7},{7,6},{8,9},{9,8},{10,11... | collective-permute-start | bytes 3538952 | tf_op jit(solution)/shard_map/ppermute | solution.py:513
  164.9 4.7 %collective-permute-start.28 = (bf16[192,3072]{1,0:T(8,128)(2,1)}, bf16[192,3072]{1,0:T(8,128)(2,1)S(1)}, u32[]{:S(2)}, u32[]{:S(2)}) collective-permute-start(bf16[192,3072]{1,0:T(8,128)(2,1)} %collective-permute-done.24.refs_5_.refs_21_), channel_id=1, source_target_pairs={{0,1},{1,0},{2,3},{3,2},{4,5},{5,4},{6,7},{7,6},{8,9},{9,8},{10,11... | collective-permute-start | bytes 3538952 | tf_op jit(solution)/shard_map/ppermute | solution.py:513
  164.9 32.1 %collective-permute-start.32 = (bf16[192,3072]{1,0:T(8,128)(2,1)}, bf16[192,3072]{1,0:T(8,128)(2,1)}, u32[]{:S(2)}, u32[]{:S(2)}) collective-permute-start(bf16[192,3072]{1,0:T(8,128)(2,1)} %collective-permute-done.24.refs_5_.refs_21_), channel_id=1, source_target_pairs={{0,16},{16,0},{1,17},{17,1},{2,18},{18,2},{3,19},{19,3},{4,20},{20... | collective-permute-start | bytes 3538952 | tf_op jit(solution)/shard_map/ppermute | solution.py:506
  165.5 31.5 %collective-permute-start.29 = (bf16[1536,384]{1,0:T(8,128)(2,1)}, bf16[1536,384]{1,0:T(8,128)(2,1)}, u32[]{:S(2)}, u32[]{:S(2)}) collective-permute-start(bf16[1536,384]{1,0:T(8,128)(2,1)} %collective-permute-done.23.refs_16_), channel_id=1, source_target_pairs={{4,0},{8,12},{5,1},{9,13},{6,2},{10,14},{7,3},{11,15},{20,16},{24,... | collective-permute-start | bytes 3538952 | tf_op jit(solution)/shard_map/ppermute | solution.py:499
  166.8 30.2 %collective-permute-start.30 = (bf16[1536,384]{1,0:T(8,128)(2,1)}, bf16[1536,384]{1,0:T(8,128)(2,1)}, u32[]{:S(2)}, u32[]{:S(2)}) collective-permute-start(bf16[1536,384]{1,0:T(8,128)(2,1)} %collective-permute-done.22.refs_18_.refs_8_), channel_id=1, source_target_pairs={{4,8},{8,4},{5,9},{9,5},{6,10},{10,6},{7,11},{11,7},{20,24},{24,20... | collective-permute-start | bytes 3538952 | tf_op jit(solution)/shard_map/ppermute | solution.py:502
  168.5 28.5 %collective-permute-start.31 = (bf16[192,3072]{1,0:T(8,128)(2,1)}, bf16[192,3072]{1,0:T(8,128)(2,1)}, u32[]{:S(2)}, u32[]{:S(2)}) collective-permute-start(bf16[192,3072]{1,0:T(8,128)(2,1)} %collective-permute-done.19.refs_0_), channel_id=1, source_target_pairs={{0,2},{2,0},{1,3},{3,1},{4,6},{6,4},{5,7},{7,5},{8,10},{10,8},{9,1... | collective-permute-start | bytes 3538952 | tf_op jit(solution)/shard_map/ppermute | solution.py:505
  169.6 14.2 %copy-start.7 = (bf16[192,3072]{1,0:T(8,128)(2,1)}, bf16[192,3072]{1,0:T(8,128)(2,1)S(1)}, u32[]{:S(2)}) copy-start(bf16[192,3072]{1,0:T(8,128)(2,1)S(1)} %collective-permute-done.28.refs_7_.refs_23_) | copy-start | bytes 3538948
  169.6 27.4 %collective-permute-start.33 = (bf16[192,3072]{1,0:T(8,128)(2,1)}, bf16[192,3072]{1,0:T(8,128)(2,1)}, u32[]{:S(2)}, u32[]{:S(2)}) collective-permute-start(bf16[192,3072]{1,0:T(8,128)(2,1)} %collective-permute-done.19.refs_0_), channel_id=1, source_target_pairs={{0,1},{1,0},{2,3},{3,2},{4,5},{5,4},{6,7},{7,6},{8,9},{9,8},{10,11... | collective-permute-start | bytes 3538952 | tf_op jit(solution)/shard_map/ppermute | solution.py:513
  197.0 17.3 %collective-permute-start.39 = (bf16[192,3072]{1,0:T(8,128)(2,1)}, bf16[192,3072]{1,0:T(8,128)(2,1)S(1)}, u32[]{:S(2)}, u32[]{:S(2)}) collective-permute-start(bf16[192,3072]{1,0:T(8,128)(2,1)} %collective-permute-done.25.refs_1_), channel_id=1, source_target_pairs={{0,1},{1,0},{2,3},{3,2},{4,5},{5,4},{6,7},{7,6},{8,9},{9,8},{10,11... | collective-permute-start | bytes 3538952 | tf_op jit(solution)/shard_map/ppermute | solution.py:632
  197.1 18.1 %collective-permute-start.40 = (bf16[192,3072]{1,0:T(8,128)(2,1)}, bf16[192,3072]{1,0:T(8,128)(2,1)}, u32[]{:S(2)}, u32[]{:S(2)}) collective-permute-start(bf16[192,3072]{1,0:T(8,128)(2,1)} %collective-permute-done.31.refs_4_), channel_id=1, source_target_pairs={{0,1},{1,0},{2,3},{3,2},{4,5},{5,4},{6,7},{7,6},{8,9},{9,8},{10,11... | collective-permute-start | bytes 3538952 | tf_op jit(solution)/shard_map/ppermute | solution.py:632
  197.6 18.9 %collective-permute-start.41 = (bf16[192,3072]{1,0:T(8,128)(2,1)}, bf16[192,3072]{1,0:T(8,128)(2,1)}, u32[]{:S(2)}, u32[]{:S(2)}) collective-permute-start(bf16[192,3072]{1,0:T(8,128)(2,1)} %collective-permute-done.32.refs_5_), channel_id=1, source_target_pairs={{0,1},{1,0},{2,3},{3,2},{4,5},{5,4},{6,7},{7,6},{8,9},{9,8},{10,11... | collective-permute-start | bytes 3538952 | tf_op jit(solution)/shard_map/ppermute | solution.py:632
  211.7 20.6 %collective-permute-start.34 = (bf16[384,384]{1,0:T(8,128)(2,1)}, bf16[384,384]{1,0:T(8,128)(2,1)S(1)}, u32[]{:S(2)}, u32[]{:S(2)}) collective-permute-start(bf16[384,384]{1,0:T(8,128)(2,1)} %get-tuple-element.226), channel_id=1, source_target_pairs={{0,2},{2,0},{16,18},{18,16},{1,3},{3,1},{17,19},{19,17},{4,6},{6,4... | collective-permute-start | bytes 884744 | tf_op jit(solution)/shard_map/ppermute | solution.py:528
  212.8 19.4 %collective-permute-start.35 = (bf16[384,384]{1,0:T(8,128)(2,1)}, bf16[384,384]{1,0:T(8,128)(2,1)S(1)}, u32[]{:S(2)}, u32[]{:S(2)}) collective-permute-start(bf16[384,384]{1,0:T(8,128)(2,1)} %get-tuple-element.227), channel_id=1, source_target_pairs={{0,16},{2,18},{16,0},{18,2},{1,17},{3,19},{17,1},{19,3},{4,20},{6,... | collective-permute-start | bytes 884744 | tf_op jit(solution)/shard_map/ppermute | solution.py:528
  214.3 3.8 %copy-start.9 = (bf16[192,3072]{1,0:T(8,128)(2,1)}, bf16[192,3072]{1,0:T(8,128)(2,1)S(1)}, u32[]{:S(2)}) copy-start(bf16[192,3072]{1,0:T(8,128)(2,1)S(1)} %collective-permute-done.39.refs_3_) | copy-start | bytes 3538948
  214.3 17.9 %collective-permute-start.36 = (bf16[384,384]{1,0:T(8,128)(2,1)}, bf16[384,384]{1,0:T(8,128)(2,1)}, u32[]{:S(2)}, u32[]{:S(2)}) collective-permute-start(bf16[384,384]{1,0:T(8,128)(2,1)} %get-tuple-element.228), channel_id=1, source_target_pairs={{0,18},{2,16},{16,2},{18,0},{1,19},{3,17},{17,3},{19,1},{4,22},{6,... | collective-permute-start | bytes 884744 | tf_op jit(solution)/shard_map/ppermute | solution.py:528
  215.2 13.7 %collective-permute-start.37 = (bf16[384,128]{1,0:T(8,128)(2,1)}, bf16[384,128]{1,0:T(8,128)(2,1)S(1)}, u32[]{:S(2)}, u32[]{:S(2)}) collective-permute-start(bf16[384,128]{1,0:T(8,128)(2,1)} %get-tuple-element.229), channel_id=1, source_target_pairs={{4,0},{6,2},{8,12},{10,14},{20,16},{22,18},{24,28},{26,30},{5,1},{... | collective-permute-start | bytes 294920 | tf_op jit(solution)/shard_map/ppermute | solution.py:663
  216.5 13.7 %collective-permute-start.38 = (bf16[384,128]{1,0:T(8,128)(2,1)}, bf16[384,128]{1,0:T(8,128)(2,1)S(1)}, u32[]{:S(2)}, u32[]{:S(2)}) collective-permute-start(bf16[384,128]{1,0:T(8,128)(2,1)} %get-tuple-element.230), channel_id=1, source_target_pairs={{4,2},{6,0},{8,14},{10,12},{20,18},{22,16},{24,30},{26,28},{5,3},{... | collective-permute-start | bytes 294920 | tf_op jit(solution)/shard_map/ppermute | solution.py:663
  228.9 12.3 %copy-start.12 = (bf16[384,128]{1,0:T(8,128)(2,1)}, bf16[384,128]{1,0:T(8,128)(2,1)S(1)}, u32[]{:S(2)}) copy-start(bf16[384,128]{1,0:T(8,128)(2,1)S(1)} %collective-permute-done.37.refs_4_) | copy-start | bytes 294916
  228.9 10.5 %collective-permute-start.42 = (bf16[384,128]{1,0:T(8,128)(2,1)}, bf16[384,128]{1,0:T(8,128)(2,1)S(1)}, u32[]{:S(2)}, u32[]{:S(2)}) collective-permute-start(bf16[384,128]{1,0:T(8,128)(2,1)} %get-tuple-element.235), channel_id=1, source_target_pairs={{4,16},{6,18},{8,28},{10,30},{20,0},{22,2},{24,12},{26,14},{5,17},... | collective-permute-start | bytes 294920 | tf_op jit(solution)/shard_map/ppermute | solution.py:663
  230.2 11.0 %copy-start.13 = (bf16[384,128]{1,0:T(8,128)(2,1)}, bf16[384,128]{1,0:T(8,128)(2,1)S(1)}, u32[]{:S(2)}) copy-start(bf16[384,128]{1,0:T(8,128)(2,1)S(1)} %collective-permute-done.38.refs_5_) | copy-start | bytes 294916
  230.2 11.0 %collective-permute-start.43 = (bf16[384,128]{1,0:T(8,128)(2,1)}, bf16[384,128]{1,0:T(8,128)(2,1)S(1)}, u32[]{:S(2)}, u32[]{:S(2)}) collective-permute-start(bf16[384,128]{1,0:T(8,128)(2,1)} %get-tuple-element.236), channel_id=1, source_target_pairs={{4,18},{6,16},{8,30},{10,28},{20,2},{22,0},{24,14},{26,12},{5,19},... | collective-permute-start | bytes 294920 | tf_op jit(solution)/shard_map/ppermute | solution.py:663
  232.3 9.0 %copy-start.10 = (bf16[384,384]{1,0:T(8,128)(2,1)}, bf16[384,384]{1,0:T(8,128)(2,1)S(1)}, u32[]{:S(2)}) copy-start(bf16[384,384]{1,0:T(8,128)(2,1)S(1)} %collective-permute-done.34.refs_1_) | copy-start | bytes 884740
  232.3 9.0 %copy-start.11 = (bf16[384,384]{1,0:T(8,128)(2,1)}, bf16[384,384]{1,0:T(8,128)(2,1)S(1)}, u32[]{:S(2)}) copy-start(bf16[384,384]{1,0:T(8,128)(2,1)S(1)} %collective-permute-done.35.refs_2_) | copy-start | bytes 884740
  239.4 1.8 copy-start.14
  241.2 0.6 copy-start.15

commit v2 on v0

--- a/solution.py
+++ b/solution.py
@@ -141,7 +141,7 @@
 def normalize_part(tokens, ln_gain, weight, part, other, taken=()):
     width = tokens.shape[2]
     piece = weight.shape[1:]
-    step = 64 if part % 64 == 0 else 32
+    step = 96 if part % 96 == 0 else 32
     anywhere = pl.BlockSpec(memory_space=pl.ANY)
     half = jax.ShapeDtypeStruct((part, width // 2), jnp.bfloat16)
     got = pl.pallas_call(
@@ -291,7 +291,7 @@
             for j in plan.added[i]:
                 partial_copy(i, j).start()
 
-    ahead = 2
+    ahead = 1
     for stage in stages[:ahead]:
         start_stage(*stage)
     for copy in carry_copies():

time: 245 us -> 246 us (level)
  Pallas kernels: 92.4 us -> 96.2 us
    pallas_call x6, Pallas kernels: 79.4 us -> 82.7 us  [run_jobs(): pl.pallas_call(functools.partial(job_kernel, plan), out_shape=shapes, in_...]
  transfers between devices with their start and end apart: 44 -> 44, of which waited for: 11 -> 11; matrix products, arithmetic and copies ran while one was open for 7% -> 7% of each run, Pallas kernels for 35% -> 36%
where the time goes in v2:
time: 246 us; the launch traced here: 245 us
  Pallas kernels  96.2 us (39%)
  waiting for transfers between devices  78.2 us (32%)
  starting transfers between devices  50.9 us (21%)
  local copies, waits for them, and re-layouts  9.87 us (4%)
  other arithmetic  9.6 us (4%)
    pallas_call x6, Pallas kernels, run_jobs(): pl.pallas_call(functools.partial(job_kernel, plan), out_shape=shapes, in_...  82.7 us
    ppermute x5, waiting for transfers between devices, pair(): return lax.ppermute(value, 'dp', [(0, 1), (1, 0), (2, 3), (3, 2)])  44.2 us
    ppermute x6, waiting for transfers between devices, shared(): beside = lambda value: lax.ppermute(value, 'seq', swap)  17.2 us
    ppermute x5, starting transfers between devices, pair(): return lax.ppermute(value, 'dp', [(0, 1), (1, 0), (2, 3), (3, 2)])  16.1 us
    pallas_call x2, Pallas kernels, normalize_part(): pl.pallas_call(functools.partial(normalize_kernel, step, other, taken), o...  10.4 us
    ppermute x4, waiting for transfers between devices, hand_back(): got.append(lax.ppermute(sent, ('groups', 'dp', 'seq'), steps))  9.42 us
    ppermute x6, starting transfers between devices, middle(): return lax.ppermute(value, 'dp', [(1, 2), (2, 1)])  9.15 us
    ppermute x6, starting transfers between devices, shared(): beside = lambda value: lax.ppermute(value, 'seq', swap)  8.12 us
  transfers between devices with their start and end apart: 44, of which 11 were waited for; matrix products, arithmetic and copies ran while one was open for 7% of the time, Pallas kernels for 36%

profile of v2, /device:TPU:0, one launch (start us, length us, event | category | flops | bytes accessed | tf_op | source)
XLA Modules:
  0.0 245.4 jit_solution(18243055281365961152)
XLA Ops:
  0.0 5.4 %shard_map.37 = (bf16[192,3072]{1,0:T(8,128)(2,1)}, bf16[192,3072]{1,0:T(8,128)(2,1)}, bf16[1536,384]{1,0:T(8,128)(2,1)}) custom-call(bf16[1,384,6144]{2,1,0:T(8,128)(2,1)} %tokens_ref.2, f32[1,6144]{1,0:T(1,128)} %bitcast.35, bf16[6,1536,384]{2,1,0:T(8,128)(2,1)} %bitcast.23), custom_call_target="tpu_custom_call" | custom-call | flops 9437184 | bytes 4718592 | tf_op jit(solution)/shard_map/pallas_call | solution.py:147
  5.4 3.0 %collective-permute-start = (bf16[192,3072]{1,0:T(8,128)(2,1)}, bf16[192,3072]{1,0:T(8,128)(2,1)}, u32[]{:S(2)}, u32[]{:S(2)}) collective-permute-start(bf16[192,3072]{1,0:T(8,128)(2,1)} %get-tuple-element.124.refs_0_.refs_8_), channel_id=1, source_target_pairs={{0,2},{2,0},{1,3},{3,1},{4,6},{6,4},{5,7},{7,5},{8,10},{10,8},{9,1... | collective-permute-start | bytes 3538952 | tf_op jit(solution)/shard_map/ppermute | solution.py:505
  8.4 1.5 collective-permute-start.1
  9.9 1.6 collective-permute-start.2
  11.5 1.7 collective-permute-start.3
  13.2 2.9 %dynamic-slice_bitcast_fusion = (bf16[1536,384]{1,0:T(8,128)(2,1)}, bf16[1,1536,384]{2,1,0:T(8,128)(2,1)S(1)}) fusion(bf16[6,1536,384]{2,1,0:T(8,128)(2,1)} %bitcast.24, s32[]{:T(128)S(6)} %select_n.63, s32[]{:T(128)S(6)} %select_n.62), kind=kLoop, calls=%fused_computation.1 | loop fusion | bytes 4718600 | tf_op jit(solution)/shard_map/jit(dynamic_index_in_dim)/squeeze | solution.py:539
  16.1 1.2 copy.7
  17.3 0.9 copy-done.1
  18.2 1.1 broadcast_select_fusion.3
  19.4 0.6 pad_add_fusion.role_ref
  19.9 14.8 %collective-permute-done.refs_4_.refs_12_ = bf16[192,3072]{1,0:T(8,128)(2,1)} collective-permute-done((bf16[192,3072]{1,0:T(8,128)(2,1)}, bf16[192,3072]{1,0:T(8,128)(2,1)}, u32[]{:S(2)}, u32[]{:S(2)}) %collective-permute-start) | collective-permute-done | bytes 1179680 | tf_op jit(solution)/shard_map/ppermute | solution.py:505
  34.7 1.5 collective-permute-done.1.refs_0_.refs_8_
  36.6 1.7 collective-permute-start.7
  38.2 3.8 %collective-permute-start.4 = (bf16[192,3072]{1,0:T(8,128)(2,1)}, bf16[192,3072]{1,0:T(8,128)(2,1)}, u32[]{:S(2)}, u32[]{:S(2)}) collective-permute-start(bf16[192,3072]{1,0:T(8,128)(2,1)} %broadcast_select_fusion.3), channel_id=1, source_target_pairs={{0,4},{4,0},{8,12},{12,8},{1,5},{5,1},{9,13},{13,9},{2,6},{6,2},{1... | collective-permute-start | bytes 3538952 | tf_op jit(solution)/shard_map/ppermute | solution.py:496
  42.0 1.7 collective-permute-start.5
  43.7 2.5 %copy.8 = bf16[24,8,8,384]{3,1,2,0:T(8,128)(2,1)} copy(bf16[24,8,8,384]{3,1,0,2:T(8,128)(2,1)} %bitcast.21) | data formatting | bytes 2359296
  46.2 5.0 %shard_map.38 = (bf16[192,3072]{1,0:T(8,128)(2,1)}, bf16[192,3072]{1,0:T(8,128)(2,1)}) custom-call(bf16[1,384,6144]{2,1,0:T(8,128)(2,1)} %tokens_ref.2, f32[1,6144]{1,0:T(1,128)} %bitcast.36, bf16[6,1536,384]{2,1,0:T(8,128)(2,1)} %bitcast.25), custom_call_target="tpu_custom_call" | custom-call | flops 9437184 | bytes 4718592 | tf_op jit(solution)/shard_map/pallas_call | solution.py:147
  51.2 1.4 broadcast_select_fusion.2
  52.6 14.2 %collective-permute-done.4.refs_25_.refs_0_.refs_16_ = bf16[192,3072]{1,0:T(8,128)(2,1)} collective-permute-done((bf16[192,3072]{1,0:T(8,128)(2,1)}, bf16[192,3072]{1,0:T(8,128)(2,1)}, u32[]{:S(2)}, u32[]{:S(2)}) %collective-permute-start.4) | collective-permute-done | bytes 1179680 | tf_op jit(solution)/shard_map/ppermute | solution.py:496
  66.9 4.2 %collective-permute-start.10 = (bf16[192,3072]{1,0:T(8,128)(2,1)S(1)}, bf16[192,3072]{1,0:T(8,128)(2,1)S(1)}, u32[]{:S(2)}, u32[]{:S(2)}) collective-permute-start(bf16[192,3072]{1,0:T(8,128)(2,1)S(1)} %broadcast_select_fusion.2), channel_id=1, source_target_pairs={{0,4},{4,0},{8,12},{12,8},{1,5},{5,1},{9,13},{13,9},{2,6},{6,2},{1... | collective-permute-start | bytes 3538952 | tf_op jit(solution)/shard_map/ppermute | solution.py:496
  71.1 0.7 collective-permute-start.11
  71.9 1.6 collective-permute-start.12
  73.4 0.5 collective-permute-start.13
  73.9 1.2 broadcast_select_fusion.1
  75.2 22.5 %collective-permute-done.10.refs_28_.refs_1_.refs_17_ = bf16[192,3072]{1,0:T(8,128)(2,1)S(1)} collective-permute-done((bf16[192,3072]{1,0:T(8,128)(2,1)S(1)}, bf16[192,3072]{1,0:T(8,128)(2,1)S(1)}, u32[]{:S(2)}, u32[]{:S(2)}) %collective-permute-start.10) | collective-permute-done | bytes 1179680 | tf_op jit(solution)/shard_map/ppermute | solution.py:496
  97.7 2.5 %collective-permute-done.12.refs_4_.refs_12_ = bf16[192,3072]{1,0:T(8,128)(2,1)S(1)} collective-permute-done((bf16[192,3072]{1,0:T(8,128)(2,1)}, bf16[192,3072]{1,0:T(8,128)(2,1)S(1)}, u32[]{:S(2)}, u32[]{:S(2)}) %collective-permute-start.12) | collective-permute-done | bytes 1179680 | tf_op jit(solution)/shard_map/ppermute | solution.py:505
  100.2 1.3 collective-permute-done.13.refs_5_.refs_13_
  101.6 1.1 collective-permute-start.18
  102.7 0.5 collective-permute-start.19
  103.2 2.9 %collective-permute-start.16 = (bf16[1536,384]{1,0:T(8,128)(2,1)}, bf16[1536,384]{1,0:T(8,128)(2,1)}, u32[]{:S(2)}, u32[]{:S(2)}) collective-permute-start(bf16[1536,384]{1,0:T(8,128)(2,1)} %broadcast_select_fusion.1), channel_id=1, source_target_pairs={{0,4},{4,0},{8,12},{12,8},{1,5},{5,1},{9,13},{13,9},{2,6},{6,2},{1... | collective-permute-start | bytes 3538952 | tf_op jit(solution)/shard_map/ppermute | solution.py:496
  106.1 1.7 collective-permute-start.17
  107.8 1.0 copy-done.6
  108.8 2.8 %pad_maximum_fusion = bf16[384,3072]{1,0:T(8,128)(2,1)} fusion(bf16[192,3072]{1,0:T(8,128)(2,1)S(1)} %collective-permute-done.10.refs_28_.refs_1_.refs_17_, bf16[192,3072]{1,0:T(8,128)(2,1)} %collective-permute-done.4.refs_25_.refs_0_.refs_16_), kind=kLoop, calls=%fused_computation | loop fusion | flops 4718592 | bytes 4718592 | tf_op jit(solution)/shard_map/concatenate | solution.py:579
  111.6 2.5 %broadcast_select_fusion = bf16[1536,384]{1,0:T(8,128)(2,1)} fusion(bf16[1536,384]{1,0:T(8,128)(2,1)S(1)} %collective-permute-done.11.refs_14_.refs_22_, bf16[1536,384]{1,0:T(8,128)(2,1)} %get-tuple-element.210.refs_11_.refs_19_.refs_10_, pred[]{:T(512)S(6)} %or.3), kind=kLoop, calls=%fused_computation.2 | loop fusion | flops 589824 | bytes 3538945 | tf_op jit(solution)/shard_map/jit(_where)/select_n | solution.py:493
  114.1 15.1 %shard_map.39 = (bf16[384,128]{1,0:T(8,128)(2,1)}, bf16[384,128]{1,0:T(8,128)(2,1)}, f32[768,384]{1,0:T(8,128)}, f32[768,384]{1,0:T(8,128)}) custom-call(s32[2]{0:T(128)} %pad_add_fusion.role_ref, bf16[192,3072]{1,0:T(8,128)(2,1)} %get-tuple-element.124.refs_0_.refs_8_, bf16[192,3072]{1,0:T(8,128)(2,1)} %get-tuple-element.132.refs_1_.refs_9_, ...), custom_call_target="tpu_custom_call" | custom-call | flops 6341787648 | tf_op jit(solution)/shard_map/pallas_call | solution.py:406
  129.2 3.3 %collective-permute-done.16.refs_27_.refs_17_ = bf16[1536,384]{1,0:T(8,128)(2,1)} collective-permute-done((bf16[1536,384]{1,0:T(8,128)(2,1)}, bf16[1536,384]{1,0:T(8,128)(2,1)}, u32[]{:S(2)}, u32[]{:S(2)}) %collective-permute-start.16) | collective-permute-done | bytes 1179680 | tf_op jit(solution)/shard_map/ppermute | solution.py:496
  132.6 1.0 collective-permute-start.24
  133.6 1.5 collective-permute-start.25
  135.1 3.6 %collective-permute-start.22 = (bf16[1536,384]{1,0:T(8,128)(2,1)}, bf16[1536,384]{1,0:T(8,128)(2,1)}, u32[]{:S(2)}, u32[]{:S(2)}) collective-permute-start(bf16[1536,384]{1,0:T(8,128)(2,1)} %broadcast_select_fusion), channel_id=1, source_target_pairs={{0,4},{4,0},{8,12},{12,8},{1,5},{5,1},{9,13},{13,9},{2,6},{6,2},{1... | collective-permute-start | bytes 3538952 | tf_op jit(solution)/shard_map/ppermute | solution.py:496
  138.8 1.7 collective-permute-start.23
  140.5 20.4 %shard_map.40 = (bf16[384,128]{1,0:T(8,128)(2,1)}, bf16[384,128]{1,0:T(8,128)(2,1)}, f32[768,384]{1,0:T(8,128)}, f32[768,384]{1,0:T(8,128)}, f32[768,384]{1,0:T(8,128)}, /*index=5*/f32[768,384]{1,0:T(8,128)}) custom-call(s32[2]{0:T(128)} %pad_add_fusion.role_ref, bf16[192,3072]{1,0:T(8,128)(2,1)} %collective-permute-done.1.refs_0_.refs_8_, ...), custom_call_target="tpu_custom_call" | custom-call | flops 9965666304 | tf_op jit(solution)/shard_map/pallas_call | solution.py:406
  160.9 4.2 %collective-permute-done.22.refs_18_.refs_8_ = bf16[1536,384]{1,0:T(8,128)(2,1)} collective-permute-done((bf16[1536,384]{1,0:T(8,128)(2,1)}, bf16[1536,384]{1,0:T(8,128)(2,1)}, u32[]{:S(2)}, u32[]{:S(2)}) %collective-permute-start.22) | collective-permute-done | bytes 1179680 | tf_op jit(solution)/shard_map/ppermute | solution.py:496
  165.2 0.6 collective-permute-start.32
  165.8 1.3 collective-permute-start.29
  167.0 1.7 collective-permute-start.30
  168.7 1.1 collective-permute-start.31
  169.8 13.6 %shard_map.41 = (bf16[384,128]{1,0:T(8,128)(2,1)}, bf16[384,128]{1,0:T(8,128)(2,1)}, f32[768,384]{1,0:T(8,128)}, bf16[384,128]{1,0:T(8,128)(2,1)}, bf16[384,128]{1,0:T(8,128)(2,1)}, /*index=5*/f32[768,384]{1,0:T(8,128)}) custom-call(s32[2]{0:T(128)} %pad_add_fusion.role_ref, bf16[192,3072]{1,0:T(8,128)(2,1)} %get-tuple-element.124.refs_0_.refs_8_, ...), custom_call_target="tpu_custom_call" | custom-call | flops 3623878656 | tf_op jit(solution)/shard_map/pallas_call | solution.py:406
  183.4 9.3 %shard_map.42.refs_28_ = f32[768,384]{1,0:T(8,128)} custom-call(s32[2]{0:T(128)} %pad_add_fusion.role_ref, bf16[192,3072]{1,0:T(8,128)(2,1)} %collective-permute-done.4.refs_25_.refs_0_.refs_16_, bf16[192,3072]{1,0:T(8,128)(2,1)} %copy-done.2, bf16[384,3072]{1,0:T(8,128)(2,1)} %collective-permute-done.26.refs_2_.refs_3_.refs_18_.refs_19_, ...), custom_call_target="tpu_custom_call" | custom-call | flops 2717908992 | tf_op jit(solution)/shard_map/pallas_call | solution.py:406
  192.7 4.5 %collective-permute-done.29.refs_25_ = bf16[1536,384]{1,0:T(8,128)(2,1)} collective-permute-done((bf16[1536,384]{1,0:T(8,128)(2,1)}, bf16[1536,384]{1,0:T(8,128)(2,1)}, u32[]{:S(2)}, u32[]{:S(2)}) %collective-permute-start.29) | collective-permute-done | bytes 1179680 | tf_op jit(solution)/shard_map/ppermute | solution.py:499
  197.3 0.5 collective-permute-start.40
  197.9 12.6 %shard_map.43 = (bf16[384,384]{1,0:T(8,128)(2,1)}, bf16[384,384]{1,0:T(8,128)(2,1)}, bf16[384,384]{1,0:T(8,128)(2,1)}, bf16[384,384]{1,0:T(8,128)(2,1)}, bf16[38...) custom-call(s32[2]{0:T(128)} %pad_add_fusion.role_ref, bf16[192,3072]{1,0:T(8,128)(2,1)} %get-tuple-element.124.refs_0_.refs_8_, ...), custom_call_target="tpu_custom_call" | custom-call | flops 2717908992 | tf_op jit(solution)/shard_map/pallas_call | solution.py:406
  210.5 1.1 collective-permute-start.34
  211.7 1.5 collective-permute-start.35
  213.2 0.9 collective-permute-start.36
  214.1 1.3 collective-permute-start.37
  215.4 1.6 collective-permute-start.38
  216.9 11.7 %shard_map.44 = (bf16[384,128]{1,0:T(8,128)(2,1)}, bf16[384,128]{1,0:T(8,128)(2,1)}) custom-call(s32[2]{0:T(128)} %pad_add_fusion.role_ref, bf16[192,3072]{1,0:T(8,128)(2,1)} %collective-permute-done.19.refs_0_, bf16[192,3072]{1,0:T(8,128)(2,1)} %collective-permute-done.25.refs_1_, bf16[192,3072]{1,0:T(8,128)(2,1)} %collective-permute-done.33.refs_2_, ...), custom_call_target="tpu_custom_call" | custom-call | flops 3623878656 | tf_op jit(solution)/shard_map/pallas_call | solution.py:406
  228.6 1.3 collective-permute-start.42
  230.0 1.3 collective-permute-start.43
  231.3 0.7 stack.34.place_ref
  232.0 7.6 %collective-permute-done.42.refs_6_ = bf16[384,128]{1,0:T(8,128)(2,1)S(1)} collective-permute-done((bf16[384,128]{1,0:T(8,128)(2,1)}, bf16[384,128]{1,0:T(8,128)(2,1)S(1)}, u32[]{:S(2)}, u32[]{:S(2)}) %collective-permute-start.42) | collective-permute-done | bytes 98336 | tf_op jit(solution)/shard_map/ppermute | solution.py:663
  239.6 1.8 collective-permute-done.43.refs_7_
  241.5 0.6 copy-done.15
  242.1 3.1 %shard_map.45 = bf16[384,1536]{1,0:T(8,128)(2,1)} custom-call(s32[5]{0:T(128)} %stack.34.place_ref, bf16[384,384]{1,0:T(8,128)(2,1)} %get-tuple-element.225.refs_0_, bf16[384,384]{1,0:T(8,128)(2,1)} %copy-done.10, bf16[384,384]{1,0:T(8,128)(2,1)} %copy-done.11, bf16[384,384]{1,0:T(8,128)(2,1)} %collective-permute-done.36.refs_3_, ...), custom_call_target="tpu_custom_call" | custom-call | bytes 2359296 | tf_op jit(solution)/shard_map/pallas_call | solution.py:467
  (75 shorter events, 1.0 us)
Async XLA Ops:
  5.4 29.3 %collective-permute-start = (bf16[192,3072]{1,0:T(8,128)(2,1)}, bf16[192,3072]{1,0:T(8,128)(2,1)}, u32[]{:S(2)}, u32[]{:S(2)}) collective-permute-start(bf16[192,3072]{1,0:T(8,128)(2,1)} %get-tuple-element.124.refs_0_.refs_8_), channel_id=1, source_target_pairs={{0,2},{2,0},{1,3},{3,1},{4,6},{6,4},{5,7},{7,5},{8,10},{10,8},{9,1... | collective-permute-start | bytes 3538952 | tf_op jit(solution)/shard_map/ppermute | solution.py:505
  8.4 27.7 %collective-permute-start.1 = (bf16[192,3072]{1,0:T(8,128)(2,1)}, bf16[192,3072]{1,0:T(8,128)(2,1)}, u32[]{:S(2)}, u32[]{:S(2)}) collective-permute-start(bf16[192,3072]{1,0:T(8,128)(2,1)} %get-tuple-element.124.refs_0_.refs_8_), channel_id=1, source_target_pairs={{0,16},{16,0},{1,17},{17,1},{2,18},{18,2},{3,19},{19,3},{4,20},{20... | collective-permute-start | bytes 3538952 | tf_op jit(solution)/shard_map/ppermute | solution.py:506
  9.9 28.3 %collective-permute-start.2 = (bf16[1536,384]{1,0:T(8,128)(2,1)}, bf16[1536,384]{1,0:T(8,128)(2,1)}, u32[]{:S(2)}, u32[]{:S(2)}) collective-permute-start(bf16[1536,384]{1,0:T(8,128)(2,1)} %get-tuple-element.128.refs_8_.refs_10_.refs_16_.refs_18_), channel_id=1, source_target_pairs={{0,4},{4,0},{8,12},{12,8},{1,5},{5,1},{9,13},{13,9},{2,6},{6,2},{1... | collective-permute-start | bytes 3538952 | tf_op jit(solution)/shard_map/ppermute | solution.py:496
  11.5 26.7 %collective-permute-start.3 = (bf16[1536,384]{1,0:T(8,128)(2,1)}, bf16[1536,384]{1,0:T(8,128)(2,1)}, u32[]{:S(2)}, u32[]{:S(2)}) collective-permute-start(bf16[1536,384]{1,0:T(8,128)(2,1)} %get-tuple-element.128.refs_8_.refs_10_.refs_16_.refs_18_), channel_id=1, source_target_pairs={{4,8},{8,4},{5,9},{9,5},{6,10},{10,6},{7,11},{11,7},{20,24},{24,20... | collective-permute-start | bytes 3538952 | tf_op jit(solution)/shard_map/ppermute | solution.py:502
  16.1 57.8 %copy-start = (bf16[1,1536,384]{2,1,0:T(8,128)(2,1)}, bf16[1,1536,384]{2,1,0:T(8,128)(2,1)S(1)}, u32[]{:S(2)}) copy-start(bf16[1,1536,384]{2,1,0:T(8,128)(2,1)S(1)} %get-tuple-element.238) | copy-start | bytes 3538948
  16.1 2.1 copy-start.1
  36.2 7.5 %collective-permute-start.8 = (bf16[192,3072]{1,0:T(8,128)(2,1)}, bf16[192,3072]{1,0:T(8,128)(2,1)}, u32[]{:S(2)}, u32[]{:S(2)}) collective-permute-start(bf16[192,3072]{1,0:T(8,128)(2,1)} %collective-permute-done.refs_4_.refs_12_), channel_id=1, source_target_pairs={{0,1},{1,0},{2,3},{3,2},{4,5},{5,4},{6,7},{7,6},{8,9},{9,8},{10,11... | collective-permute-start | bytes 3538952 | tf_op jit(solution)/shard_map/ppermute | solution.py:513
  36.2 30.6 %collective-permute-start.6 = (bf16[192,3072]{1,0:T(8,128)(2,1)}, bf16[192,3072]{1,0:T(8,128)(2,1)}, u32[]{:S(2)}, u32[]{:S(2)}) collective-permute-start(bf16[192,3072]{1,0:T(8,128)(2,1)} %get-tuple-element.132.refs_1_.refs_9_), channel_id=1, source_target_pairs={{0,2},{2,0},{1,3},{3,1},{4,6},{6,4},{5,7},{7,5},{8,10},{10,8},{9,1... | collective-permute-start | bytes 3538952 | tf_op jit(solution)/shard_map/ppermute | solution.py:505
  36.6 30.3 %collective-permute-start.7 = (bf16[192,3072]{1,0:T(8,128)(2,1)}, bf16[192,3072]{1,0:T(8,128)(2,1)}, u32[]{:S(2)}, u32[]{:S(2)}) collective-permute-start(bf16[192,3072]{1,0:T(8,128)(2,1)} %get-tuple-element.132.refs_1_.refs_9_), channel_id=1, source_target_pairs={{0,16},{16,0},{1,17},{17,1},{2,18},{18,2},{3,19},{19,3},{4,20},{20... | collective-permute-start | bytes 3538952 | tf_op jit(solution)/shard_map/ppermute | solution.py:506
  38.2 28.6 %collective-permute-start.4 = (bf16[192,3072]{1,0:T(8,128)(2,1)}, bf16[192,3072]{1,0:T(8,128)(2,1)}, u32[]{:S(2)}, u32[]{:S(2)}) collective-permute-start(bf16[192,3072]{1,0:T(8,128)(2,1)} %broadcast_select_fusion.3), channel_id=1, source_target_pairs={{0,4},{4,0},{8,12},{12,8},{1,5},{5,1},{9,13},{13,9},{2,6},{6,2},{1... | collective-permute-start | bytes 3538952 | tf_op jit(solution)/shard_map/ppermute | solution.py:496
  42.0 24.8 %collective-permute-start.5 = (bf16[1536,384]{1,0:T(8,128)(2,1)}, bf16[1536,384]{1,0:T(8,128)(2,1)}, u32[]{:S(2)}, u32[]{:S(2)}) collective-permute-start(bf16[1536,384]{1,0:T(8,128)(2,1)} %collective-permute-done.2.refs_15_.refs_16_.refs_23_.refs_26_), channel_id=1, source_target_pairs={{4,8},{8,4},{5,9},{9,5},{6,10},{10,6},{7,11},{11,7},{20,24},{24,20... | collective-permute-start | bytes 3538952 | tf_op jit(solution)/shard_map/ppermute | solution.py:502
  43.7 23.1 %collective-permute-start.9 = (bf16[192,3072]{1,0:T(8,128)(2,1)}, bf16[192,3072]{1,0:T(8,128)(2,1)}, u32[]{:S(2)}, u32[]{:S(2)}) collective-permute-start(bf16[192,3072]{1,0:T(8,128)(2,1)} %collective-permute-done.1.refs_0_.refs_8_), channel_id=1, source_target_pairs={{0,1},{1,0},{2,3},{3,2},{4,5},{5,4},{6,7},{7,6},{8,9},{9,8},{10,11... | collective-permute-start | bytes 3538952 | tf_op jit(solution)/shard_map/ppermute | solution.py:513
  66.8 7.1 %collective-permute-start.14 = (bf16[192,3072]{1,0:T(8,128)(2,1)}, bf16[192,3072]{1,0:T(8,128)(2,1)}, u32[]{:S(2)}, u32[]{:S(2)}) collective-permute-start(bf16[192,3072]{1,0:T(8,128)(2,1)} %collective-permute-done.7.refs_1_.refs_9_), channel_id=1, source_target_pairs={{0,1},{1,0},{2,3},{3,2},{4,5},{5,4},{6,7},{7,6},{8,9},{9,8},{10,11... | collective-permute-start | bytes 3538952 | tf_op jit(solution)/shard_map/ppermute | solution.py:513
  66.9 30.8 %collective-permute-start.10 = (bf16[192,3072]{1,0:T(8,128)(2,1)S(1)}, bf16[192,3072]{1,0:T(8,128)(2,1)S(1)}, u32[]{:S(2)}, u32[]{:S(2)}) collective-permute-start(bf16[192,3072]{1,0:T(8,128)(2,1)S(1)} %broadcast_select_fusion.2), channel_id=1, source_target_pairs={{0,4},{4,0},{8,12},{12,8},{1,5},{5,1},{9,13},{13,9},{2,6},{6,2},{1... | collective-permute-start | bytes 3538952 | tf_op jit(solution)/shard_map/ppermute | solution.py:496
  71.1 26.6 %collective-permute-start.11 = (bf16[1536,384]{1,0:T(8,128)(2,1)S(1)}, bf16[1536,384]{1,0:T(8,128)(2,1)S(1)}, u32[]{:S(2)}, u32[]{:S(2)}) collective-permute-start(bf16[1536,384]{1,0:T(8,128)(2,1)S(1)} %bitcast.27), channel_id=1, source_target_pairs={{4,8},{8,4},{5,9},{9,5},{6,10},{10,6},{7,11},{11,7},{20,24},{24,20... | collective-permute-start | bytes 3538952 | tf_op jit(solution)/shard_map/ppermute | solution.py:502
  71.9 28.3 %collective-permute-start.12 = (bf16[192,3072]{1,0:T(8,128)(2,1)}, bf16[192,3072]{1,0:T(8,128)(2,1)S(1)}, u32[]{:S(2)}, u32[]{:S(2)}) collective-permute-start(bf16[192,3072]{1,0:T(8,128)(2,1)} %collective-permute-done.1.refs_0_.refs_8_), channel_id=1, source_target_pairs={{0,2},{2,0},{1,3},{3,1},{4,6},{6,4},{5,7},{7,5},{8,10},{10,8},{9,1... | collective-permute-start | bytes 3538952 | tf_op jit(solution)/shard_map/ppermute | solution.py:505
  73.4 28.1 %collective-permute-start.13 = (bf16[192,3072]{1,0:T(8,128)(2,1)}, bf16[192,3072]{1,0:T(8,128)(2,1)}, u32[]{:S(2)}, u32[]{:S(2)}) collective-permute-start(bf16[192,3072]{1,0:T(8,128)(2,1)} %collective-permute-done.6.refs_5_.refs_13_), channel_id=1, source_target_pairs={{0,16},{16,0},{1,17},{17,1},{2,18},{18,2},{3,19},{19,3},{4,20},{20... | collective-permute-start | bytes 3538952 | tf_op jit(solution)/shard_map/ppermute | solution.py:506
  73.9 27.6 %collective-permute-start.15 = (bf16[192,3072]{1,0:T(8,128)(2,1)}, bf16[192,3072]{1,0:T(8,128)(2,1)S(1)}, u32[]{:S(2)}, u32[]{:S(2)}) collective-permute-start(bf16[192,3072]{1,0:T(8,128)(2,1)} %collective-permute-done.6.refs_5_.refs_13_), channel_id=1, source_target_pairs={{0,1},{1,0},{2,3},{3,2},{4,5},{5,4},{6,7},{7,6},{8,9},{9,8},{10,11... | collective-permute-start | bytes 3538952 | tf_op jit(solution)/shard_map/ppermute | solution.py:513
  97.7 13.9 %copy-start.2 = (bf16[192,3072]{1,0:T(8,128)(2,1)}, bf16[192,3072]{1,0:T(8,128)(2,1)S(1)}, u32[]{:S(2)}) copy-start(bf16[192,3072]{1,0:T(8,128)(2,1)S(1)} %collective-permute-done.10.refs_28_.refs_1_.refs_17_) | copy-start | bytes 3538948
  97.7 13.9 %copy-start.8 = (bf16[1536,384]{1,0:T(8,128)(2,1)}, bf16[1536,384]{1,0:T(8,128)(2,1)S(1)}, u32[]{:S(2)}) copy-start(bf16[1536,384]{1,0:T(8,128)(2,1)S(1)} %collective-permute-done.11.refs_14_.refs_22_) | copy-start | bytes 3538948
  100.2 1.3 copy-start.4
  101.5 6.3 %copy-start.5 = (bf16[192,3072]{1,0:T(8,128)(2,1)}, bf16[192,3072]{1,0:T(8,128)(2,1)S(1)}, u32[]{:S(2)}) copy-start(bf16[192,3072]{1,0:T(8,128)(2,1)S(1)} %collective-permute-done.15.refs_7_.refs_15_) | copy-start | bytes 3538948
  101.5 6.3 %collective-permute-start.20 = (bf16[192,3072]{1,0:T(8,128)(2,1)S(1)}, bf16[192,3072]{1,0:T(8,128)(2,1)S(1)}, u32[]{:S(2)}, u32[]{:S(2)}) collective-permute-start(bf16[192,3072]{1,0:T(8,128)(2,1)S(1)} %collective-permute-done.12.refs_4_.refs_12_), channel_id=1, source_target_pairs={{0,1},{1,0},{2,3},{3,2},{4,5},{5,4},{6,7},{7,6},{8,9},{9,8},{10,11... | collective-permute-start | bytes 3538952 | tf_op jit(solution)/shard_map/ppermute | solution.py:513
  101.6 30.9 %collective-permute-start.18 = (bf16[192,3072]{1,0:T(8,128)(2,1)}, bf16[192,3072]{1,0:T(8,128)(2,1)}, u32[]{:S(2)}, u32[]{:S(2)}) collective-permute-start(bf16[192,3072]{1,0:T(8,128)(2,1)} %collective-permute-done.4.refs_25_.refs_0_.refs_16_), channel_id=1, source_target_pairs={{0,2},{2,0},{1,3},{3,1},{4,6},{6,4},{5,7},{7,5},{8,10},{10,8},{9,1... | collective-permute-start | bytes 3538952 | tf_op jit(solution)/shard_map/ppermute | solution.py:505
  102.7 29.8 %collective-permute-start.19 = (bf16[192,3072]{1,0:T(8,128)(2,1)}, bf16[192,3072]{1,0:T(8,128)(2,1)}, u32[]{:S(2)}, u32[]{:S(2)}) collective-permute-start(bf16[192,3072]{1,0:T(8,128)(2,1)} %collective-permute-done.4.refs_25_.refs_0_.refs_16_), channel_id=1, source_target_pairs={{0,16},{16,0},{1,17},{17,1},{2,18},{18,2},{3,19},{19,3},{4,20},{20... | collective-permute-start | bytes 3538952 | tf_op jit(solution)/shard_map/ppermute | solution.py:506
  103.2 29.3 %collective-permute-start.16 = (bf16[1536,384]{1,0:T(8,128)(2,1)}, bf16[1536,384]{1,0:T(8,128)(2,1)}, u32[]{:S(2)}, u32[]{:S(2)}) collective-permute-start(bf16[1536,384]{1,0:T(8,128)(2,1)} %broadcast_select_fusion.1), channel_id=1, source_target_pairs={{0,4},{4,0},{8,12},{12,8},{1,5},{5,1},{9,13},{13,9},{2,6},{6,2},{1... | collective-permute-start | bytes 3538952 | tf_op jit(solution)/shard_map/ppermute | solution.py:496
  106.1 26.4 %collective-permute-start.17 = (bf16[1536,384]{1,0:T(8,128)(2,1)}, bf16[1536,384]{1,0:T(8,128)(2,1)}, u32[]{:S(2)}, u32[]{:S(2)}) collective-permute-start(bf16[1536,384]{1,0:T(8,128)(2,1)} %get-tuple-element.210.refs_11_.refs_19_.refs_10_), channel_id=1, source_target_pairs={{4,8},{8,4},{5,9},{9,5},{6,10},{10,6},{7,11},{11,7},{20,24},{24,20... | collective-permute-start | bytes 3538952 | tf_op jit(solution)/shard_map/ppermute | solution.py:502
  107.8 1.0 copy-start.6
  108.8 23.7 %collective-permute-start.21 = (bf16[192,3072]{1,0:T(8,128)(2,1)}, bf16[192,3072]{1,0:T(8,128)(2,1)}, u32[]{:S(2)}, u32[]{:S(2)}) collective-permute-start(bf16[192,3072]{1,0:T(8,128)(2,1)} %collective-permute-done.13.refs_5_.refs_13_), channel_id=1, source_target_pairs={{0,1},{1,0},{2,3},{3,2},{4,5},{5,4},{6,7},{7,6},{8,9},{9,8},{10,11... | collective-permute-start | bytes 3538952 | tf_op jit(solution)/shard_map/ppermute | solution.py:513
  114.1 18.5 %copy-start.3 = (bf16[192,3072]{1,0:T(8,128)(2,1)S(1)}, bf16[192,3072]{1,0:T(8,128)(2,1)}, u32[]{:S(2)}) copy-start(bf16[192,3072]{1,0:T(8,128)(2,1)} %copy-done.2) | copy-start | bytes 3538948
  132.5 8.0 %collective-permute-start.26 = (bf16[384,3072]{1,0:T(8,128)(2,1)}, bf16[384,3072]{1,0:T(8,128)(2,1)}, u32[]{:S(2)}, u32[]{:S(2)}) collective-permute-start(bf16[384,3072]{1,0:T(8,128)(2,1)} %pad_maximum_fusion), channel_id=1, source_target_pairs={{0,1},{1,0},{2,3},{3,2},{4,5},{5,4},{6,7},{7,6},{8,9},{9,8},{10,11... | collective-permute-start | bytes 7077896 | tf_op jit(solution)/shard_map/ppermute | solution.py:513
  132.6 32.5 %collective-permute-start.24 = (bf16[192,3072]{1,0:T(8,128)(2,1)S(1)}, bf16[192,3072]{1,0:T(8,128)(2,1)}, u32[]{:S(2)}, u32[]{:S(2)}) collective-permute-start(bf16[192,3072]{1,0:T(8,128)(2,1)S(1)} %copy-done.3), channel_id=1, source_target_pairs={{0,2},{2,0},{1,3},{3,1},{4,6},{6,4},{5,7},{7,5},{8,10},{10,8},{9,1... | collective-permute-start | bytes 3538952 | tf_op jit(solution)/shard_map/ppermute | solution.py:505
  133.6 31.5 %collective-permute-start.25 = (bf16[192,3072]{1,0:T(8,128)(2,1)S(1)}, bf16[192,3072]{1,0:T(8,128)(2,1)}, u32[]{:S(2)}, u32[]{:S(2)}) collective-permute-start(bf16[192,3072]{1,0:T(8,128)(2,1)S(1)} %copy-done.3), channel_id=1, source_target_pairs={{0,16},{16,0},{1,17},{17,1},{2,18},{18,2},{3,19},{19,3},{4,20},{20... | collective-permute-start | bytes 3538952 | tf_op jit(solution)/shard_map/ppermute | solution.py:506
  135.1 29.9 %collective-permute-start.22 = (bf16[1536,384]{1,0:T(8,128)(2,1)}, bf16[1536,384]{1,0:T(8,128)(2,1)}, u32[]{:S(2)}, u32[]{:S(2)}) collective-permute-start(bf16[1536,384]{1,0:T(8,128)(2,1)} %broadcast_select_fusion), channel_id=1, source_target_pairs={{0,4},{4,0},{8,12},{12,8},{1,5},{5,1},{9,13},{13,9},{2,6},{6,2},{1... | collective-permute-start | bytes 3538952 | tf_op jit(solution)/shard_map/ppermute | solution.py:496
  138.8 26.3 %collective-permute-start.23 = (bf16[1536,384]{1,0:T(8,128)(2,1)}, bf16[1536,384]{1,0:T(8,128)(2,1)}, u32[]{:S(2)}, u32[]{:S(2)}) collective-permute-start(bf16[1536,384]{1,0:T(8,128)(2,1)} %collective-permute-done.16.refs_27_.refs_17_), channel_id=1, source_target_pairs={{4,8},{8,4},{5,9},{9,5},{6,10},{10,6},{7,11},{11,7},{20,24},{24,20... | collective-permute-start | bytes 3538952 | tf_op jit(solution)/shard_map/ppermute | solution.py:502
  140.5 24.6 %collective-permute-start.27 = (bf16[192,3072]{1,0:T(8,128)(2,1)}, bf16[192,3072]{1,0:T(8,128)(2,1)}, u32[]{:S(2)}, u32[]{:S(2)}) collective-permute-start(bf16[192,3072]{1,0:T(8,128)(2,1)} %collective-permute-done.18.refs_4_.refs_20_), channel_id=1, source_target_pairs={{0,1},{1,0},{2,3},{3,2},{4,5},{5,4},{6,7},{7,6},{8,9},{9,8},{10,11... | collective-permute-start | bytes 3538952 | tf_op jit(solution)/shard_map/ppermute | solution.py:513
  165.1 4.7 %collective-permute-start.28 = (bf16[192,3072]{1,0:T(8,128)(2,1)}, bf16[192,3072]{1,0:T(8,128)(2,1)S(1)}, u32[]{:S(2)}, u32[]{:S(2)}) collective-permute-start(bf16[192,3072]{1,0:T(8,128)(2,1)} %collective-permute-done.24.refs_5_.refs_21_), channel_id=1, source_target_pairs={{0,1},{1,0},{2,3},{3,2},{4,5},{5,4},{6,7},{7,6},{8,9},{9,8},{10,11... | collective-permute-start | bytes 3538952 | tf_op jit(solution)/shard_map/ppermute | solution.py:513
  165.2 32.1 %collective-permute-start.32 = (bf16[192,3072]{1,0:T(8,128)(2,1)}, bf16[192,3072]{1,0:T(8,128)(2,1)}, u32[]{:S(2)}, u32[]{:S(2)}) collective-permute-start(bf16[192,3072]{1,0:T(8,128)(2,1)} %collective-permute-done.24.refs_5_.refs_21_), channel_id=1, source_target_pairs={{0,16},{16,0},{1,17},{17,1},{2,18},{18,2},{3,19},{19,3},{4,20},{20... | collective-permute-start | bytes 3538952 | tf_op jit(solution)/shard_map/ppermute | solution.py:506
  165.8 31.5 %collective-permute-start.29 = (bf16[1536,384]{1,0:T(8,128)(2,1)}, bf16[1536,384]{1,0:T(8,128)(2,1)}, u32[]{:S(2)}, u32[]{:S(2)}) collective-permute-start(bf16[1536,384]{1,0:T(8,128)(2,1)} %collective-permute-done.23.refs_16_), channel_id=1, source_target_pairs={{4,0},{8,12},{5,1},{9,13},{6,2},{10,14},{7,3},{11,15},{20,16},{24,... | collective-permute-start | bytes 3538952 | tf_op jit(solution)/shard_map/ppermute | solution.py:499
  167.0 30.2 %collective-permute-start.30 = (bf16[1536,384]{1,0:T(8,128)(2,1)}, bf16[1536,384]{1,0:T(8,128)(2,1)}, u32[]{:S(2)}, u32[]{:S(2)}) collective-permute-start(bf16[1536,384]{1,0:T(8,128)(2,1)} %collective-permute-done.22.refs_18_.refs_8_), channel_id=1, source_target_pairs={{4,8},{8,4},{5,9},{9,5},{6,10},{10,6},{7,11},{11,7},{20,24},{24,20... | collective-permute-start | bytes 3538952 | tf_op jit(solution)/shard_map/ppermute | solution.py:502
  168.7 28.5 %collective-permute-start.31 = (bf16[192,3072]{1,0:T(8,128)(2,1)}, bf16[192,3072]{1,0:T(8,128)(2,1)}, u32[]{:S(2)}, u32[]{:S(2)}) collective-permute-start(bf16[192,3072]{1,0:T(8,128)(2,1)} %collective-permute-done.19.refs_0_), channel_id=1, source_target_pairs={{0,2},{2,0},{1,3},{3,1},{4,6},{6,4},{5,7},{7,5},{8,10},{10,8},{9,1... | collective-permute-start | bytes 3538952 | tf_op jit(solution)/shard_map/ppermute | solution.py:505
  169.8 13.6 %copy-start.7 = (bf16[192,3072]{1,0:T(8,128)(2,1)}, bf16[192,3072]{1,0:T(8,128)(2,1)S(1)}, u32[]{:S(2)}) copy-start(bf16[192,3072]{1,0:T(8,128)(2,1)S(1)} %collective-permute-done.28.refs_7_.refs_23_) | copy-start | bytes 3538948
  169.8 27.4 %collective-permute-start.33 = (bf16[192,3072]{1,0:T(8,128)(2,1)}, bf16[192,3072]{1,0:T(8,128)(2,1)}, u32[]{:S(2)}, u32[]{:S(2)}) collective-permute-start(bf16[192,3072]{1,0:T(8,128)(2,1)} %collective-permute-done.19.refs_0_), channel_id=1, source_target_pairs={{0,1},{1,0},{2,3},{3,2},{4,5},{5,4},{6,7},{7,6},{8,9},{9,8},{10,11... | collective-permute-start | bytes 3538952 | tf_op jit(solution)/shard_map/ppermute | solution.py:513
  197.3 15.9 %collective-permute-start.39 = (bf16[192,3072]{1,0:T(8,128)(2,1)}, bf16[192,3072]{1,0:T(8,128)(2,1)S(1)}, u32[]{:S(2)}, u32[]{:S(2)}) collective-permute-start(bf16[192,3072]{1,0:T(8,128)(2,1)} %collective-permute-done.25.refs_1_), channel_id=1, source_target_pairs={{0,1},{1,0},{2,3},{3,2},{4,5},{5,4},{6,7},{7,6},{8,9},{9,8},{10,11... | collective-permute-start | bytes 3538952 | tf_op jit(solution)/shard_map/ppermute | solution.py:632
  197.3 16.7 %collective-permute-start.40 = (bf16[192,3072]{1,0:T(8,128)(2,1)}, bf16[192,3072]{1,0:T(8,128)(2,1)}, u32[]{:S(2)}, u32[]{:S(2)}) collective-permute-start(bf16[192,3072]{1,0:T(8,128)(2,1)} %collective-permute-done.31.refs_4_), channel_id=1, source_target_pairs={{0,1},{1,0},{2,3},{3,2},{4,5},{5,4},{6,7},{7,6},{8,9},{9,8},{10,11... | collective-permute-start | bytes 3538952 | tf_op jit(solution)/shard_map/ppermute | solution.py:632
  197.8 17.5 %collective-permute-start.41 = (bf16[192,3072]{1,0:T(8,128)(2,1)}, bf16[192,3072]{1,0:T(8,128)(2,1)}, u32[]{:S(2)}, u32[]{:S(2)}) collective-permute-start(bf16[192,3072]{1,0:T(8,128)(2,1)} %collective-permute-done.32.refs_5_), channel_id=1, source_target_pairs={{0,1},{1,0},{2,3},{3,2},{4,5},{5,4},{6,7},{7,6},{8,9},{9,8},{10,11... | collective-permute-start | bytes 3538952 | tf_op jit(solution)/shard_map/ppermute | solution.py:632
  210.5 21.5 %collective-permute-start.34 = (bf16[384,384]{1,0:T(8,128)(2,1)}, bf16[384,384]{1,0:T(8,128)(2,1)S(1)}, u32[]{:S(2)}, u32[]{:S(2)}) collective-permute-start(bf16[384,384]{1,0:T(8,128)(2,1)} %get-tuple-element.226), channel_id=1, source_target_pairs={{0,2},{2,0},{16,18},{18,16},{1,3},{3,1},{17,19},{19,17},{4,6},{6,4... | collective-permute-start | bytes 884744 | tf_op jit(solution)/shard_map/ppermute | solution.py:528
  211.7 20.3 %collective-permute-start.35 = (bf16[384,384]{1,0:T(8,128)(2,1)}, bf16[384,384]{1,0:T(8,128)(2,1)S(1)}, u32[]{:S(2)}, u32[]{:S(2)}) collective-permute-start(bf16[384,384]{1,0:T(8,128)(2,1)} %get-tuple-element.227), channel_id=1, source_target_pairs={{0,16},{2,18},{16,0},{18,2},{1,17},{3,19},{17,1},{19,3},{4,20},{6,... | collective-permute-start | bytes 884744 | tf_op jit(solution)/shard_map/ppermute | solution.py:528
  213.2 3.8 %copy-start.9 = (bf16[192,3072]{1,0:T(8,128)(2,1)}, bf16[192,3072]{1,0:T(8,128)(2,1)S(1)}, u32[]{:S(2)}) copy-start(bf16[192,3072]{1,0:T(8,128)(2,1)S(1)} %collective-permute-done.39.refs_3_) | copy-start | bytes 3538948
  213.2 18.8 %collective-permute-start.36 = (bf16[384,384]{1,0:T(8,128)(2,1)}, bf16[384,384]{1,0:T(8,128)(2,1)}, u32[]{:S(2)}, u32[]{:S(2)}) collective-permute-start(bf16[384,384]{1,0:T(8,128)(2,1)} %get-tuple-element.228), channel_id=1, source_target_pairs={{0,18},{2,16},{16,2},{18,0},{1,19},{3,17},{17,3},{19,1},{4,22},{6,... | collective-permute-start | bytes 884744 | tf_op jit(solution)/shard_map/ppermute | solution.py:528
  214.1 14.5 %collective-permute-start.37 = (bf16[384,128]{1,0:T(8,128)(2,1)}, bf16[384,128]{1,0:T(8,128)(2,1)S(1)}, u32[]{:S(2)}, u32[]{:S(2)}) collective-permute-start(bf16[384,128]{1,0:T(8,128)(2,1)} %get-tuple-element.229), channel_id=1, source_target_pairs={{4,0},{6,2},{8,12},{10,14},{20,16},{22,18},{24,28},{26,30},{5,1},{... | collective-permute-start | bytes 294920 | tf_op jit(solution)/shard_map/ppermute | solution.py:663
  215.4 14.6 %collective-permute-start.38 = (bf16[384,128]{1,0:T(8,128)(2,1)}, bf16[384,128]{1,0:T(8,128)(2,1)S(1)}, u32[]{:S(2)}, u32[]{:S(2)}) collective-permute-start(bf16[384,128]{1,0:T(8,128)(2,1)} %get-tuple-element.230), channel_id=1, source_target_pairs={{4,2},{6,0},{8,14},{10,12},{20,18},{22,16},{24,30},{26,28},{5,3},{... | collective-permute-start | bytes 294920 | tf_op jit(solution)/shard_map/ppermute | solution.py:663
  228.6 12.8 %copy-start.12 = (bf16[384,128]{1,0:T(8,128)(2,1)}, bf16[384,128]{1,0:T(8,128)(2,1)S(1)}, u32[]{:S(2)}) copy-start(bf16[384,128]{1,0:T(8,128)(2,1)S(1)} %collective-permute-done.37.refs_4_) | copy-start | bytes 294916
  228.6 11.0 %collective-permute-start.42 = (bf16[384,128]{1,0:T(8,128)(2,1)}, bf16[384,128]{1,0:T(8,128)(2,1)S(1)}, u32[]{:S(2)}, u32[]{:S(2)}) collective-permute-start(bf16[384,128]{1,0:T(8,128)(2,1)} %get-tuple-element.235), channel_id=1, source_target_pairs={{4,16},{6,18},{8,28},{10,30},{20,0},{22,2},{24,12},{26,14},{5,17},... | collective-permute-start | bytes 294920 | tf_op jit(solution)/shard_map/ppermute | solution.py:663
  229.9 11.5 %copy-start.13 = (bf16[384,128]{1,0:T(8,128)(2,1)}, bf16[384,128]{1,0:T(8,128)(2,1)S(1)}, u32[]{:S(2)}) copy-start(bf16[384,128]{1,0:T(8,128)(2,1)S(1)} %collective-permute-done.38.refs_5_) | copy-start | bytes 294916
  230.0 11.5 %collective-permute-start.43 = (bf16[384,128]{1,0:T(8,128)(2,1)}, bf16[384,128]{1,0:T(8,128)(2,1)S(1)}, u32[]{:S(2)}, u32[]{:S(2)}) collective-permute-start(bf16[384,128]{1,0:T(8,128)(2,1)} %get-tuple-element.236), channel_id=1, source_target_pairs={{4,18},{6,16},{8,30},{10,28},{20,2},{22,0},{24,14},{26,12},{5,19},... | collective-permute-start | bytes 294920 | tf_op jit(solution)/shard_map/ppermute | solution.py:663
  232.0 9.5 %copy-start.10 = (bf16[384,384]{1,0:T(8,128)(2,1)}, bf16[384,384]{1,0:T(8,128)(2,1)S(1)}, u32[]{:S(2)}) copy-start(bf16[384,384]{1,0:T(8,128)(2,1)S(1)} %collective-permute-done.34.refs_1_) | copy-start | bytes 884740
  232.0 9.5 %copy-start.11 = (bf16[384,384]{1,0:T(8,128)(2,1)}, bf16[384,384]{1,0:T(8,128)(2,1)S(1)}, u32[]{:S(2)}) copy-start(bf16[384,384]{1,0:T(8,128)(2,1)S(1)} %collective-permute-done.35.refs_2_) | copy-start | bytes 884740
  239.6 1.8 copy-start.14
  241.4 0.6 copy-start.15

commit v3 on v0

--- a/solution.py
+++ b/solution.py
@@ -495,9 +495,6 @@
     def pair(value):
         return lax.ppermute(value, "dp", [(0, 1), (1, 0), (2, 3), (3, 2)])
 
-    def outward(value):
-        return lax.ppermute(value, "dp", [(1, 0), (2, 3)])
-
     def middle(value):
         return lax.ppermute(value, "dp", [(1, 2), (2, 1)])
 
@@ -604,7 +601,7 @@
         )
     )
 
-    pair6, middle6 = outward(middle5), middle(pair5)
+    pair6, middle6 = pair(middle5), middle(pair5)
     beside6, across6 = beside(across4), across(beside5)
     far5, far_across4 = others(beside5, across4)
     ahead0, ahead1 = run(

time: 245 us -> 244 us (level)
    ppermute x1 -> x0, waiting for transfers between devices: 5.5 us -> none  [outward(): return lax.ppermute(value, 'dp', [(1, 0), (2, 3)])]
    ppermute x5 -> x6, starting transfers between devices: 16.1 us -> 19.7 us  [pair(): return lax.ppermute(value, 'dp', [(0, 1), (1, 0), (2, 3), (3, 2)])]
    ppermute x6, waiting for transfers between devices: 17.3 us -> 20.4 us  [shared(): beside = lambda value: lax.ppermute(value, 'seq', swap)]
    ppermute x5 -> x6, waiting for transfers between devices: 45.5 us -> 47.5 us  [pair(): return lax.ppermute(value, 'dp', [(0, 1), (1, 0), (2, 3), (3, 2)])]
  transfers between devices with their start and end apart: 44 -> 44, of which waited for: 11 -> 12; matrix products, arithmetic and copies ran while one was open for 7% -> 7% of each run, Pallas kernels for 35% -> 35%
where the time goes in v3:
time: 244 us
  Pallas kernels  92.4 us (38%)
  waiting for transfers between devices  78 us (32%)
  starting transfers between devices  53.1 us (22%)
  local copies, waits for them, and re-layouts  9.87 us (4%)
  other arithmetic  9.6 us (4%)
    pallas_call x6, Pallas kernels, run_jobs(): pl.pallas_call(functools.partial(job_kernel, plan), out_shape=shapes, in_...  79.4 us
    ppermute x6, waiting for transfers between devices, pair(): return lax.ppermute(value, 'dp', [(0, 1), (1, 0), (2, 3), (3, 2)])  47.5 us
    ppermute x6, waiting for transfers between devices, shared(): beside = lambda value: lax.ppermute(value, 'seq', swap)  20.4 us
    ppermute x6, starting transfers between devices, pair(): return lax.ppermute(value, 'dp', [(0, 1), (1, 0), (2, 3), (3, 2)])  19.7 us
    pallas_call x2, Pallas kernels, normalize_part(): pl.pallas_call(functools.partial(normalize_kernel, step, other, taken), o...  9.92 us
    ppermute x6, starting transfers between devices, middle(): return lax.ppermute(value, 'dp', [(1, 2), (2, 1)])  9.13 us
    ppermute x6, starting transfers between devices, shared(): beside = lambda value: lax.ppermute(value, 'seq', swap)  8.12 us
    ppermute x4, waiting for transfers between devices, hand_back(): got.append(lax.ppermute(sent, ('groups', 'dp', 'seq'), steps))  7.25 us
  transfers between devices with their start and end apart: 44, of which 12 were waited for; matrix products, arithmetic and copies ran while one was open for 7% of the time, Pallas kernels for 35%

profile of v3, /device:TPU:0, one launch (start us, length us, event | category | flops | bytes accessed | tf_op | source)
XLA Modules:
  0.0 243.6 jit_solution(6215689392157370916)
XLA Ops:
  0.0 5.2 %shard_map.37 = (bf16[192,3072]{1,0:T(8,128)(2,1)}, bf16[192,3072]{1,0:T(8,128)(2,1)}, bf16[1536,384]{1,0:T(8,128)(2,1)}) custom-call(bf16[1,384,6144]{2,1,0:T(8,128)(2,1)} %tokens_ref.2, f32[1,6144]{1,0:T(1,128)} %bitcast.35, bf16[6,1536,384]{2,1,0:T(8,128)(2,1)} %bitcast.23), custom_call_target="tpu_custom_call" | custom-call | flops 9437184 | bytes 4718592 | tf_op jit(solution)/shard_map/pallas_call | solution.py:147
  5.2 3.0 %collective-permute-start = (bf16[192,3072]{1,0:T(8,128)(2,1)}, bf16[192,3072]{1,0:T(8,128)(2,1)}, u32[]{:S(2)}, u32[]{:S(2)}) collective-permute-start(bf16[192,3072]{1,0:T(8,128)(2,1)} %get-tuple-element.124.refs_0_.refs_8_), channel_id=1, source_target_pairs={{0,2},{2,0},{1,3},{3,1},{4,6},{6,4},{5,7},{7,5},{8,10},{10,8},{9,1... | collective-permute-start | bytes 3538952 | tf_op jit(solution)/shard_map/ppermute | solution.py:502
  8.2 1.5 collective-permute-start.1
  9.7 1.6 collective-permute-start.2
  11.3 1.7 collective-permute-start.3
  13.0 2.9 %dynamic-slice_bitcast_fusion = (bf16[1536,384]{1,0:T(8,128)(2,1)}, bf16[1,1536,384]{2,1,0:T(8,128)(2,1)S(1)}) fusion(bf16[6,1536,384]{2,1,0:T(8,128)(2,1)} %bitcast.24, s32[]{:T(128)S(6)} %select_n.63, s32[]{:T(128)S(6)} %select_n.62), kind=kLoop, calls=%fused_computation.1 | loop fusion | bytes 4718600 | tf_op jit(solution)/shard_map/jit(dynamic_index_in_dim)/squeeze | solution.py:536
  15.9 1.2 copy.7
  17.1 0.9 copy-done.1
  18.0 1.1 broadcast_select_fusion.3
  19.1 0.6 pad_add_fusion.role_ref
  19.7 14.8 %collective-permute-done.refs_4_.refs_12_ = bf16[192,3072]{1,0:T(8,128)(2,1)} collective-permute-done((bf16[192,3072]{1,0:T(8,128)(2,1)}, bf16[192,3072]{1,0:T(8,128)(2,1)}, u32[]{:S(2)}, u32[]{:S(2)}) %collective-permute-start) | collective-permute-done | bytes 1179680 | tf_op jit(solution)/shard_map/ppermute | solution.py:502
  34.5 1.5 collective-permute-done.1.refs_0_.refs_8_
  36.3 1.7 collective-permute-start.7
  38.0 3.8 %collective-permute-start.4 = (bf16[192,3072]{1,0:T(8,128)(2,1)}, bf16[192,3072]{1,0:T(8,128)(2,1)}, u32[]{:S(2)}, u32[]{:S(2)}) collective-permute-start(bf16[192,3072]{1,0:T(8,128)(2,1)} %broadcast_select_fusion.3), channel_id=1, source_target_pairs={{0,4},{4,0},{8,12},{12,8},{1,5},{5,1},{9,13},{13,9},{2,6},{6,2},{1... | collective-permute-start | bytes 3538952 | tf_op jit(solution)/shard_map/ppermute | solution.py:496
  41.8 1.7 collective-permute-start.5
  43.4 2.5 %copy.8 = bf16[24,8,8,384]{3,1,2,0:T(8,128)(2,1)} copy(bf16[24,8,8,384]{3,1,0,2:T(8,128)(2,1)} %bitcast.21) | data formatting | bytes 2359296
  45.9 4.8 %shard_map.38 = (bf16[192,3072]{1,0:T(8,128)(2,1)}, bf16[192,3072]{1,0:T(8,128)(2,1)}) custom-call(bf16[1,384,6144]{2,1,0:T(8,128)(2,1)} %tokens_ref.2, f32[1,6144]{1,0:T(1,128)} %bitcast.36, bf16[6,1536,384]{2,1,0:T(8,128)(2,1)} %bitcast.25), custom_call_target="tpu_custom_call" | custom-call | flops 9437184 | bytes 4718592 | tf_op jit(solution)/shard_map/pallas_call | solution.py:147
  50.7 1.4 broadcast_select_fusion.2
  52.1 14.5 %collective-permute-done.4.refs_25_.refs_0_.refs_16_ = bf16[192,3072]{1,0:T(8,128)(2,1)} collective-permute-done((bf16[192,3072]{1,0:T(8,128)(2,1)}, bf16[192,3072]{1,0:T(8,128)(2,1)}, u32[]{:S(2)}, u32[]{:S(2)}) %collective-permute-start.4) | collective-permute-done | bytes 1179680 | tf_op jit(solution)/shard_map/ppermute | solution.py:496
  66.7 4.2 %collective-permute-start.10 = (bf16[192,3072]{1,0:T(8,128)(2,1)S(1)}, bf16[192,3072]{1,0:T(8,128)(2,1)S(1)}, u32[]{:S(2)}, u32[]{:S(2)}) collective-permute-start(bf16[192,3072]{1,0:T(8,128)(2,1)S(1)} %broadcast_select_fusion.2), channel_id=1, source_target_pairs={{0,4},{4,0},{8,12},{12,8},{1,5},{5,1},{9,13},{13,9},{2,6},{6,2},{1... | collective-permute-start | bytes 3538952 | tf_op jit(solution)/shard_map/ppermute | solution.py:496
  70.9 0.7 collective-permute-start.11
  71.6 1.6 collective-permute-start.12
  73.2 0.5 collective-permute-start.13
  73.7 1.2 broadcast_select_fusion.1
  74.9 22.5 %collective-permute-done.10.refs_28_.refs_1_.refs_17_ = bf16[192,3072]{1,0:T(8,128)(2,1)S(1)} collective-permute-done((bf16[192,3072]{1,0:T(8,128)(2,1)S(1)}, bf16[192,3072]{1,0:T(8,128)(2,1)S(1)}, u32[]{:S(2)}, u32[]{:S(2)}) %collective-permute-start.10) | collective-permute-done | bytes 1179680 | tf_op jit(solution)/shard_map/ppermute | solution.py:496
  97.5 2.5 %collective-permute-done.12.refs_4_.refs_12_ = bf16[192,3072]{1,0:T(8,128)(2,1)S(1)} collective-permute-done((bf16[192,3072]{1,0:T(8,128)(2,1)}, bf16[192,3072]{1,0:T(8,128)(2,1)S(1)}, u32[]{:S(2)}, u32[]{:S(2)}) %collective-permute-start.12) | collective-permute-done | bytes 1179680 | tf_op jit(solution)/shard_map/ppermute | solution.py:502
  99.9 1.3 collective-permute-done.13.refs_5_.refs_13_
  101.3 1.1 collective-permute-start.18
  102.4 0.5 collective-permute-start.19
  102.9 2.9 %collective-permute-start.16 = (bf16[1536,384]{1,0:T(8,128)(2,1)}, bf16[1536,384]{1,0:T(8,128)(2,1)}, u32[]{:S(2)}, u32[]{:S(2)}) collective-permute-start(bf16[1536,384]{1,0:T(8,128)(2,1)} %broadcast_select_fusion.1), channel_id=1, source_target_pairs={{0,4},{4,0},{8,12},{12,8},{1,5},{5,1},{9,13},{13,9},{2,6},{6,2},{1... | collective-permute-start | bytes 3538952 | tf_op jit(solution)/shard_map/ppermute | solution.py:496
  105.9 1.7 collective-permute-start.17
  107.5 1.0 copy-done.6
  108.6 2.8 %pad_maximum_fusion = bf16[384,3072]{1,0:T(8,128)(2,1)} fusion(bf16[192,3072]{1,0:T(8,128)(2,1)S(1)} %collective-permute-done.10.refs_28_.refs_1_.refs_17_, bf16[192,3072]{1,0:T(8,128)(2,1)} %collective-permute-done.4.refs_25_.refs_0_.refs_16_), kind=kLoop, calls=%fused_computation | loop fusion | flops 4718592 | bytes 4718592 | tf_op jit(solution)/shard_map/concatenate | solution.py:576
  111.4 2.5 %broadcast_select_fusion = bf16[1536,384]{1,0:T(8,128)(2,1)} fusion(bf16[1536,384]{1,0:T(8,128)(2,1)S(1)} %collective-permute-done.11.refs_14_.refs_22_, bf16[1536,384]{1,0:T(8,128)(2,1)} %get-tuple-element.210.refs_11_.refs_19_.refs_10_, pred[]{:T(512)S(6)} %or.3), kind=kLoop, calls=%fused_computation.2 | loop fusion | flops 589824 | bytes 3538945 | tf_op jit(solution)/shard_map/jit(_where)/select_n | solution.py:493
  113.8 14.5 %shard_map.39 = (bf16[384,128]{1,0:T(8,128)(2,1)}, bf16[384,128]{1,0:T(8,128)(2,1)}, f32[768,384]{1,0:T(8,128)}, f32[768,384]{1,0:T(8,128)}) custom-call(s32[2]{0:T(128)} %pad_add_fusion.role_ref, bf16[192,3072]{1,0:T(8,128)(2,1)} %get-tuple-element.124.refs_0_.refs_8_, bf16[192,3072]{1,0:T(8,128)(2,1)} %get-tuple-element.132.refs_1_.refs_9_, ...), custom_call_target="tpu_custom_call" | custom-call | flops 6341787648 | tf_op jit(solution)/shard_map/pallas_call | solution.py:406
  128.3 3.9 %collective-permute-done.16.refs_27_.refs_17_ = bf16[1536,384]{1,0:T(8,128)(2,1)} collective-permute-done((bf16[1536,384]{1,0:T(8,128)(2,1)}, bf16[1536,384]{1,0:T(8,128)(2,1)}, u32[]{:S(2)}, u32[]{:S(2)}) %collective-permute-start.16) | collective-permute-done | bytes 1179680 | tf_op jit(solution)/shard_map/ppermute | solution.py:496
  132.4 1.0 collective-permute-start.24
  133.4 1.5 collective-permute-start.25
  134.9 3.6 %collective-permute-start.22 = (bf16[1536,384]{1,0:T(8,128)(2,1)}, bf16[1536,384]{1,0:T(8,128)(2,1)}, u32[]{:S(2)}, u32[]{:S(2)}) collective-permute-start(bf16[1536,384]{1,0:T(8,128)(2,1)} %broadcast_select_fusion), channel_id=1, source_target_pairs={{0,4},{4,0},{8,12},{12,8},{1,5},{5,1},{9,13},{13,9},{2,6},{6,2},{1... | collective-permute-start | bytes 3538952 | tf_op jit(solution)/shard_map/ppermute | solution.py:496
  138.5 1.7 collective-permute-start.23
  140.2 20.0 %shard_map.40 = (bf16[384,128]{1,0:T(8,128)(2,1)}, bf16[384,128]{1,0:T(8,128)(2,1)}, f32[768,384]{1,0:T(8,128)}, f32[768,384]{1,0:T(8,128)}, f32[768,384]{1,0:T(8,128)}, /*index=5*/f32[768,384]{1,0:T(8,128)}) custom-call(s32[2]{0:T(128)} %pad_add_fusion.role_ref, bf16[192,3072]{1,0:T(8,128)(2,1)} %collective-permute-done.1.refs_0_.refs_8_, ...), custom_call_target="tpu_custom_call" | custom-call | flops 9965666304 | tf_op jit(solution)/shard_map/pallas_call | solution.py:406
  160.2 4.6 %collective-permute-done.22.refs_18_.refs_8_ = bf16[1536,384]{1,0:T(8,128)(2,1)} collective-permute-done((bf16[1536,384]{1,0:T(8,128)(2,1)}, bf16[1536,384]{1,0:T(8,128)(2,1)}, u32[]{:S(2)}, u32[]{:S(2)}) %collective-permute-start.22) | collective-permute-done | bytes 1179680 | tf_op jit(solution)/shard_map/ppermute | solution.py:496
  164.9 0.6 collective-permute-start.32
  165.5 3.6 %collective-permute-start.29 = (bf16[1536,384]{1,0:T(8,128)(2,1)}, bf16[1536,384]{1,0:T(8,128)(2,1)}, u32[]{:S(2)}, u32[]{:S(2)}) collective-permute-start(bf16[1536,384]{1,0:T(8,128)(2,1)} %collective-permute-done.23.refs_16_), channel_id=1, source_target_pairs={{0,4},{4,0},{8,12},{12,8},{1,5},{5,1},{9,13},{13,9},{2,6},{6,2},{1... | collective-permute-start | bytes 3538952 | tf_op jit(solution)/shard_map/ppermute | solution.py:496
  169.1 1.7 collective-permute-start.30
  170.8 1.1 collective-permute-start.31
  171.9 13.1 %shard_map.41 = (bf16[384,128]{1,0:T(8,128)(2,1)}, bf16[384,128]{1,0:T(8,128)(2,1)}, f32[768,384]{1,0:T(8,128)}, bf16[384,128]{1,0:T(8,128)(2,1)}, bf16[384,128]{1,0:T(8,128)(2,1)}, /*index=5*/f32[768,384]{1,0:T(8,128)}) custom-call(s32[2]{0:T(128)} %pad_add_fusion.role_ref, bf16[192,3072]{1,0:T(8,128)(2,1)} %get-tuple-element.124.refs_0_.refs_8_, ...), custom_call_target="tpu_custom_call" | custom-call | flops 3623878656 | tf_op jit(solution)/shard_map/pallas_call | solution.py:406
  185.0 8.8 %shard_map.42.refs_28_ = f32[768,384]{1,0:T(8,128)} custom-call(s32[2]{0:T(128)} %pad_add_fusion.role_ref, bf16[192,3072]{1,0:T(8,128)(2,1)} %collective-permute-done.4.refs_25_.refs_0_.refs_16_, bf16[192,3072]{1,0:T(8,128)(2,1)} %copy-done.2, bf16[384,3072]{1,0:T(8,128)(2,1)} %collective-permute-done.26.refs_2_.refs_3_.refs_18_.refs_19_, ...), custom_call_target="tpu_custom_call" | custom-call | flops 2717908992 | tf_op jit(solution)/shard_map/pallas_call | solution.py:406
  193.8 1.9 collective-permute-done.29.refs_25_
  195.7 3.1 %collective-permute-done.31.refs_4_ = bf16[192,3072]{1,0:T(8,128)(2,1)} collective-permute-done((bf16[192,3072]{1,0:T(8,128)(2,1)}, bf16[192,3072]{1,0:T(8,128)(2,1)}, u32[]{:S(2)}, u32[]{:S(2)}) %collective-permute-start.31) | collective-permute-done | bytes 1179680 | tf_op jit(solution)/shard_map/ppermute | solution.py:502
  199.5 12.9 %shard_map.43 = (bf16[384,384]{1,0:T(8,128)(2,1)}, bf16[384,384]{1,0:T(8,128)(2,1)}, bf16[384,384]{1,0:T(8,128)(2,1)}, bf16[384,384]{1,0:T(8,128)(2,1)}, bf16[38...) custom-call(s32[2]{0:T(128)} %pad_add_fusion.role_ref, bf16[192,3072]{1,0:T(8,128)(2,1)} %get-tuple-element.124.refs_0_.refs_8_, ...), custom_call_target="tpu_custom_call" | custom-call | flops 2717908992 | tf_op jit(solution)/shard_map/pallas_call | solution.py:406
  212.3 1.1 collective-permute-start.34
  213.5 1.5 collective-permute-start.35
  215.0 0.9 collective-permute-start.36
  215.9 1.3 collective-permute-start.37
  217.2 1.6 collective-permute-start.38
  218.8 10.2 %shard_map.44 = (bf16[384,128]{1,0:T(8,128)(2,1)}, bf16[384,128]{1,0:T(8,128)(2,1)}) custom-call(s32[2]{0:T(128)} %pad_add_fusion.role_ref, bf16[192,3072]{1,0:T(8,128)(2,1)} %collective-permute-done.19.refs_0_, bf16[192,3072]{1,0:T(8,128)(2,1)} %collective-permute-done.25.refs_1_, bf16[192,3072]{1,0:T(8,128)(2,1)} %collective-permute-done.33.refs_2_, ...), custom_call_target="tpu_custom_call" | custom-call | flops 3623878656 | tf_op jit(solution)/shard_map/pallas_call | solution.py:406
  229.0 1.3 collective-permute-start.42
  230.3 1.3 collective-permute-start.43
  231.7 0.7 stack.34.place_ref
  232.4 5.9 %collective-permute-done.42.refs_6_ = bf16[384,128]{1,0:T(8,128)(2,1)S(1)} collective-permute-done((bf16[384,128]{1,0:T(8,128)(2,1)}, bf16[384,128]{1,0:T(8,128)(2,1)S(1)}, u32[]{:S(2)}, u32[]{:S(2)}) %collective-permute-start.42) | collective-permute-done | bytes 98336 | tf_op jit(solution)/shard_map/ppermute | solution.py:660
  238.3 1.4 collective-permute-done.43.refs_7_
  239.7 0.6 copy-done.15
  240.3 3.1 %shard_map.45 = bf16[384,1536]{1,0:T(8,128)(2,1)} custom-call(s32[5]{0:T(128)} %stack.34.place_ref, bf16[384,384]{1,0:T(8,128)(2,1)} %get-tuple-element.225.refs_0_, bf16[384,384]{1,0:T(8,128)(2,1)} %copy-done.10, bf16[384,384]{1,0:T(8,128)(2,1)} %copy-done.11, bf16[384,384]{1,0:T(8,128)(2,1)} %collective-permute-done.36.refs_3_, ...), custom_call_target="tpu_custom_call" | custom-call | bytes 2359296 | tf_op jit(solution)/shard_map/pallas_call | solution.py:467
  (75 shorter events, 1.4 us)
Async XLA Ops:
  5.2 29.3 %collective-permute-start = (bf16[192,3072]{1,0:T(8,128)(2,1)}, bf16[192,3072]{1,0:T(8,128)(2,1)}, u32[]{:S(2)}, u32[]{:S(2)}) collective-permute-start(bf16[192,3072]{1,0:T(8,128)(2,1)} %get-tuple-element.124.refs_0_.refs_8_), channel_id=1, source_target_pairs={{0,2},{2,0},{1,3},{3,1},{4,6},{6,4},{5,7},{7,5},{8,10},{10,8},{9,1... | collective-permute-start | bytes 3538952 | tf_op jit(solution)/shard_map/ppermute | solution.py:502
  8.2 27.7 %collective-permute-start.1 = (bf16[192,3072]{1,0:T(8,128)(2,1)}, bf16[192,3072]{1,0:T(8,128)(2,1)}, u32[]{:S(2)}, u32[]{:S(2)}) collective-permute-start(bf16[192,3072]{1,0:T(8,128)(2,1)} %get-tuple-element.124.refs_0_.refs_8_), channel_id=1, source_target_pairs={{0,16},{16,0},{1,17},{17,1},{2,18},{18,2},{3,19},{19,3},{4,20},{20... | collective-permute-start | bytes 3538952 | tf_op jit(solution)/shard_map/ppermute | solution.py:503
  9.7 28.3 %collective-permute-start.2 = (bf16[1536,384]{1,0:T(8,128)(2,1)}, bf16[1536,384]{1,0:T(8,128)(2,1)}, u32[]{:S(2)}, u32[]{:S(2)}) collective-permute-start(bf16[1536,384]{1,0:T(8,128)(2,1)} %get-tuple-element.128.refs_8_.refs_10_.refs_16_.refs_18_), channel_id=1, source_target_pairs={{0,4},{4,0},{8,12},{12,8},{1,5},{5,1},{9,13},{13,9},{2,6},{6,2},{1... | collective-permute-start | bytes 3538952 | tf_op jit(solution)/shard_map/ppermute | solution.py:496
  11.3 26.7 %collective-permute-start.3 = (bf16[1536,384]{1,0:T(8,128)(2,1)}, bf16[1536,384]{1,0:T(8,128)(2,1)}, u32[]{:S(2)}, u32[]{:S(2)}) collective-permute-start(bf16[1536,384]{1,0:T(8,128)(2,1)} %get-tuple-element.128.refs_8_.refs_10_.refs_16_.refs_18_), channel_id=1, source_target_pairs={{4,8},{8,4},{5,9},{9,5},{6,10},{10,6},{7,11},{11,7},{20,24},{24,20... | collective-permute-start | bytes 3538952 | tf_op jit(solution)/shard_map/ppermute | solution.py:499
  15.9 57.8 %copy-start = (bf16[1,1536,384]{2,1,0:T(8,128)(2,1)}, bf16[1,1536,384]{2,1,0:T(8,128)(2,1)S(1)}, u32[]{:S(2)}) copy-start(bf16[1,1536,384]{2,1,0:T(8,128)(2,1)S(1)} %get-tuple-element.238) | copy-start | bytes 3538948
  15.9 2.1 copy-start.1
  35.9 7.5 %collective-permute-start.8 = (bf16[192,3072]{1,0:T(8,128)(2,1)}, bf16[192,3072]{1,0:T(8,128)(2,1)}, u32[]{:S(2)}, u32[]{:S(2)}) collective-permute-start(bf16[192,3072]{1,0:T(8,128)(2,1)} %collective-permute-done.refs_4_.refs_12_), channel_id=1, source_target_pairs={{0,1},{1,0},{2,3},{3,2},{4,5},{5,4},{6,7},{7,6},{8,9},{9,8},{10,11... | collective-permute-start | bytes 3538952 | tf_op jit(solution)/shard_map/ppermute | solution.py:510
  35.9 30.6 %collective-permute-start.6 = (bf16[192,3072]{1,0:T(8,128)(2,1)}, bf16[192,3072]{1,0:T(8,128)(2,1)}, u32[]{:S(2)}, u32[]{:S(2)}) collective-permute-start(bf16[192,3072]{1,0:T(8,128)(2,1)} %get-tuple-element.132.refs_1_.refs_9_), channel_id=1, source_target_pairs={{0,2},{2,0},{1,3},{3,1},{4,6},{6,4},{5,7},{7,5},{8,10},{10,8},{9,1... | collective-permute-start | bytes 3538952 | tf_op jit(solution)/shard_map/ppermute | solution.py:502
  36.3 30.3 %collective-permute-start.7 = (bf16[192,3072]{1,0:T(8,128)(2,1)}, bf16[192,3072]{1,0:T(8,128)(2,1)}, u32[]{:S(2)}, u32[]{:S(2)}) collective-permute-start(bf16[192,3072]{1,0:T(8,128)(2,1)} %get-tuple-element.132.refs_1_.refs_9_), channel_id=1, source_target_pairs={{0,16},{16,0},{1,17},{17,1},{2,18},{18,2},{3,19},{19,3},{4,20},{20... | collective-permute-start | bytes 3538952 | tf_op jit(solution)/shard_map/ppermute | solution.py:503
  38.0 28.6 %collective-permute-start.4 = (bf16[192,3072]{1,0:T(8,128)(2,1)}, bf16[192,3072]{1,0:T(8,128)(2,1)}, u32[]{:S(2)}, u32[]{:S(2)}) collective-permute-start(bf16[192,3072]{1,0:T(8,128)(2,1)} %broadcast_select_fusion.3), channel_id=1, source_target_pairs={{0,4},{4,0},{8,12},{12,8},{1,5},{5,1},{9,13},{13,9},{2,6},{6,2},{1... | collective-permute-start | bytes 3538952 | tf_op jit(solution)/shard_map/ppermute | solution.py:496
  41.8 24.8 %collective-permute-start.5 = (bf16[1536,384]{1,0:T(8,128)(2,1)}, bf16[1536,384]{1,0:T(8,128)(2,1)}, u32[]{:S(2)}, u32[]{:S(2)}) collective-permute-start(bf16[1536,384]{1,0:T(8,128)(2,1)} %collective-permute-done.2.refs_15_.refs_16_.refs_23_.refs_26_), channel_id=1, source_target_pairs={{4,8},{8,4},{5,9},{9,5},{6,10},{10,6},{7,11},{11,7},{20,24},{24,20... | collective-permute-start | bytes 3538952 | tf_op jit(solution)/shard_map/ppermute | solution.py:499
  43.4 23.1 %collective-permute-start.9 = (bf16[192,3072]{1,0:T(8,128)(2,1)}, bf16[192,3072]{1,0:T(8,128)(2,1)}, u32[]{:S(2)}, u32[]{:S(2)}) collective-permute-start(bf16[192,3072]{1,0:T(8,128)(2,1)} %collective-permute-done.1.refs_0_.refs_8_), channel_id=1, source_target_pairs={{0,1},{1,0},{2,3},{3,2},{4,5},{5,4},{6,7},{7,6},{8,9},{9,8},{10,11... | collective-permute-start | bytes 3538952 | tf_op jit(solution)/shard_map/ppermute | solution.py:510
  66.6 7.1 %collective-permute-start.14 = (bf16[192,3072]{1,0:T(8,128)(2,1)}, bf16[192,3072]{1,0:T(8,128)(2,1)}, u32[]{:S(2)}, u32[]{:S(2)}) collective-permute-start(bf16[192,3072]{1,0:T(8,128)(2,1)} %collective-permute-done.7.refs_1_.refs_9_), channel_id=1, source_target_pairs={{0,1},{1,0},{2,3},{3,2},{4,5},{5,4},{6,7},{7,6},{8,9},{9,8},{10,11... | collective-permute-start | bytes 3538952 | tf_op jit(solution)/shard_map/ppermute | solution.py:510
  66.7 30.8 %collective-permute-start.10 = (bf16[192,3072]{1,0:T(8,128)(2,1)S(1)}, bf16[192,3072]{1,0:T(8,128)(2,1)S(1)}, u32[]{:S(2)}, u32[]{:S(2)}) collective-permute-start(bf16[192,3072]{1,0:T(8,128)(2,1)S(1)} %broadcast_select_fusion.2), channel_id=1, source_target_pairs={{0,4},{4,0},{8,12},{12,8},{1,5},{5,1},{9,13},{13,9},{2,6},{6,2},{1... | collective-permute-start | bytes 3538952 | tf_op jit(solution)/shard_map/ppermute | solution.py:496
  70.9 26.6 %collective-permute-start.11 = (bf16[1536,384]{1,0:T(8,128)(2,1)S(1)}, bf16[1536,384]{1,0:T(8,128)(2,1)S(1)}, u32[]{:S(2)}, u32[]{:S(2)}) collective-permute-start(bf16[1536,384]{1,0:T(8,128)(2,1)S(1)} %bitcast.27), channel_id=1, source_target_pairs={{4,8},{8,4},{5,9},{9,5},{6,10},{10,6},{7,11},{11,7},{20,24},{24,20... | collective-permute-start | bytes 3538952 | tf_op jit(solution)/shard_map/ppermute | solution.py:499
  71.6 28.3 %collective-permute-start.12 = (bf16[192,3072]{1,0:T(8,128)(2,1)}, bf16[192,3072]{1,0:T(8,128)(2,1)S(1)}, u32[]{:S(2)}, u32[]{:S(2)}) collective-permute-start(bf16[192,3072]{1,0:T(8,128)(2,1)} %collective-permute-done.1.refs_0_.refs_8_), channel_id=1, source_target_pairs={{0,2},{2,0},{1,3},{3,1},{4,6},{6,4},{5,7},{7,5},{8,10},{10,8},{9,1... | collective-permute-start | bytes 3538952 | tf_op jit(solution)/shard_map/ppermute | solution.py:502
  73.2 28.1 %collective-permute-start.13 = (bf16[192,3072]{1,0:T(8,128)(2,1)}, bf16[192,3072]{1,0:T(8,128)(2,1)}, u32[]{:S(2)}, u32[]{:S(2)}) collective-permute-start(bf16[192,3072]{1,0:T(8,128)(2,1)} %collective-permute-done.6.refs_5_.refs_13_), channel_id=1, source_target_pairs={{0,16},{16,0},{1,17},{17,1},{2,18},{18,2},{3,19},{19,3},{4,20},{20... | collective-permute-start | bytes 3538952 | tf_op jit(solution)/shard_map/ppermute | solution.py:503
  73.7 27.6 %collective-permute-start.15 = (bf16[192,3072]{1,0:T(8,128)(2,1)}, bf16[192,3072]{1,0:T(8,128)(2,1)S(1)}, u32[]{:S(2)}, u32[]{:S(2)}) collective-permute-start(bf16[192,3072]{1,0:T(8,128)(2,1)} %collective-permute-done.6.refs_5_.refs_13_), channel_id=1, source_target_pairs={{0,1},{1,0},{2,3},{3,2},{4,5},{5,4},{6,7},{7,6},{8,9},{9,8},{10,11... | collective-permute-start | bytes 3538952 | tf_op jit(solution)/shard_map/ppermute | solution.py:510
  97.5 13.9 %copy-start.2 = (bf16[192,3072]{1,0:T(8,128)(2,1)}, bf16[192,3072]{1,0:T(8,128)(2,1)S(1)}, u32[]{:S(2)}) copy-start(bf16[192,3072]{1,0:T(8,128)(2,1)S(1)} %collective-permute-done.10.refs_28_.refs_1_.refs_17_) | copy-start | bytes 3538948
  97.5 13.9 %copy-start.8 = (bf16[1536,384]{1,0:T(8,128)(2,1)}, bf16[1536,384]{1,0:T(8,128)(2,1)S(1)}, u32[]{:S(2)}) copy-start(bf16[1536,384]{1,0:T(8,128)(2,1)S(1)} %collective-permute-done.11.refs_14_.refs_22_) | copy-start | bytes 3538948
  99.9 1.3 copy-start.4
  101.3 6.3 %copy-start.5 = (bf16[192,3072]{1,0:T(8,128)(2,1)}, bf16[192,3072]{1,0:T(8,128)(2,1)S(1)}, u32[]{:S(2)}) copy-start(bf16[192,3072]{1,0:T(8,128)(2,1)S(1)} %collective-permute-done.15.refs_7_.refs_15_) | copy-start | bytes 3538948
  101.3 6.3 %collective-permute-start.20 = (bf16[192,3072]{1,0:T(8,128)(2,1)S(1)}, bf16[192,3072]{1,0:T(8,128)(2,1)S(1)}, u32[]{:S(2)}, u32[]{:S(2)}) collective-permute-start(bf16[192,3072]{1,0:T(8,128)(2,1)S(1)} %collective-permute-done.12.refs_4_.refs_12_), channel_id=1, source_target_pairs={{0,1},{1,0},{2,3},{3,2},{4,5},{5,4},{6,7},{7,6},{8,9},{9,8},{10,11... | collective-permute-start | bytes 3538952 | tf_op jit(solution)/shard_map/ppermute | solution.py:510
  101.3 30.9 %collective-permute-start.18 = (bf16[192,3072]{1,0:T(8,128)(2,1)}, bf16[192,3072]{1,0:T(8,128)(2,1)}, u32[]{:S(2)}, u32[]{:S(2)}) collective-permute-start(bf16[192,3072]{1,0:T(8,128)(2,1)} %collective-permute-done.4.refs_25_.refs_0_.refs_16_), channel_id=1, source_target_pairs={{0,2},{2,0},{1,3},{3,1},{4,6},{6,4},{5,7},{7,5},{8,10},{10,8},{9,1... | collective-permute-start | bytes 3538952 | tf_op jit(solution)/shard_map/ppermute | solution.py:502
  102.4 29.8 %collective-permute-start.19 = (bf16[192,3072]{1,0:T(8,128)(2,1)}, bf16[192,3072]{1,0:T(8,128)(2,1)}, u32[]{:S(2)}, u32[]{:S(2)}) collective-permute-start(bf16[192,3072]{1,0:T(8,128)(2,1)} %collective-permute-done.4.refs_25_.refs_0_.refs_16_), channel_id=1, source_target_pairs={{0,16},{16,0},{1,17},{17,1},{2,18},{18,2},{3,19},{19,3},{4,20},{20... | collective-permute-start | bytes 3538952 | tf_op jit(solution)/shard_map/ppermute | solution.py:503
  102.9 29.3 %collective-permute-start.16 = (bf16[1536,384]{1,0:T(8,128)(2,1)}, bf16[1536,384]{1,0:T(8,128)(2,1)}, u32[]{:S(2)}, u32[]{:S(2)}) collective-permute-start(bf16[1536,384]{1,0:T(8,128)(2,1)} %broadcast_select_fusion.1), channel_id=1, source_target_pairs={{0,4},{4,0},{8,12},{12,8},{1,5},{5,1},{9,13},{13,9},{2,6},{6,2},{1... | collective-permute-start | bytes 3538952 | tf_op jit(solution)/shard_map/ppermute | solution.py:496
  105.9 26.4 %collective-permute-start.17 = (bf16[1536,384]{1,0:T(8,128)(2,1)}, bf16[1536,384]{1,0:T(8,128)(2,1)}, u32[]{:S(2)}, u32[]{:S(2)}) collective-permute-start(bf16[1536,384]{1,0:T(8,128)(2,1)} %get-tuple-element.210.refs_11_.refs_19_.refs_10_), channel_id=1, source_target_pairs={{4,8},{8,4},{5,9},{9,5},{6,10},{10,6},{7,11},{11,7},{20,24},{24,20... | collective-permute-start | bytes 3538952 | tf_op jit(solution)/shard_map/ppermute | solution.py:499
  107.5 1.0 copy-start.6
  108.6 23.7 %collective-permute-start.21 = (bf16[192,3072]{1,0:T(8,128)(2,1)}, bf16[192,3072]{1,0:T(8,128)(2,1)}, u32[]{:S(2)}, u32[]{:S(2)}) collective-permute-start(bf16[192,3072]{1,0:T(8,128)(2,1)} %collective-permute-done.13.refs_5_.refs_13_), channel_id=1, source_target_pairs={{0,1},{1,0},{2,3},{3,2},{4,5},{5,4},{6,7},{7,6},{8,9},{9,8},{10,11... | collective-permute-start | bytes 3538952 | tf_op jit(solution)/shard_map/ppermute | solution.py:510
  113.8 18.5 %copy-start.3 = (bf16[192,3072]{1,0:T(8,128)(2,1)S(1)}, bf16[192,3072]{1,0:T(8,128)(2,1)}, u32[]{:S(2)}) copy-start(bf16[192,3072]{1,0:T(8,128)(2,1)} %copy-done.2) | copy-start | bytes 3538948
  132.3 8.0 %collective-permute-start.26 = (bf16[384,3072]{1,0:T(8,128)(2,1)}, bf16[384,3072]{1,0:T(8,128)(2,1)}, u32[]{:S(2)}, u32[]{:S(2)}) collective-permute-start(bf16[384,3072]{1,0:T(8,128)(2,1)} %pad_maximum_fusion), channel_id=1, source_target_pairs={{0,1},{1,0},{2,3},{3,2},{4,5},{5,4},{6,7},{7,6},{8,9},{9,8},{10,11... | collective-permute-start | bytes 7077896 | tf_op jit(solution)/shard_map/ppermute | solution.py:510
  132.4 32.5 %collective-permute-start.24 = (bf16[192,3072]{1,0:T(8,128)(2,1)S(1)}, bf16[192,3072]{1,0:T(8,128)(2,1)}, u32[]{:S(2)}, u32[]{:S(2)}) collective-permute-start(bf16[192,3072]{1,0:T(8,128)(2,1)S(1)} %copy-done.3), channel_id=1, source_target_pairs={{0,2},{2,0},{1,3},{3,1},{4,6},{6,4},{5,7},{7,5},{8,10},{10,8},{9,1... | collective-permute-start | bytes 3538952 | tf_op jit(solution)/shard_map/ppermute | solution.py:502
  133.4 31.5 %collective-permute-start.25 = (bf16[192,3072]{1,0:T(8,128)(2,1)S(1)}, bf16[192,3072]{1,0:T(8,128)(2,1)}, u32[]{:S(2)}, u32[]{:S(2)}) collective-permute-start(bf16[192,3072]{1,0:T(8,128)(2,1)S(1)} %copy-done.3), channel_id=1, source_target_pairs={{0,16},{16,0},{1,17},{17,1},{2,18},{18,2},{3,19},{19,3},{4,20},{20... | collective-permute-start | bytes 3538952 | tf_op jit(solution)/shard_map/ppermute | solution.py:503
  134.9 29.9 %collective-permute-start.22 = (bf16[1536,384]{1,0:T(8,128)(2,1)}, bf16[1536,384]{1,0:T(8,128)(2,1)}, u32[]{:S(2)}, u32[]{:S(2)}) collective-permute-start(bf16[1536,384]{1,0:T(8,128)(2,1)} %broadcast_select_fusion), channel_id=1, source_target_pairs={{0,4},{4,0},{8,12},{12,8},{1,5},{5,1},{9,13},{13,9},{2,6},{6,2},{1... | collective-permute-start | bytes 3538952 | tf_op jit(solution)/shard_map/ppermute | solution.py:496
  138.5 26.3 %collective-permute-start.23 = (bf16[1536,384]{1,0:T(8,128)(2,1)}, bf16[1536,384]{1,0:T(8,128)(2,1)}, u32[]{:S(2)}, u32[]{:S(2)}) collective-permute-start(bf16[1536,384]{1,0:T(8,128)(2,1)} %collective-permute-done.16.refs_27_.refs_17_), channel_id=1, source_target_pairs={{4,8},{8,4},{5,9},{9,5},{6,10},{10,6},{7,11},{11,7},{20,24},{24,20... | collective-permute-start | bytes 3538952 | tf_op jit(solution)/shard_map/ppermute | solution.py:499
  140.2 24.6 %collective-permute-start.27 = (bf16[192,3072]{1,0:T(8,128)(2,1)}, bf16[192,3072]{1,0:T(8,128)(2,1)}, u32[]{:S(2)}, u32[]{:S(2)}) collective-permute-start(bf16[192,3072]{1,0:T(8,128)(2,1)} %collective-permute-done.18.refs_4_.refs_20_), channel_id=1, source_target_pairs={{0,1},{1,0},{2,3},{3,2},{4,5},{5,4},{6,7},{7,6},{8,9},{9,8},{10,11... | collective-permute-start | bytes 3538952 | tf_op jit(solution)/shard_map/ppermute | solution.py:510
  164.9 7.0 %collective-permute-start.28 = (bf16[192,3072]{1,0:T(8,128)(2,1)}, bf16[192,3072]{1,0:T(8,128)(2,1)S(1)}, u32[]{:S(2)}, u32[]{:S(2)}) collective-permute-start(bf16[192,3072]{1,0:T(8,128)(2,1)} %collective-permute-done.24.refs_5_.refs_21_), channel_id=1, source_target_pairs={{0,1},{1,0},{2,3},{3,2},{4,5},{5,4},{6,7},{7,6},{8,9},{9,8},{10,11... | collective-permute-start | bytes 3538952 | tf_op jit(solution)/shard_map/ppermute | solution.py:510
  164.9 34.0 %collective-permute-start.32 = (bf16[192,3072]{1,0:T(8,128)(2,1)}, bf16[192,3072]{1,0:T(8,128)(2,1)}, u32[]{:S(2)}, u32[]{:S(2)}) collective-permute-start(bf16[192,3072]{1,0:T(8,128)(2,1)} %collective-permute-done.24.refs_5_.refs_21_), channel_id=1, source_target_pairs={{0,16},{16,0},{1,17},{17,1},{2,18},{18,2},{3,19},{19,3},{4,20},{20... | collective-permute-start | bytes 3538952 | tf_op jit(solution)/shard_map/ppermute | solution.py:503
  165.5 30.2 %collective-permute-start.29 = (bf16[1536,384]{1,0:T(8,128)(2,1)}, bf16[1536,384]{1,0:T(8,128)(2,1)}, u32[]{:S(2)}, u32[]{:S(2)}) collective-permute-start(bf16[1536,384]{1,0:T(8,128)(2,1)} %collective-permute-done.23.refs_16_), channel_id=1, source_target_pairs={{0,4},{4,0},{8,12},{12,8},{1,5},{5,1},{9,13},{13,9},{2,6},{6,2},{1... | collective-permute-start | bytes 3538952 | tf_op jit(solution)/shard_map/ppermute | solution.py:496
  169.1 26.6 %collective-permute-start.30 = (bf16[1536,384]{1,0:T(8,128)(2,1)}, bf16[1536,384]{1,0:T(8,128)(2,1)}, u32[]{:S(2)}, u32[]{:S(2)}) collective-permute-start(bf16[1536,384]{1,0:T(8,128)(2,1)} %collective-permute-done.22.refs_18_.refs_8_), channel_id=1, source_target_pairs={{4,8},{8,4},{5,9},{9,5},{6,10},{10,6},{7,11},{11,7},{20,24},{24,20... | collective-permute-start | bytes 3538952 | tf_op jit(solution)/shard_map/ppermute | solution.py:499
  170.8 28.1 %collective-permute-start.31 = (bf16[192,3072]{1,0:T(8,128)(2,1)}, bf16[192,3072]{1,0:T(8,128)(2,1)}, u32[]{:S(2)}, u32[]{:S(2)}) collective-permute-start(bf16[192,3072]{1,0:T(8,128)(2,1)} %collective-permute-done.19.refs_0_), channel_id=1, source_target_pairs={{0,2},{2,0},{1,3},{3,1},{4,6},{6,4},{5,7},{7,5},{8,10},{10,8},{9,1... | collective-permute-start | bytes 3538952 | tf_op jit(solution)/shard_map/ppermute | solution.py:502
  171.9 13.1 %copy-start.7 = (bf16[192,3072]{1,0:T(8,128)(2,1)}, bf16[192,3072]{1,0:T(8,128)(2,1)S(1)}, u32[]{:S(2)}) copy-start(bf16[192,3072]{1,0:T(8,128)(2,1)S(1)} %collective-permute-done.28.refs_7_.refs_23_) | copy-start | bytes 3538948
  171.9 27.0 %collective-permute-start.33 = (bf16[192,3072]{1,0:T(8,128)(2,1)}, bf16[192,3072]{1,0:T(8,128)(2,1)}, u32[]{:S(2)}, u32[]{:S(2)}) collective-permute-start(bf16[192,3072]{1,0:T(8,128)(2,1)} %collective-permute-done.19.refs_0_), channel_id=1, source_target_pairs={{0,1},{1,0},{2,3},{3,2},{4,5},{5,4},{6,7},{7,6},{8,9},{9,8},{10,11... | collective-permute-start | bytes 3538952 | tf_op jit(solution)/shard_map/ppermute | solution.py:510
  198.9 16.1 %collective-permute-start.39 = (bf16[192,3072]{1,0:T(8,128)(2,1)}, bf16[192,3072]{1,0:T(8,128)(2,1)S(1)}, u32[]{:S(2)}, u32[]{:S(2)}) collective-permute-start(bf16[192,3072]{1,0:T(8,128)(2,1)} %collective-permute-done.25.refs_1_), channel_id=1, source_target_pairs={{0,1},{1,0},{2,3},{3,2},{4,5},{5,4},{6,7},{7,6},{8,9},{9,8},{10,11... | collective-permute-start | bytes 3538952 | tf_op jit(solution)/shard_map/ppermute | solution.py:629
  198.9 17.0 %collective-permute-start.40 = (bf16[192,3072]{1,0:T(8,128)(2,1)}, bf16[192,3072]{1,0:T(8,128)(2,1)}, u32[]{:S(2)}, u32[]{:S(2)}) collective-permute-start(bf16[192,3072]{1,0:T(8,128)(2,1)} %collective-permute-done.31.refs_4_), channel_id=1, source_target_pairs={{0,1},{1,0},{2,3},{3,2},{4,5},{5,4},{6,7},{7,6},{8,9},{9,8},{10,11... | collective-permute-start | bytes 3538952 | tf_op jit(solution)/shard_map/ppermute | solution.py:629
  199.4 17.8 %collective-permute-start.41 = (bf16[192,3072]{1,0:T(8,128)(2,1)}, bf16[192,3072]{1,0:T(8,128)(2,1)}, u32[]{:S(2)}, u32[]{:S(2)}) collective-permute-start(bf16[192,3072]{1,0:T(8,128)(2,1)} %collective-permute-done.32.refs_5_), channel_id=1, source_target_pairs={{0,1},{1,0},{2,3},{3,2},{4,5},{5,4},{6,7},{7,6},{8,9},{9,8},{10,11... | collective-permute-start | bytes 3538952 | tf_op jit(solution)/shard_map/ppermute | solution.py:629
  212.3 20.0 %collective-permute-start.34 = (bf16[384,384]{1,0:T(8,128)(2,1)}, bf16[384,384]{1,0:T(8,128)(2,1)S(1)}, u32[]{:S(2)}, u32[]{:S(2)}) collective-permute-start(bf16[384,384]{1,0:T(8,128)(2,1)} %get-tuple-element.226), channel_id=1, source_target_pairs={{0,2},{2,0},{16,18},{18,16},{1,3},{3,1},{17,19},{19,17},{4,6},{6,4... | collective-permute-start | bytes 884744 | tf_op jit(solution)/shard_map/ppermute | solution.py:525
  213.5 18.9 %collective-permute-start.35 = (bf16[384,384]{1,0:T(8,128)(2,1)}, bf16[384,384]{1,0:T(8,128)(2,1)S(1)}, u32[]{:S(2)}, u32[]{:S(2)}) collective-permute-start(bf16[384,384]{1,0:T(8,128)(2,1)} %get-tuple-element.227), channel_id=1, source_target_pairs={{0,16},{2,18},{16,0},{18,2},{1,17},{3,19},{17,1},{19,3},{4,20},{6,... | collective-permute-start | bytes 884744 | tf_op jit(solution)/shard_map/ppermute | solution.py:525
  215.0 3.8 %copy-start.9 = (bf16[192,3072]{1,0:T(8,128)(2,1)}, bf16[192,3072]{1,0:T(8,128)(2,1)S(1)}, u32[]{:S(2)}) copy-start(bf16[192,3072]{1,0:T(8,128)(2,1)S(1)} %collective-permute-done.39.refs_3_) | copy-start | bytes 3538948
  215.0 17.4 %collective-permute-start.36 = (bf16[384,384]{1,0:T(8,128)(2,1)}, bf16[384,384]{1,0:T(8,128)(2,1)}, u32[]{:S(2)}, u32[]{:S(2)}) collective-permute-start(bf16[384,384]{1,0:T(8,128)(2,1)} %get-tuple-element.228), channel_id=1, source_target_pairs={{0,18},{2,16},{16,2},{18,0},{1,19},{3,17},{17,3},{19,1},{4,22},{6,... | collective-permute-start | bytes 884744 | tf_op jit(solution)/shard_map/ppermute | solution.py:525
  215.9 13.1 %collective-permute-start.37 = (bf16[384,128]{1,0:T(8,128)(2,1)}, bf16[384,128]{1,0:T(8,128)(2,1)S(1)}, u32[]{:S(2)}, u32[]{:S(2)}) collective-permute-start(bf16[384,128]{1,0:T(8,128)(2,1)} %get-tuple-element.229), channel_id=1, source_target_pairs={{4,0},{6,2},{8,12},{10,14},{20,16},{22,18},{24,28},{26,30},{5,1},{... | collective-permute-start | bytes 294920 | tf_op jit(solution)/shard_map/ppermute | solution.py:660
  217.2 13.1 %collective-permute-start.38 = (bf16[384,128]{1,0:T(8,128)(2,1)}, bf16[384,128]{1,0:T(8,128)(2,1)S(1)}, u32[]{:S(2)}, u32[]{:S(2)}) collective-permute-start(bf16[384,128]{1,0:T(8,128)(2,1)} %get-tuple-element.230), channel_id=1, source_target_pairs={{4,2},{6,0},{8,14},{10,12},{20,18},{22,16},{24,30},{26,28},{5,3},{... | collective-permute-start | bytes 294920 | tf_op jit(solution)/shard_map/ppermute | solution.py:660
  229.0 10.7 %copy-start.12 = (bf16[384,128]{1,0:T(8,128)(2,1)}, bf16[384,128]{1,0:T(8,128)(2,1)S(1)}, u32[]{:S(2)}) copy-start(bf16[384,128]{1,0:T(8,128)(2,1)S(1)} %collective-permute-done.37.refs_4_) | copy-start | bytes 294916
  229.0 9.3 %collective-permute-start.42 = (bf16[384,128]{1,0:T(8,128)(2,1)}, bf16[384,128]{1,0:T(8,128)(2,1)S(1)}, u32[]{:S(2)}, u32[]{:S(2)}) collective-permute-start(bf16[384,128]{1,0:T(8,128)(2,1)} %get-tuple-element.235), channel_id=1, source_target_pairs={{4,16},{6,18},{8,28},{10,30},{20,0},{22,2},{24,12},{26,14},{5,17},... | collective-permute-start | bytes 294920 | tf_op jit(solution)/shard_map/ppermute | solution.py:660
  230.3 9.3 %copy-start.13 = (bf16[384,128]{1,0:T(8,128)(2,1)}, bf16[384,128]{1,0:T(8,128)(2,1)S(1)}, u32[]{:S(2)}) copy-start(bf16[384,128]{1,0:T(8,128)(2,1)S(1)} %collective-permute-done.38.refs_5_) | copy-start | bytes 294916
  230.3 9.3 %collective-permute-start.43 = (bf16[384,128]{1,0:T(8,128)(2,1)}, bf16[384,128]{1,0:T(8,128)(2,1)S(1)}, u32[]{:S(2)}, u32[]{:S(2)}) collective-permute-start(bf16[384,128]{1,0:T(8,128)(2,1)} %get-tuple-element.236), channel_id=1, source_target_pairs={{4,18},{6,16},{8,30},{10,28},{20,2},{22,0},{24,14},{26,12},{5,19},... | collective-permute-start | bytes 294920 | tf_op jit(solution)/shard_map/ppermute | solution.py:660
  232.4 7.3 %copy-start.10 = (bf16[384,384]{1,0:T(8,128)(2,1)}, bf16[384,384]{1,0:T(8,128)(2,1)S(1)}, u32[]{:S(2)}) copy-start(bf16[384,384]{1,0:T(8,128)(2,1)S(1)} %collective-permute-done.34.refs_1_) | copy-start | bytes 884740
  232.4 7.3 %copy-start.11 = (bf16[384,384]{1,0:T(8,128)(2,1)}, bf16[384,384]{1,0:T(8,128)(2,1)S(1)}, u32[]{:S(2)}) copy-start(bf16[384,384]{1,0:T(8,128)(2,1)S(1)} %collective-permute-done.35.refs_2_) | copy-start | bytes 884740
  238.3 1.4 copy-start.14
  239.6 0.6 copy-start.15

commit v4 on v3

--- a/solution.py
+++ b/solution.py
@@ -621,13 +621,11 @@
     ((sum4,),) = [
         tuple(got.values()) for got in run([dict(pieces=lent0, uses=[(0, 1)] * 3)], lent_weights)
     ]
-    pair6, middle6, beside6, across6, across5, ahead0, ahead1, sum4, far_across4 = wait(
-        (pair6, middle6, beside6, across6, across5, ahead0, ahead1, sum4, far_across4)
-    )
-
-    far_across5, *far6 = [
-        lax.ppermute(value, "head", swap) for value in (across5, beside6, across6)
-    ]
+    pair6, middle6, across5, ahead0, ahead1, sum4, far_across4 = wait(
+        (pair6, middle6, across5, ahead0, ahead1, sum4, far_across4)
+    )
+
+    far_across5 = lax.ppermute(across5, "head", swap)
     done0, done1, lent0 = run(
         [
             dict(pieces=p, uses=[(0, 1)], sums={0: x[1]}, finish=(0,), carry=tuple(zip(h, x[0])))
@@ -636,6 +634,8 @@
         + [dict(pieces=lent0, uses=[(0, 1)], sums={0: sum4}, finish=(0,))],
         [(3, 0, [(middle6, pair6)])],
     )
+    beside6, across6, done0, done1, lent0 = wait((beside6, across6, done0, done1, lent0))
+    far6 = [lax.ppermute(value, "head", swap) for value in (beside6, across6)]
     lent1 = (((across4, across5), (far_across4, far_across5)), ((beside6, across6), far6))
     (lent1,) = run(
         [dict(pieces=lent1, uses=[(0, 1)] * 4, finish=(0,))],

time: 244 us -> 242 us (level)
    ppermute x6, waiting for transfers between devices: 20.4 us -> 17.3 us  [shared(): beside = lambda value: lax.ppermute(value, 'seq', swap)]
  transfers between devices with their start and end apart: 44 -> 44, of which waited for: 12 -> 13; matrix products, arithmetic and copies ran while one was open for 7% -> 7% of each run, Pallas kernels for 35% -> 35%
where the time goes in v4:
time: 242 us
  Pallas kernels  92.4 us (38%)
  waiting for transfers between devices  76.5 us (32%)
  starting transfers between devices  52.8 us (22%)
  local copies, waits for them, and re-layouts  9.85 us (4%)
  other arithmetic  9.6 us (4%)
    pallas_call x6, Pallas kernels, run_jobs(): pl.pallas_call(functools.partial(job_kernel, plan), out_shape=shapes, in_...  79.3 us
    ppermute x6, waiting for transfers between devices, pair(): return lax.ppermute(value, 'dp', [(0, 1), (1, 0), (2, 3), (3, 2)])  47 us
    ppermute x6, starting transfers between devices, pair(): return lax.ppermute(value, 'dp', [(0, 1), (1, 0), (2, 3), (3, 2)])  19.8 us
    ppermute x6, waiting for transfers between devices, shared(): beside = lambda value: lax.ppermute(value, 'seq', swap)  17.3 us
    pallas_call x2, Pallas kernels, normalize_part(): pl.pallas_call(functools.partial(normalize_kernel, step, other, taken), o...  9.94 us
    ppermute x6, starting transfers between devices, middle(): return lax.ppermute(value, 'dp', [(1, 2), (2, 1)])  9.15 us
    ppermute x6, starting transfers between devices, shared(): beside = lambda value: lax.ppermute(value, 'seq', swap)  8.24 us
    ppermute x4, waiting for transfers between devices, hand_back(): got.append(lax.ppermute(sent, ('groups', 'dp', 'seq'), steps))  7.6 us
  transfers between devices with their start and end apart: 44, of which 13 were waited for; matrix products, arithmetic and copies ran while one was open for 7% of the time, Pallas kernels for 35%

profile of v4, /device:TPU:0, one launch (start us, length us, event | category | flops | bytes accessed | tf_op | source)
XLA Modules:
  0.0 241.7 jit_solution(2613472749653557892)
XLA Ops:
  0.0 5.2 %shard_map.37 = (bf16[192,3072]{1,0:T(8,128)(2,1)}, bf16[192,3072]{1,0:T(8,128)(2,1)}, bf16[1536,384]{1,0:T(8,128)(2,1)}) custom-call(bf16[1,384,6144]{2,1,0:T(8,128)(2,1)} %tokens_ref.2, f32[1,6144]{1,0:T(1,128)} %bitcast.35, bf16[6,1536,384]{2,1,0:T(8,128)(2,1)} %bitcast.23), custom_call_target="tpu_custom_call" | custom-call | flops 9437184 | bytes 4718592 | tf_op jit(solution)/shard_map/pallas_call | solution.py:147
  5.2 3.0 %collective-permute-start.2 = (bf16[192,3072]{1,0:T(8,128)(2,1)}, bf16[192,3072]{1,0:T(8,128)(2,1)}, u32[]{:S(2)}, u32[]{:S(2)}) collective-permute-start(bf16[192,3072]{1,0:T(8,128)(2,1)} %get-tuple-element.131.refs_0_.refs_8_), channel_id=1, source_target_pairs={{0,2},{2,0},{1,3},{3,1},{4,6},{6,4},{5,7},{7,5},{8,10},{10,8},{9,1... | collective-permute-start | bytes 3538952 | tf_op jit(solution)/shard_map/ppermute | solution.py:502
  8.2 1.5 collective-permute-start.3
  9.7 1.6 collective-permute-start
  11.3 1.7 collective-permute-start.1
  13.0 2.9 %dynamic-slice_bitcast_fusion = (bf16[1536,384]{1,0:T(8,128)(2,1)}, bf16[1,1536,384]{2,1,0:T(8,128)(2,1)S(1)}) fusion(bf16[6,1536,384]{2,1,0:T(8,128)(2,1)} %bitcast.24, s32[]{:T(128)S(6)} %select_n.63, s32[]{:T(128)S(6)} %select_n.62), kind=kLoop, calls=%fused_computation.1 | loop fusion | bytes 4718600 | tf_op jit(solution)/shard_map/jit(dynamic_index_in_dim)/squeeze | solution.py:536
  15.9 1.2 copy.7
  17.1 0.9 copy-done.1
  18.0 1.1 broadcast_select_fusion.3
  19.2 0.6 pad_add_fusion.role_ref
  19.7 14.8 %collective-permute-done.2.refs_4_.refs_12_ = bf16[192,3072]{1,0:T(8,128)(2,1)} collective-permute-done((bf16[192,3072]{1,0:T(8,128)(2,1)}, bf16[192,3072]{1,0:T(8,128)(2,1)}, u32[]{:S(2)}, u32[]{:S(2)}) %collective-permute-start.2) | collective-permute-done | bytes 1179680 | tf_op jit(solution)/shard_map/ppermute | solution.py:502
  34.5 1.5 collective-permute-done.3.refs_0_.refs_8_
  36.3 1.7 collective-permute-start.7
  38.0 3.8 %collective-permute-start.4 = (bf16[192,3072]{1,0:T(8,128)(2,1)}, bf16[192,3072]{1,0:T(8,128)(2,1)}, u32[]{:S(2)}, u32[]{:S(2)}) collective-permute-start(bf16[192,3072]{1,0:T(8,128)(2,1)} %broadcast_select_fusion.3), channel_id=1, source_target_pairs={{0,4},{4,0},{8,12},{12,8},{1,5},{5,1},{9,13},{13,9},{2,6},{6,2},{1... | collective-permute-start | bytes 3538952 | tf_op jit(solution)/shard_map/ppermute | solution.py:496
  41.8 1.7 collective-permute-start.5
  43.5 2.5 %copy.8 = bf16[24,8,8,384]{3,1,2,0:T(8,128)(2,1)} copy(bf16[24,8,8,384]{3,1,0,2:T(8,128)(2,1)} %bitcast.21) | data formatting | bytes 2359296
  46.0 4.8 %shard_map.38 = (bf16[192,3072]{1,0:T(8,128)(2,1)}, bf16[192,3072]{1,0:T(8,128)(2,1)}) custom-call(bf16[1,384,6144]{2,1,0:T(8,128)(2,1)} %tokens_ref.2, f32[1,6144]{1,0:T(1,128)} %bitcast.36, bf16[6,1536,384]{2,1,0:T(8,128)(2,1)} %bitcast.25), custom_call_target="tpu_custom_call" | custom-call | flops 9437184 | bytes 4718592 | tf_op jit(solution)/shard_map/pallas_call | solution.py:147
  50.7 1.4 broadcast_select_fusion.2
  52.1 14.5 %collective-permute-done.4.refs_25_.refs_0_.refs_16_ = bf16[192,3072]{1,0:T(8,128)(2,1)} collective-permute-done((bf16[192,3072]{1,0:T(8,128)(2,1)}, bf16[192,3072]{1,0:T(8,128)(2,1)}, u32[]{:S(2)}, u32[]{:S(2)}) %collective-permute-start.4) | collective-permute-done | bytes 1179680 | tf_op jit(solution)/shard_map/ppermute | solution.py:496
  66.7 4.2 %collective-permute-start.10 = (bf16[192,3072]{1,0:T(8,128)(2,1)S(1)}, bf16[192,3072]{1,0:T(8,128)(2,1)S(1)}, u32[]{:S(2)}, u32[]{:S(2)}) collective-permute-start(bf16[192,3072]{1,0:T(8,128)(2,1)S(1)} %broadcast_select_fusion.2), channel_id=1, source_target_pairs={{0,4},{4,0},{8,12},{12,8},{1,5},{5,1},{9,13},{13,9},{2,6},{6,2},{1... | collective-permute-start | bytes 3538952 | tf_op jit(solution)/shard_map/ppermute | solution.py:496
  70.9 0.7 collective-permute-start.11
  71.6 1.6 collective-permute-start.12
  73.2 0.5 collective-permute-start.13
  73.7 1.2 broadcast_select_fusion.1
  74.9 22.6 %collective-permute-done.10.refs_28_.refs_1_.refs_17_ = bf16[192,3072]{1,0:T(8,128)(2,1)S(1)} collective-permute-done((bf16[192,3072]{1,0:T(8,128)(2,1)S(1)}, bf16[192,3072]{1,0:T(8,128)(2,1)S(1)}, u32[]{:S(2)}, u32[]{:S(2)}) %collective-permute-start.10) | collective-permute-done | bytes 1179680 | tf_op jit(solution)/shard_map/ppermute | solution.py:496
  97.5 2.5 %collective-permute-done.12.refs_4_.refs_12_ = bf16[192,3072]{1,0:T(8,128)(2,1)S(1)} collective-permute-done((bf16[192,3072]{1,0:T(8,128)(2,1)}, bf16[192,3072]{1,0:T(8,128)(2,1)S(1)}, u32[]{:S(2)}, u32[]{:S(2)}) %collective-permute-start.12) | collective-permute-done | bytes 1179680 | tf_op jit(solution)/shard_map/ppermute | solution.py:502
  100.0 1.3 collective-permute-done.13.refs_5_.refs_13_
  101.4 1.2 collective-permute-start.18
  102.6 0.5 collective-permute-start.19
  103.1 2.9 %collective-permute-start.16 = (bf16[1536,384]{1,0:T(8,128)(2,1)}, bf16[1536,384]{1,0:T(8,128)(2,1)}, u32[]{:S(2)}, u32[]{:S(2)}) collective-permute-start(bf16[1536,384]{1,0:T(8,128)(2,1)} %broadcast_select_fusion.1), channel_id=1, source_target_pairs={{0,4},{4,0},{8,12},{12,8},{1,5},{5,1},{9,13},{13,9},{2,6},{6,2},{1... | collective-permute-start | bytes 3538952 | tf_op jit(solution)/shard_map/ppermute | solution.py:496
  106.0 1.7 collective-permute-start.17
  107.7 1.0 copy-done.6
  108.7 2.8 %pad_maximum_fusion = bf16[384,3072]{1,0:T(8,128)(2,1)} fusion(bf16[192,3072]{1,0:T(8,128)(2,1)S(1)} %collective-permute-done.10.refs_28_.refs_1_.refs_17_, bf16[192,3072]{1,0:T(8,128)(2,1)} %collective-permute-done.4.refs_25_.refs_0_.refs_16_), kind=kLoop, calls=%fused_computation | loop fusion | flops 4718592 | bytes 4718592 | tf_op jit(solution)/shard_map/concatenate | solution.py:576
  111.5 2.5 %broadcast_select_fusion = bf16[1536,384]{1,0:T(8,128)(2,1)} fusion(bf16[1536,384]{1,0:T(8,128)(2,1)S(1)} %collective-permute-done.11.refs_14_.refs_22_, bf16[1536,384]{1,0:T(8,128)(2,1)} %get-tuple-element.216.refs_11_.refs_19_.refs_10_, pred[]{:T(512)S(6)} %or.3), kind=kLoop, calls=%fused_computation.2 | loop fusion | flops 589824 | bytes 3538945 | tf_op jit(solution)/shard_map/jit(_where)/select_n | solution.py:493
  114.0 14.6 %shard_map.39 = (bf16[384,128]{1,0:T(8,128)(2,1)}, bf16[384,128]{1,0:T(8,128)(2,1)}, f32[768,384]{1,0:T(8,128)}, f32[768,384]{1,0:T(8,128)}) custom-call(s32[2]{0:T(128)} %pad_add_fusion.role_ref, bf16[192,3072]{1,0:T(8,128)(2,1)} %get-tuple-element.131.refs_0_.refs_8_, bf16[192,3072]{1,0:T(8,128)(2,1)} %get-tuple-element.137.refs_1_.refs_9_, ...), custom_call_target="tpu_custom_call" | custom-call | flops 6341787648 | tf_op jit(solution)/shard_map/pallas_call | solution.py:406
  128.6 3.8 %collective-permute-done.16.refs_27_.refs_17_ = bf16[1536,384]{1,0:T(8,128)(2,1)} collective-permute-done((bf16[1536,384]{1,0:T(8,128)(2,1)}, bf16[1536,384]{1,0:T(8,128)(2,1)}, u32[]{:S(2)}, u32[]{:S(2)}) %collective-permute-start.16) | collective-permute-done | bytes 1179680 | tf_op jit(solution)/shard_map/ppermute | solution.py:496
  132.5 0.9 collective-permute-start.24
  133.4 1.5 collective-permute-start.25
  134.9 3.6 %collective-permute-start.22 = (bf16[1536,384]{1,0:T(8,128)(2,1)}, bf16[1536,384]{1,0:T(8,128)(2,1)}, u32[]{:S(2)}, u32[]{:S(2)}) collective-permute-start(bf16[1536,384]{1,0:T(8,128)(2,1)} %broadcast_select_fusion), channel_id=1, source_target_pairs={{0,4},{4,0},{8,12},{12,8},{1,5},{5,1},{9,13},{13,9},{2,6},{6,2},{1... | collective-permute-start | bytes 3538952 | tf_op jit(solution)/shard_map/ppermute | solution.py:496
  138.5 1.7 collective-permute-start.23
  140.2 20.0 %shard_map.40 = (bf16[384,128]{1,0:T(8,128)(2,1)}, bf16[384,128]{1,0:T(8,128)(2,1)}, f32[768,384]{1,0:T(8,128)}, f32[768,384]{1,0:T(8,128)}, f32[768,384]{1,0:T(8,128)}, /*index=5*/f32[768,384]{1,0:T(8,128)}) custom-call(s32[2]{0:T(128)} %pad_add_fusion.role_ref, bf16[192,3072]{1,0:T(8,128)(2,1)} %collective-permute-done.3.refs_0_.refs_8_, ...), custom_call_target="tpu_custom_call" | custom-call | flops 9965666304 | tf_op jit(solution)/shard_map/pallas_call | solution.py:406
  160.2 4.6 %collective-permute-done.22.refs_18_.refs_8_ = bf16[1536,384]{1,0:T(8,128)(2,1)} collective-permute-done((bf16[1536,384]{1,0:T(8,128)(2,1)}, bf16[1536,384]{1,0:T(8,128)(2,1)}, u32[]{:S(2)}, u32[]{:S(2)}) %collective-permute-start.22) | collective-permute-done | bytes 1179680 | tf_op jit(solution)/shard_map/ppermute | solution.py:496
  165.0 3.7 %collective-permute-start.31 = (bf16[1536,384]{1,0:T(8,128)(2,1)}, bf16[1536,384]{1,0:T(8,128)(2,1)}, u32[]{:S(2)}, u32[]{:S(2)}) collective-permute-start(bf16[1536,384]{1,0:T(8,128)(2,1)} %collective-permute-done.23.refs_16_), channel_id=1, source_target_pairs={{0,4},{4,0},{8,12},{12,8},{1,5},{5,1},{9,13},{13,9},{2,6},{6,2},{1... | collective-permute-start | bytes 3538952 | tf_op jit(solution)/shard_map/ppermute | solution.py:496
  168.6 1.7 collective-permute-start.32
  170.5 1.2 collective-permute-start.28
  171.7 0.5 collective-permute-start.29
  172.2 13.0 %shard_map.41 = (bf16[384,128]{1,0:T(8,128)(2,1)}, bf16[384,128]{1,0:T(8,128)(2,1)}, f32[768,384]{1,0:T(8,128)}, bf16[384,128]{1,0:T(8,128)(2,1)}, bf16[384,128]{1,0:T(8,128)(2,1)}, /*index=5*/f32[768,384]{1,0:T(8,128)}) custom-call(s32[2]{0:T(128)} %pad_add_fusion.role_ref, bf16[192,3072]{1,0:T(8,128)(2,1)} %get-tuple-element.131.refs_0_.refs_8_, ...), custom_call_target="tpu_custom_call" | custom-call | flops 3623878656 | tf_op jit(solution)/shard_map/pallas_call | solution.py:406
  185.2 8.7 %shard_map.42.refs_28_ = f32[768,384]{1,0:T(8,128)} custom-call(s32[2]{0:T(128)} %pad_add_fusion.role_ref, bf16[192,3072]{1,0:T(8,128)(2,1)} %collective-permute-done.4.refs_25_.refs_0_.refs_16_, bf16[192,3072]{1,0:T(8,128)(2,1)} %copy-done.2, bf16[384,3072]{1,0:T(8,128)(2,1)} %collective-permute-done.26.refs_2_.refs_3_.refs_18_.refs_19_, ...), custom_call_target="tpu_custom_call" | custom-call | flops 2717908992 | tf_op jit(solution)/shard_map/pallas_call | solution.py:406
  194.0 1.5 collective-permute-done.31.refs_25_
  195.5 12.9 %shard_map.43 = (bf16[384,384]{1,0:T(8,128)(2,1)}, bf16[384,384]{1,0:T(8,128)(2,1)}, bf16[384,384]{1,0:T(8,128)(2,1)}, bf16[384,384]{1,0:T(8,128)(2,1)}, bf16[38...) custom-call(s32[2]{0:T(128)} %pad_add_fusion.role_ref, bf16[192,3072]{1,0:T(8,128)(2,1)} %get-tuple-element.131.refs_0_.refs_8_, ...), custom_call_target="tpu_custom_call" | custom-call | flops 2717908992 | tf_op jit(solution)/shard_map/pallas_call | solution.py:406
  209.1 1.2 collective-permute-start.34
  210.3 0.5 collective-permute-start.35
  210.8 1.7 collective-permute-done.40.refs_6_
  212.4 1.1 collective-permute-start.36
  213.6 1.3 collective-permute-start.37
  215.0 1.5 collective-permute-start.38
  216.6 10.2 %shard_map.44 = (bf16[384,128]{1,0:T(8,128)(2,1)}, bf16[384,128]{1,0:T(8,128)(2,1)}) custom-call(s32[2]{0:T(128)} %pad_add_fusion.role_ref, bf16[192,3072]{1,0:T(8,128)(2,1)} %collective-permute-done.19.refs_0_, bf16[192,3072]{1,0:T(8,128)(2,1)} %collective-permute-done.25.refs_1_, bf16[192,3072]{1,0:T(8,128)(2,1)} %collective-permute-done.33.refs_2_, ...), custom_call_target="tpu_custom_call" | custom-call | flops 3623878656 | tf_op jit(solution)/shard_map/pallas_call | solution.py:406
  226.8 1.3 collective-permute-start.42
  228.1 1.3 collective-permute-start.43
  229.5 0.6 stack.34.place_ref
  230.1 6.0 %collective-permute-done.42.refs_6_ = bf16[384,128]{1,0:T(8,128)(2,1)S(1)} collective-permute-done((bf16[384,128]{1,0:T(8,128)(2,1)}, bf16[384,128]{1,0:T(8,128)(2,1)S(1)}, u32[]{:S(2)}, u32[]{:S(2)}) %collective-permute-start.42) | collective-permute-done | bytes 98336 | tf_op jit(solution)/shard_map/ppermute | solution.py:660
  236.1 1.6 collective-permute-done.43.refs_7_
  237.8 0.6 copy-done.15
  238.4 3.1 %shard_map.45 = bf16[384,1536]{1,0:T(8,128)(2,1)} custom-call(s32[5]{0:T(128)} %stack.34.place_ref, bf16[384,384]{1,0:T(8,128)(2,1)} %get-tuple-element.237.refs_0_, bf16[384,384]{1,0:T(8,128)(2,1)} %copy-done.10, bf16[384,384]{1,0:T(8,128)(2,1)} %copy-done.11, bf16[384,384]{1,0:T(8,128)(2,1)} %collective-permute-done.36.refs_3_, ...), custom_call_target="tpu_custom_call" | custom-call | bytes 2359296 | tf_op jit(solution)/shard_map/pallas_call | solution.py:467
  (75 shorter events, 1.8 us)
Async XLA Ops:
  5.2 29.3 %collective-permute-start.2 = (bf16[192,3072]{1,0:T(8,128)(2,1)}, bf16[192,3072]{1,0:T(8,128)(2,1)}, u32[]{:S(2)}, u32[]{:S(2)}) collective-permute-start(bf16[192,3072]{1,0:T(8,128)(2,1)} %get-tuple-element.131.refs_0_.refs_8_), channel_id=1, source_target_pairs={{0,2},{2,0},{1,3},{3,1},{4,6},{6,4},{5,7},{7,5},{8,10},{10,8},{9,1... | collective-permute-start | bytes 3538952 | tf_op jit(solution)/shard_map/ppermute | solution.py:502
  8.2 27.7 %collective-permute-start.3 = (bf16[192,3072]{1,0:T(8,128)(2,1)}, bf16[192,3072]{1,0:T(8,128)(2,1)}, u32[]{:S(2)}, u32[]{:S(2)}) collective-permute-start(bf16[192,3072]{1,0:T(8,128)(2,1)} %get-tuple-element.131.refs_0_.refs_8_), channel_id=1, source_target_pairs={{0,16},{16,0},{1,17},{17,1},{2,18},{18,2},{3,19},{19,3},{4,20},{20... | collective-permute-start | bytes 3538952 | tf_op jit(solution)/shard_map/ppermute | solution.py:503
  9.7 28.3 %collective-permute-start = (bf16[1536,384]{1,0:T(8,128)(2,1)}, bf16[1536,384]{1,0:T(8,128)(2,1)}, u32[]{:S(2)}, u32[]{:S(2)}) collective-permute-start(bf16[1536,384]{1,0:T(8,128)(2,1)} %get-tuple-element.130.refs_8_.refs_10_.refs_16_.refs_18_), channel_id=1, source_target_pairs={{0,4},{4,0},{8,12},{12,8},{1,5},{5,1},{9,13},{13,9},{2,6},{6,2},{1... | collective-permute-start | bytes 3538952 | tf_op jit(solution)/shard_map/ppermute | solution.py:496
  11.3 26.7 %collective-permute-start.1 = (bf16[1536,384]{1,0:T(8,128)(2,1)}, bf16[1536,384]{1,0:T(8,128)(2,1)}, u32[]{:S(2)}, u32[]{:S(2)}) collective-permute-start(bf16[1536,384]{1,0:T(8,128)(2,1)} %get-tuple-element.130.refs_8_.refs_10_.refs_16_.refs_18_), channel_id=1, source_target_pairs={{4,8},{8,4},{5,9},{9,5},{6,10},{10,6},{7,11},{11,7},{20,24},{24,20... | collective-permute-start | bytes 3538952 | tf_op jit(solution)/shard_map/ppermute | solution.py:499
  15.9 57.8 %copy-start = (bf16[1,1536,384]{2,1,0:T(8,128)(2,1)}, bf16[1,1536,384]{2,1,0:T(8,128)(2,1)S(1)}, u32[]{:S(2)}) copy-start(bf16[1,1536,384]{2,1,0:T(8,128)(2,1)S(1)} %get-tuple-element.250) | copy-start | bytes 3538948
  15.9 2.1 copy-start.1
  35.9 7.5 %collective-permute-start.8 = (bf16[192,3072]{1,0:T(8,128)(2,1)}, bf16[192,3072]{1,0:T(8,128)(2,1)}, u32[]{:S(2)}, u32[]{:S(2)}) collective-permute-start(bf16[192,3072]{1,0:T(8,128)(2,1)} %collective-permute-done.2.refs_4_.refs_12_), channel_id=1, source_target_pairs={{0,1},{1,0},{2,3},{3,2},{4,5},{5,4},{6,7},{7,6},{8,9},{9,8},{10,11... | collective-permute-start | bytes 3538952 | tf_op jit(solution)/shard_map/ppermute | solution.py:510
  36.0 30.6 %collective-permute-start.6 = (bf16[192,3072]{1,0:T(8,128)(2,1)}, bf16[192,3072]{1,0:T(8,128)(2,1)}, u32[]{:S(2)}, u32[]{:S(2)}) collective-permute-start(bf16[192,3072]{1,0:T(8,128)(2,1)} %get-tuple-element.137.refs_1_.refs_9_), channel_id=1, source_target_pairs={{0,2},{2,0},{1,3},{3,1},{4,6},{6,4},{5,7},{7,5},{8,10},{10,8},{9,1... | collective-permute-start | bytes 3538952 | tf_op jit(solution)/shard_map/ppermute | solution.py:502
  36.3 30.3 %collective-permute-start.7 = (bf16[192,3072]{1,0:T(8,128)(2,1)}, bf16[192,3072]{1,0:T(8,128)(2,1)}, u32[]{:S(2)}, u32[]{:S(2)}) collective-permute-start(bf16[192,3072]{1,0:T(8,128)(2,1)} %get-tuple-element.137.refs_1_.refs_9_), channel_id=1, source_target_pairs={{0,16},{16,0},{1,17},{17,1},{2,18},{18,2},{3,19},{19,3},{4,20},{20... | collective-permute-start | bytes 3538952 | tf_op jit(solution)/shard_map/ppermute | solution.py:503
  38.0 28.6 %collective-permute-start.4 = (bf16[192,3072]{1,0:T(8,128)(2,1)}, bf16[192,3072]{1,0:T(8,128)(2,1)}, u32[]{:S(2)}, u32[]{:S(2)}) collective-permute-start(bf16[192,3072]{1,0:T(8,128)(2,1)} %broadcast_select_fusion.3), channel_id=1, source_target_pairs={{0,4},{4,0},{8,12},{12,8},{1,5},{5,1},{9,13},{13,9},{2,6},{6,2},{1... | collective-permute-start | bytes 3538952 | tf_op jit(solution)/shard_map/ppermute | solution.py:496
  41.8 24.8 %collective-permute-start.5 = (bf16[1536,384]{1,0:T(8,128)(2,1)}, bf16[1536,384]{1,0:T(8,128)(2,1)}, u32[]{:S(2)}, u32[]{:S(2)}) collective-permute-start(bf16[1536,384]{1,0:T(8,128)(2,1)} %collective-permute-done.refs_15_.refs_16_.refs_23_.refs_26_), channel_id=1, source_target_pairs={{4,8},{8,4},{5,9},{9,5},{6,10},{10,6},{7,11},{11,7},{20,24},{24,20... | collective-permute-start | bytes 3538952 | tf_op jit(solution)/shard_map/ppermute | solution.py:499
  43.5 23.1 %collective-permute-start.9 = (bf16[192,3072]{1,0:T(8,128)(2,1)}, bf16[192,3072]{1,0:T(8,128)(2,1)}, u32[]{:S(2)}, u32[]{:S(2)}) collective-permute-start(bf16[192,3072]{1,0:T(8,128)(2,1)} %collective-permute-done.3.refs_0_.refs_8_), channel_id=1, source_target_pairs={{0,1},{1,0},{2,3},{3,2},{4,5},{5,4},{6,7},{7,6},{8,9},{9,8},{10,11... | collective-permute-start | bytes 3538952 | tf_op jit(solution)/shard_map/ppermute | solution.py:510
  66.6 7.1 %collective-permute-start.14 = (bf16[192,3072]{1,0:T(8,128)(2,1)}, bf16[192,3072]{1,0:T(8,128)(2,1)}, u32[]{:S(2)}, u32[]{:S(2)}) collective-permute-start(bf16[192,3072]{1,0:T(8,128)(2,1)} %collective-permute-done.7.refs_1_.refs_9_), channel_id=1, source_target_pairs={{0,1},{1,0},{2,3},{3,2},{4,5},{5,4},{6,7},{7,6},{8,9},{9,8},{10,11... | collective-permute-start | bytes 3538952 | tf_op jit(solution)/shard_map/ppermute | solution.py:510
  66.7 30.8 %collective-permute-start.10 = (bf16[192,3072]{1,0:T(8,128)(2,1)S(1)}, bf16[192,3072]{1,0:T(8,128)(2,1)S(1)}, u32[]{:S(2)}, u32[]{:S(2)}) collective-permute-start(bf16[192,3072]{1,0:T(8,128)(2,1)S(1)} %broadcast_select_fusion.2), channel_id=1, source_target_pairs={{0,4},{4,0},{8,12},{12,8},{1,5},{5,1},{9,13},{13,9},{2,6},{6,2},{1... | collective-permute-start | bytes 3538952 | tf_op jit(solution)/shard_map/ppermute | solution.py:496
  70.9 26.6 %collective-permute-start.11 = (bf16[1536,384]{1,0:T(8,128)(2,1)S(1)}, bf16[1536,384]{1,0:T(8,128)(2,1)S(1)}, u32[]{:S(2)}, u32[]{:S(2)}) collective-permute-start(bf16[1536,384]{1,0:T(8,128)(2,1)S(1)} %bitcast.27), channel_id=1, source_target_pairs={{4,8},{8,4},{5,9},{9,5},{6,10},{10,6},{7,11},{11,7},{20,24},{24,20... | collective-permute-start | bytes 3538952 | tf_op jit(solution)/shard_map/ppermute | solution.py:499
  71.6 28.3 %collective-permute-start.12 = (bf16[192,3072]{1,0:T(8,128)(2,1)}, bf16[192,3072]{1,0:T(8,128)(2,1)S(1)}, u32[]{:S(2)}, u32[]{:S(2)}) collective-permute-start(bf16[192,3072]{1,0:T(8,128)(2,1)} %collective-permute-done.3.refs_0_.refs_8_), channel_id=1, source_target_pairs={{0,2},{2,0},{1,3},{3,1},{4,6},{6,4},{5,7},{7,5},{8,10},{10,8},{9,1... | collective-permute-start | bytes 3538952 | tf_op jit(solution)/shard_map/ppermute | solution.py:502
  73.2 28.1 %collective-permute-start.13 = (bf16[192,3072]{1,0:T(8,128)(2,1)}, bf16[192,3072]{1,0:T(8,128)(2,1)}, u32[]{:S(2)}, u32[]{:S(2)}) collective-permute-start(bf16[192,3072]{1,0:T(8,128)(2,1)} %collective-permute-done.6.refs_5_.refs_13_), channel_id=1, source_target_pairs={{0,16},{16,0},{1,17},{17,1},{2,18},{18,2},{3,19},{19,3},{4,20},{20... | collective-permute-start | bytes 3538952 | tf_op jit(solution)/shard_map/ppermute | solution.py:503
  73.7 27.6 %collective-permute-start.15 = (bf16[192,3072]{1,0:T(8,128)(2,1)}, bf16[192,3072]{1,0:T(8,128)(2,1)S(1)}, u32[]{:S(2)}, u32[]{:S(2)}) collective-permute-start(bf16[192,3072]{1,0:T(8,128)(2,1)} %collective-permute-done.6.refs_5_.refs_13_), channel_id=1, source_target_pairs={{0,1},{1,0},{2,3},{3,2},{4,5},{5,4},{6,7},{7,6},{8,9},{9,8},{10,11... | collective-permute-start | bytes 3538952 | tf_op jit(solution)/shard_map/ppermute | solution.py:510
  97.5 14.1 %copy-start.2 = (bf16[192,3072]{1,0:T(8,128)(2,1)}, bf16[192,3072]{1,0:T(8,128)(2,1)S(1)}, u32[]{:S(2)}) copy-start(bf16[192,3072]{1,0:T(8,128)(2,1)S(1)} %collective-permute-done.10.refs_28_.refs_1_.refs_17_) | copy-start | bytes 3538948
  97.5 14.1 %copy-start.8 = (bf16[1536,384]{1,0:T(8,128)(2,1)}, bf16[1536,384]{1,0:T(8,128)(2,1)S(1)}, u32[]{:S(2)}) copy-start(bf16[1536,384]{1,0:T(8,128)(2,1)S(1)} %collective-permute-done.11.refs_14_.refs_22_) | copy-start | bytes 3538948
  100.0 1.3 copy-start.4
  101.3 6.4 %copy-start.5 = (bf16[192,3072]{1,0:T(8,128)(2,1)}, bf16[192,3072]{1,0:T(8,128)(2,1)S(1)}, u32[]{:S(2)}) copy-start(bf16[192,3072]{1,0:T(8,128)(2,1)S(1)} %collective-permute-done.15.refs_7_.refs_15_) | copy-start | bytes 3538948
  101.3 6.4 %collective-permute-start.20 = (bf16[192,3072]{1,0:T(8,128)(2,1)S(1)}, bf16[192,3072]{1,0:T(8,128)(2,1)S(1)}, u32[]{:S(2)}, u32[]{:S(2)}) collective-permute-start(bf16[192,3072]{1,0:T(8,128)(2,1)S(1)} %collective-permute-done.12.refs_4_.refs_12_), channel_id=1, source_target_pairs={{0,1},{1,0},{2,3},{3,2},{4,5},{5,4},{6,7},{7,6},{8,9},{9,8},{10,11... | collective-permute-start | bytes 3538952 | tf_op jit(solution)/shard_map/ppermute | solution.py:510
  101.4 31.0 %collective-permute-start.18 = (bf16[192,3072]{1,0:T(8,128)(2,1)}, bf16[192,3072]{1,0:T(8,128)(2,1)}, u32[]{:S(2)}, u32[]{:S(2)}) collective-permute-start(bf16[192,3072]{1,0:T(8,128)(2,1)} %collective-permute-done.4.refs_25_.refs_0_.refs_16_), channel_id=1, source_target_pairs={{0,2},{2,0},{1,3},{3,1},{4,6},{6,4},{5,7},{7,5},{8,10},{10,8},{9,1... | collective-permute-start | bytes 3538952 | tf_op jit(solution)/shard_map/ppermute | solution.py:502
  102.6 29.8 %collective-permute-start.19 = (bf16[192,3072]{1,0:T(8,128)(2,1)}, bf16[192,3072]{1,0:T(8,128)(2,1)}, u32[]{:S(2)}, u32[]{:S(2)}) collective-permute-start(bf16[192,3072]{1,0:T(8,128)(2,1)} %collective-permute-done.4.refs_25_.refs_0_.refs_16_), channel_id=1, source_target_pairs={{0,16},{16,0},{1,17},{17,1},{2,18},{18,2},{3,19},{19,3},{4,20},{20... | collective-permute-start | bytes 3538952 | tf_op jit(solution)/shard_map/ppermute | solution.py:503
  103.1 29.3 %collective-permute-start.16 = (bf16[1536,384]{1,0:T(8,128)(2,1)}, bf16[1536,384]{1,0:T(8,128)(2,1)}, u32[]{:S(2)}, u32[]{:S(2)}) collective-permute-start(bf16[1536,384]{1,0:T(8,128)(2,1)} %broadcast_select_fusion.1), channel_id=1, source_target_pairs={{0,4},{4,0},{8,12},{12,8},{1,5},{5,1},{9,13},{13,9},{2,6},{6,2},{1... | collective-permute-start | bytes 3538952 | tf_op jit(solution)/shard_map/ppermute | solution.py:496
  106.0 26.4 %collective-permute-start.17 = (bf16[1536,384]{1,0:T(8,128)(2,1)}, bf16[1536,384]{1,0:T(8,128)(2,1)}, u32[]{:S(2)}, u32[]{:S(2)}) collective-permute-start(bf16[1536,384]{1,0:T(8,128)(2,1)} %get-tuple-element.216.refs_11_.refs_19_.refs_10_), channel_id=1, source_target_pairs={{4,8},{8,4},{5,9},{9,5},{6,10},{10,6},{7,11},{11,7},{20,24},{24,20... | collective-permute-start | bytes 3538952 | tf_op jit(solution)/shard_map/ppermute | solution.py:499
  107.7 1.0 copy-start.6
  108.7 23.7 %collective-permute-start.21 = (bf16[192,3072]{1,0:T(8,128)(2,1)}, bf16[192,3072]{1,0:T(8,128)(2,1)}, u32[]{:S(2)}, u32[]{:S(2)}) collective-permute-start(bf16[192,3072]{1,0:T(8,128)(2,1)} %collective-permute-done.13.refs_5_.refs_13_), channel_id=1, source_target_pairs={{0,1},{1,0},{2,3},{3,2},{4,5},{5,4},{6,7},{7,6},{8,9},{9,8},{10,11... | collective-permute-start | bytes 3538952 | tf_op jit(solution)/shard_map/ppermute | solution.py:510
  114.0 18.5 %copy-start.3 = (bf16[192,3072]{1,0:T(8,128)(2,1)S(1)}, bf16[192,3072]{1,0:T(8,128)(2,1)}, u32[]{:S(2)}) copy-start(bf16[192,3072]{1,0:T(8,128)(2,1)} %copy-done.2) | copy-start | bytes 3538948
  132.4 7.8 %collective-permute-start.26 = (bf16[384,3072]{1,0:T(8,128)(2,1)}, bf16[384,3072]{1,0:T(8,128)(2,1)}, u32[]{:S(2)}, u32[]{:S(2)}) collective-permute-start(bf16[384,3072]{1,0:T(8,128)(2,1)} %pad_maximum_fusion), channel_id=1, source_target_pairs={{0,1},{1,0},{2,3},{3,2},{4,5},{5,4},{6,7},{7,6},{8,9},{9,8},{10,11... | collective-permute-start | bytes 7077896 | tf_op jit(solution)/shard_map/ppermute | solution.py:510
  132.5 32.4 %collective-permute-start.24 = (bf16[192,3072]{1,0:T(8,128)(2,1)S(1)}, bf16[192,3072]{1,0:T(8,128)(2,1)}, u32[]{:S(2)}, u32[]{:S(2)}) collective-permute-start(bf16[192,3072]{1,0:T(8,128)(2,1)S(1)} %copy-done.3), channel_id=1, source_target_pairs={{0,2},{2,0},{1,3},{3,1},{4,6},{6,4},{5,7},{7,5},{8,10},{10,8},{9,1... | collective-permute-start | bytes 3538952 | tf_op jit(solution)/shard_map/ppermute | solution.py:502
  133.4 31.5 %collective-permute-start.25 = (bf16[192,3072]{1,0:T(8,128)(2,1)S(1)}, bf16[192,3072]{1,0:T(8,128)(2,1)}, u32[]{:S(2)}, u32[]{:S(2)}) collective-permute-start(bf16[192,3072]{1,0:T(8,128)(2,1)S(1)} %copy-done.3), channel_id=1, source_target_pairs={{0,16},{16,0},{1,17},{17,1},{2,18},{18,2},{3,19},{19,3},{4,20},{20... | collective-permute-start | bytes 3538952 | tf_op jit(solution)/shard_map/ppermute | solution.py:503
  134.9 29.9 %collective-permute-start.22 = (bf16[1536,384]{1,0:T(8,128)(2,1)}, bf16[1536,384]{1,0:T(8,128)(2,1)}, u32[]{:S(2)}, u32[]{:S(2)}) collective-permute-start(bf16[1536,384]{1,0:T(8,128)(2,1)} %broadcast_select_fusion), channel_id=1, source_target_pairs={{0,4},{4,0},{8,12},{12,8},{1,5},{5,1},{9,13},{13,9},{2,6},{6,2},{1... | collective-permute-start | bytes 3538952 | tf_op jit(solution)/shard_map/ppermute | solution.py:496
  138.5 26.3 %collective-permute-start.23 = (bf16[1536,384]{1,0:T(8,128)(2,1)}, bf16[1536,384]{1,0:T(8,128)(2,1)}, u32[]{:S(2)}, u32[]{:S(2)}) collective-permute-start(bf16[1536,384]{1,0:T(8,128)(2,1)} %collective-permute-done.16.refs_27_.refs_17_), channel_id=1, source_target_pairs={{4,8},{8,4},{5,9},{9,5},{6,10},{10,6},{7,11},{11,7},{20,24},{24,20... | collective-permute-start | bytes 3538952 | tf_op jit(solution)/shard_map/ppermute | solution.py:499
  140.2 24.6 %collective-permute-start.27 = (bf16[192,3072]{1,0:T(8,128)(2,1)}, bf16[192,3072]{1,0:T(8,128)(2,1)}, u32[]{:S(2)}, u32[]{:S(2)}) collective-permute-start(bf16[192,3072]{1,0:T(8,128)(2,1)} %collective-permute-done.18.refs_4_.refs_20_), channel_id=1, source_target_pairs={{0,1},{1,0},{2,3},{3,2},{4,5},{5,4},{6,7},{7,6},{8,9},{9,8},{10,11... | collective-permute-start | bytes 3538952 | tf_op jit(solution)/shard_map/ppermute | solution.py:510
  164.9 5.5 %collective-permute-start.30 = (bf16[192,3072]{1,0:T(8,128)(2,1)}, bf16[192,3072]{1,0:T(8,128)(2,1)S(1)}, u32[]{:S(2)}, u32[]{:S(2)}) collective-permute-start(bf16[192,3072]{1,0:T(8,128)(2,1)} %collective-permute-done.24.refs_5_.refs_21_), channel_id=1, source_target_pairs={{0,1},{1,0},{2,3},{3,2},{4,5},{5,4},{6,7},{7,6},{8,9},{9,8},{10,11... | collective-permute-start | bytes 3538952 | tf_op jit(solution)/shard_map/ppermute | solution.py:510
  165.0 30.6 %collective-permute-start.31 = (bf16[1536,384]{1,0:T(8,128)(2,1)}, bf16[1536,384]{1,0:T(8,128)(2,1)}, u32[]{:S(2)}, u32[]{:S(2)}) collective-permute-start(bf16[1536,384]{1,0:T(8,128)(2,1)} %collective-permute-done.23.refs_16_), channel_id=1, source_target_pairs={{0,4},{4,0},{8,12},{12,8},{1,5},{5,1},{9,13},{13,9},{2,6},{6,2},{1... | collective-permute-start | bytes 3538952 | tf_op jit(solution)/shard_map/ppermute | solution.py:496
  168.6 26.9 %collective-permute-start.32 = (bf16[1536,384]{1,0:T(8,128)(2,1)}, bf16[1536,384]{1,0:T(8,128)(2,1)}, u32[]{:S(2)}, u32[]{:S(2)}) collective-permute-start(bf16[1536,384]{1,0:T(8,128)(2,1)} %collective-permute-done.22.refs_18_.refs_8_), channel_id=1, source_target_pairs={{4,8},{8,4},{5,9},{9,5},{6,10},{10,6},{7,11},{11,7},{20,24},{24,20... | collective-permute-start | bytes 3538952 | tf_op jit(solution)/shard_map/ppermute | solution.py:499
  170.3 14.9 %copy-start.7 = (bf16[192,3072]{1,0:T(8,128)(2,1)}, bf16[192,3072]{1,0:T(8,128)(2,1)S(1)}, u32[]{:S(2)}) copy-start(bf16[192,3072]{1,0:T(8,128)(2,1)S(1)} %collective-permute-done.30.refs_7_.refs_23_) | copy-start | bytes 3538948
  170.3 25.2 %collective-permute-start.33 = (bf16[192,3072]{1,0:T(8,128)(2,1)}, bf16[192,3072]{1,0:T(8,128)(2,1)}, u32[]{:S(2)}, u32[]{:S(2)}) collective-permute-start(bf16[192,3072]{1,0:T(8,128)(2,1)} %collective-permute-done.19.refs_0_), channel_id=1, source_target_pairs={{0,1},{1,0},{2,3},{3,2},{4,5},{5,4},{6,7},{7,6},{8,9},{9,8},{10,11... | collective-permute-start | bytes 3538952 | tf_op jit(solution)/shard_map/ppermute | solution.py:510
  170.5 37.9 %collective-permute-start.28 = (bf16[192,3072]{1,0:T(8,128)(2,1)}, bf16[192,3072]{1,0:T(8,128)(2,1)}, u32[]{:S(2)}, u32[]{:S(2)}) collective-permute-start(bf16[192,3072]{1,0:T(8,128)(2,1)} %collective-permute-done.19.refs_0_), channel_id=1, source_target_pairs={{0,2},{2,0},{1,3},{3,1},{4,6},{6,4},{5,7},{7,5},{8,10},{10,8},{9,1... | collective-permute-start | bytes 3538952 | tf_op jit(solution)/shard_map/ppermute | solution.py:502
  171.7 36.7 %collective-permute-start.29 = (bf16[192,3072]{1,0:T(8,128)(2,1)}, bf16[192,3072]{1,0:T(8,128)(2,1)}, u32[]{:S(2)}, u32[]{:S(2)}) collective-permute-start(bf16[192,3072]{1,0:T(8,128)(2,1)} %collective-permute-done.24.refs_5_.refs_21_), channel_id=1, source_target_pairs={{0,16},{16,0},{1,17},{17,1},{2,18},{18,2},{3,19},{19,3},{4,20},{20... | collective-permute-start | bytes 3538952 | tf_op jit(solution)/shard_map/ppermute | solution.py:503
  208.4 4.0 %collective-permute-start.40 = (bf16[192,3072]{1,0:T(8,128)(2,1)}, bf16[192,3072]{1,0:T(8,128)(2,1)S(1)}, u32[]{:S(2)}, u32[]{:S(2)}) collective-permute-start(bf16[192,3072]{1,0:T(8,128)(2,1)} %collective-permute-done.28.refs_4_), channel_id=1, source_target_pairs={{0,1},{1,0},{2,3},{3,2},{4,5},{5,4},{6,7},{7,6},{8,9},{9,8},{10,11... | collective-permute-start | bytes 3538952 | tf_op jit(solution)/shard_map/ppermute | solution.py:638
  208.5 5.1 %collective-permute-start.41 = (bf16[192,3072]{1,0:T(8,128)(2,1)}, bf16[192,3072]{1,0:T(8,128)(2,1)}, u32[]{:S(2)}, u32[]{:S(2)}) collective-permute-start(bf16[192,3072]{1,0:T(8,128)(2,1)} %collective-permute-done.29.refs_5_), channel_id=1, source_target_pairs={{0,1},{1,0},{2,3},{3,2},{4,5},{5,4},{6,7},{7,6},{8,9},{9,8},{10,11... | collective-permute-start | bytes 3538952 | tf_op jit(solution)/shard_map/ppermute | solution.py:638
  209.0 6.1 %collective-permute-start.39 = (bf16[192,3072]{1,0:T(8,128)(2,1)}, bf16[192,3072]{1,0:T(8,128)(2,1)}, u32[]{:S(2)}, u32[]{:S(2)}) collective-permute-start(bf16[192,3072]{1,0:T(8,128)(2,1)} %collective-permute-done.25.refs_1_), channel_id=1, source_target_pairs={{0,1},{1,0},{2,3},{3,2},{4,5},{5,4},{6,7},{7,6},{8,9},{9,8},{10,11... | collective-permute-start | bytes 3538952 | tf_op jit(solution)/shard_map/ppermute | solution.py:628
  209.1 21.0 %collective-permute-start.34 = (bf16[384,384]{1,0:T(8,128)(2,1)}, bf16[384,384]{1,0:T(8,128)(2,1)S(1)}, u32[]{:S(2)}, u32[]{:S(2)}) collective-permute-start(bf16[384,384]{1,0:T(8,128)(2,1)} %get-tuple-element.238), channel_id=1, source_target_pairs={{0,2},{2,0},{16,18},{18,16},{1,3},{3,1},{17,19},{19,17},{4,6},{6,4... | collective-permute-start | bytes 884744 | tf_op jit(solution)/shard_map/ppermute | solution.py:525
  210.3 19.8 %collective-permute-start.35 = (bf16[384,384]{1,0:T(8,128)(2,1)}, bf16[384,384]{1,0:T(8,128)(2,1)S(1)}, u32[]{:S(2)}, u32[]{:S(2)}) collective-permute-start(bf16[384,384]{1,0:T(8,128)(2,1)} %get-tuple-element.239), channel_id=1, source_target_pairs={{0,16},{2,18},{16,0},{18,2},{1,17},{3,19},{17,1},{19,3},{4,20},{6,... | collective-permute-start | bytes 884744 | tf_op jit(solution)/shard_map/ppermute | solution.py:525
  212.4 4.2 %copy-start.9 = (bf16[192,3072]{1,0:T(8,128)(2,1)}, bf16[192,3072]{1,0:T(8,128)(2,1)S(1)}, u32[]{:S(2)}) copy-start(bf16[192,3072]{1,0:T(8,128)(2,1)S(1)} %collective-permute-done.40.refs_6_) | copy-start | bytes 3538948
  212.4 17.7 %collective-permute-start.36 = (bf16[384,384]{1,0:T(8,128)(2,1)}, bf16[384,384]{1,0:T(8,128)(2,1)}, u32[]{:S(2)}, u32[]{:S(2)}) collective-permute-start(bf16[384,384]{1,0:T(8,128)(2,1)} %get-tuple-element.240), channel_id=1, source_target_pairs={{0,18},{2,16},{16,2},{18,0},{1,19},{3,17},{17,3},{19,1},{4,22},{6,... | collective-permute-start | bytes 884744 | tf_op jit(solution)/shard_map/ppermute | solution.py:525
  213.6 13.2 %collective-permute-start.37 = (bf16[384,128]{1,0:T(8,128)(2,1)}, bf16[384,128]{1,0:T(8,128)(2,1)S(1)}, u32[]{:S(2)}, u32[]{:S(2)}) collective-permute-start(bf16[384,128]{1,0:T(8,128)(2,1)} %get-tuple-element.241), channel_id=1, source_target_pairs={{4,0},{6,2},{8,12},{10,14},{20,16},{22,18},{24,28},{26,30},{5,1},{... | collective-permute-start | bytes 294920 | tf_op jit(solution)/shard_map/ppermute | solution.py:660
  215.0 13.0 %collective-permute-start.38 = (bf16[384,128]{1,0:T(8,128)(2,1)}, bf16[384,128]{1,0:T(8,128)(2,1)S(1)}, u32[]{:S(2)}, u32[]{:S(2)}) collective-permute-start(bf16[384,128]{1,0:T(8,128)(2,1)} %get-tuple-element.242), channel_id=1, source_target_pairs={{4,2},{6,0},{8,14},{10,12},{20,18},{22,16},{24,30},{26,28},{5,3},{... | collective-permute-start | bytes 294920 | tf_op jit(solution)/shard_map/ppermute | solution.py:660
  226.8 10.9 %copy-start.12 = (bf16[384,128]{1,0:T(8,128)(2,1)}, bf16[384,128]{1,0:T(8,128)(2,1)S(1)}, u32[]{:S(2)}) copy-start(bf16[384,128]{1,0:T(8,128)(2,1)S(1)} %collective-permute-done.37.refs_4_) | copy-start | bytes 294916
  226.8 9.3 %collective-permute-start.42 = (bf16[384,128]{1,0:T(8,128)(2,1)}, bf16[384,128]{1,0:T(8,128)(2,1)S(1)}, u32[]{:S(2)}, u32[]{:S(2)}) collective-permute-start(bf16[384,128]{1,0:T(8,128)(2,1)} %get-tuple-element.247), channel_id=1, source_target_pairs={{4,16},{6,18},{8,28},{10,30},{20,0},{22,2},{24,12},{26,14},{5,17},... | collective-permute-start | bytes 294920 | tf_op jit(solution)/shard_map/ppermute | solution.py:660
  228.1 9.6 %copy-start.13 = (bf16[384,128]{1,0:T(8,128)(2,1)}, bf16[384,128]{1,0:T(8,128)(2,1)S(1)}, u32[]{:S(2)}) copy-start(bf16[384,128]{1,0:T(8,128)(2,1)S(1)} %collective-permute-done.38.refs_5_) | copy-start | bytes 294916
  228.1 9.6 %collective-permute-start.43 = (bf16[384,128]{1,0:T(8,128)(2,1)}, bf16[384,128]{1,0:T(8,128)(2,1)S(1)}, u32[]{:S(2)}, u32[]{:S(2)}) collective-permute-start(bf16[384,128]{1,0:T(8,128)(2,1)} %get-tuple-element.248), channel_id=1, source_target_pairs={{4,18},{6,16},{8,30},{10,28},{20,2},{22,0},{24,14},{26,12},{5,19},... | collective-permute-start | bytes 294920 | tf_op jit(solution)/shard_map/ppermute | solution.py:660
  230.1 7.6 %copy-start.10 = (bf16[384,384]{1,0:T(8,128)(2,1)}, bf16[384,384]{1,0:T(8,128)(2,1)S(1)}, u32[]{:S(2)}) copy-start(bf16[384,384]{1,0:T(8,128)(2,1)S(1)} %collective-permute-done.34.refs_1_) | copy-start | bytes 884740
  230.1 7.6 %copy-start.11 = (bf16[384,384]{1,0:T(8,128)(2,1)}, bf16[384,384]{1,0:T(8,128)(2,1)S(1)}, u32[]{:S(2)}) copy-start(bf16[384,384]{1,0:T(8,128)(2,1)S(1)} %collective-permute-done.35.refs_2_) | copy-start | bytes 884740
  236.1 1.6 copy-start.14
  237.7 0.6 copy-start.15
